TPU v7x, 256 devices: a whole 4x4x8 slice. The times are simulated.
256 devices in a mesh: row: 8 (over z_hi, y), col: 32 (over z_lo, x, core).
Axes of the slice: x: 4, y: 4, z: 8 (z_hi: 2, z_lo: 4; z = z_hi * 4 + z_lo), core: 2. Of those that a mesh axis runs over, the one named last changes fastest.
Arguments:
- object_field: float32 [2, 4096, 16384], P(None, 'row', 'col'), may hold values from -6 to 6
- probe_field: float32 [2, 384, 384], replicated, may hold values from -6 to 6
- intensities: bfloat16 [8, 32, 6, 384, 384], P('row', 'col'), may hold values from 0 to 4
- positions: int32 [8, 32, 6, 2], replicated, may hold values from 0 to 511, as said below
- tile_counts: int32 [8, 32], replicated, may hold values from 1 to 6, as said below
Outputs:
- new_object: float32 [2, 4096, 16384], P(None, 'row', 'col')
- new_probe: float32 [2, 384, 384], replicated
Inputs may be any that keep to these rules, and one draw needn't show every extreme that they name: Each entry is a row in 0 to 512 - 1 (first component) or a column in 0 to 512 - 1 (second) of the tile; only slots below the tile's count are scan positions. `tile_counts`: ragged scan positions a tile; some tile holds 6.
All inputs are finite; a program needn't handle non-finite values.
Results may differ from a plain program's by a relative error of at most 0.0061.
The roundings to bfloat16 on the way count: a program that leaves them out, or rounds other values in their place, can miss the bound.
Values may be sent and summed in bfloat16 or wider, within the bound.
No kernel may reach another device: no remote copies, remote signals or barrier semaphores. Data moves between devices by JAX's collectives and lax.ppermute only.
A program may use at most 128 MiB of HBM per device.

v0:
```python
import functools

import jax
import jax.numpy as jnp
import ml_dtypes
import numpy as np
from jax import lax
from jax.experimental import pallas as pl
from jax.experimental.pallas import tpu as pltpu
from jax.sharding import PartitionSpec as P

OBJECT_REG = 0.1
PROBE_REG = 0.1
PROBE_RATE = 0.5
EPSILON = 1e-06

PS = 384
HALF = 192
TH = 512
TW = 512
PMAX = 6
EH = TH + PS
EW = TW + 512
CANVAS = 1280
USED = 108
BLOCKS = 112
STEP = 128
BAND = 96
PART = 64
EDGE = 4
F32 = jnp.float32
BF16 = jnp.bfloat16


def dft_blocks():
    index = np.arange(PS)
    product = (index[:, None] * index[None, :]) % PS
    angles = product.astype(np.float32) * np.float32(2.0 * np.pi / PS)
    norm = np.float32(1.0) / np.sqrt(np.float32(PS))
    cos = (np.cos(angles) * norm).astype(ml_dtypes.bfloat16)
    sin = (-np.sin(angles) * norm).astype(ml_dtypes.bfloat16)
    forward = np.block([[cos, sin], [-sin, cos]])
    order = np.arange(2 * PS).reshape(2, 3, 128).transpose(1, 0, 2).reshape(-1)
    return forward[:, order]


def lane_parts(column):
    block = column // 128
    return block, column - block * 128


def center_of(positions, row, col, slot):
    at = (row * PMAX + slot) * 2
    return positions[at, col], positions[at + 1, col]


def rolled_out(blocks, shift, lanes):
    turned = [pltpu.roll(b, shift, axis=1) for b in blocks]
    keep = lanes >= shift
    zero = jnp.zeros_like(turned[0])
    return [
        jnp.where(keep, turned[0], zero),
        jnp.where(keep, turned[1], turned[0]),
        jnp.where(keep, turned[2], turned[1]),
        jnp.where(keep, zero, turned[2]),
    ]


def rolled_in(blocks, shift, lanes):
    turned = [pltpu.roll(b, (128 - shift) % 128, axis=1) for b in blocks]
    keep = lanes < 128 - shift
    return [jnp.where(keep, turned[k], turned[k + 1]) for k in range(3)]


def illumination_kernel(positions, counts, probe, out, canvas, power):
    my_row, my_col = lax.axis_index("row"), lax.axis_index("col")
    for j in range(3):
        cols = pl.ds(j * 128, 128)
        power[j] = probe[0, :, cols] * probe[0, :, cols] + probe[1, :, cols] * probe[1, :, cols]
    first, last = PS // 128, (PS + TW) // 128
    for j in range(first, last):
        canvas[j, pl.ds(PS, TH), :] = jnp.zeros((TH, 128), F32)
    lanes = lax.broadcasted_iota(jnp.int32, (BAND, 128), 1)
    grid_r, grid_c = 8, 32

    def tile(k, carry):
        down, across = k // 3 - 1, k % 3 - 1
        row, col = my_row + down, my_col + across
        inside = (row >= 0) & (row < grid_r) & (col >= 0) & (col < grid_c)
        row, col = jnp.where(inside, row, 0), jnp.where(inside, col, 0)
        count = jnp.where(inside, counts[row, col], 0)

        def slot(s, inner):
            top, left = center_of(positions, row, col, s)
            top = top + down * TH - HALF + PS
            left = left + across * TW - HALF + PS
            meets = (top > 0) & (top < PS + TH) & (left > 0) & (left < PS + TW)

            @pl.when(meets)
            def _():
                block, shift = lane_parts(left)
                low = jnp.maximum(PS - top, 0) // BAND
                high = (jnp.minimum(PS + TH - top, PS) + BAND - 1) // BAND

                def band(c, deep):
                    rows = pl.ds(pl.multiple_of(c * BAND, BAND), BAND)
                    parts = rolled_out([power[j, rows, :] for j in range(3)], shift, lanes)
                    for j in range(4):
                        canvas[block + j, pl.ds(top + c * BAND, BAND), :] += parts[j]
                    return deep

                lax.fori_loop(low, high, band, 0)

            return inner

        return lax.fori_loop(0, count, slot, carry)

    lax.fori_loop(0, 9, tile, 0)
    floor = OBJECT_REG * jnp.max(power[...])
    for j in range(TW // 128):
        out[:, pl.ds(j * 128, 128)] = 1.0 / (canvas[first + j, pl.ds(PS, TH), :] + floor)


def main_kernel(
    positions, counts, center, across_in, above_in, below_in, before_in, after_in,
    corners_before_in, corners_after_in, probe_in, intensity_in, forward_in,
    field, rim_before, rim_after, rim_above, rim_below, kept, given,
    extended, total, wave, halfway, residual, returning, turned, window, probe_sum,
    probe, intensity, forward, adjoint, above, below, before, after, corners_before, corners_after,
    copied, slot_copied,
):
    my_row, my_col = lax.axis_index("row"), lax.axis_index("col")
    count = counts[my_row, my_col]

    def inward(s):
        return pltpu.make_async_copy(intensity_in.at[s], intensity.at[s], slot_copied.at[s])

    pairs = [(before_in, before), (after_in, after)]
    pairs += [(corners_before_in, corners_before), (corners_after_in, corners_after)]
    pairs += [(probe_in, probe), (forward_in, forward)]
    for p in range(2):
        for j in range(4):
            pairs.append((center.at[p, :, pl.ds(j * 128, 128)], extended.at[p, j + 2, pl.ds(HALF, TH), :]))
    copies = [pltpu.make_async_copy(a, b, copied.at[k]) for k, (a, b) in enumerate(pairs)]
    rims = ((above_in, above, my_row == EDGE), (below_in, below, my_row == EDGE - 1))
    for k, (rim_in, rim, from_across) in enumerate(rims):
        near = pltpu.make_async_copy(rim_in, rim, copied.at[14 + k])
        pl.when(from_across)(pltpu.make_async_copy(across_in, rim, copied.at[14 + k]).start)
        pl.when(jnp.logical_not(from_across))(near.start)
        copies.insert(0, near)
    for copy in copies[2:]:
        copy.start()
    lax.fori_loop(0, count, lambda s, carry: (inward(s).start(), carry)[1], 0)
    total[...] = jnp.zeros_like(total)
    probe_sum[...] = jnp.zeros_like(probe_sum)
    for copy in copies[:6]:
        copy.wait()
    for p in range(2):
        for j in range(EW // 128):
            if 2 <= j < 6:
                cols = pl.ds((j - 2) * 128, 128)
                over, under, low = above, below, 0
            else:
                cols = pl.ds(j % 2 * 128, 128)
                middle, over = (before, corners_before) if j < 2 else (after, corners_after)
                under, low = over, HALF
                extended[p, j, pl.ds(HALF, TH), :] = middle[p, :, cols].astype(F32)
            extended[p, j, pl.ds(0, HALF), :] = over[p, pl.ds(0, HALF), cols].astype(F32)
            extended[p, j, pl.ds(HALF + TH, HALF), :] = under[p, pl.ds(low, HALF), cols].astype(F32)
    for copy in copies[6:]:
        copy.wait()
    for k in range(2):
        for j in range(6):
            here = (pl.ds(k * PS, PS), pl.ds(j * 128, 128))
            adjoint[here] = forward[here] if k == j % 2 else -forward[here]

    def place_of(s):
        top, left = center_of(positions, my_row, my_col, s)
        return (top,) + lane_parts(left + 64)

    def leave(s, k):
        top, block, shift = place_of(s)
        lanes = lax.broadcasted_iota(jnp.int32, (PART, 128), 1)
        for at in range(k * 128, (k + 1) * 128, PART):
            rows = pl.ds(at, PART)
            cells = []
            for p in range(2):
                found = [extended[p, block + j, pl.ds(top + at, PART), :] for j in range(4)]
                cells.append(jnp.concatenate(rolled_in(found, shift, lanes), axis=1))
                window[s % 2, p, rows, :] = cells[p]
            pr, pi = probe[0, rows, :], probe[1, rows, :]
            wave[pl.ds(k * 128 + at, PART), :] = (pr * cells[0] - pi * cells[1]).astype(BF16)
            wave[pl.ds(k * 128 + at + 128, PART), :] = (pr * cells[1] + pi * cells[0]).astype(BF16)

    for k in range(3):
        leave(0, k)

    def slot(s, carry):
        top, block, shift = place_of(s)
        half = jnp.dot(adjoint[...], wave[...], preferred_element_type=F32).astype(BF16)
        halfway[:, pl.ds(0, PS)] = half[:PS]
        halfway[:, pl.ds(PS, PS)] = half[PS:]
        inward(s).wait()
        for j in range(3):
            cols = pl.ds(j * 128, 128)
            far = jnp.dot(halfway[...], forward[:, pl.ds(j * 256, 256)], preferred_element_type=F32)
            far_r, far_i = far[:, :128], far[:, 128:]
            misfit = far_r * far_r + far_i * far_i - intensity[s, :, cols].astype(F32)
            real, imaginary = (misfit * far_r).astype(BF16), (misfit * far_i).astype(BF16)
            for k in range(3):
                residual[pl.ds(k * 256, 128), cols] = real[k * 128 : (k + 1) * 128]
                residual[pl.ds(k * 256 + 128, 128), cols] = imaginary[k * 128 : (k + 1) * 128]
            leave(jnp.minimum(s + 1, count - 1), j)
        back = jnp.dot(forward[...], residual[...], preferred_element_type=F32).astype(BF16)
        returning[:, pl.ds(0, PS)] = back[:PS]
        returning[:, pl.ds(PS, PS)] = back[PS:]
        lanes = lax.broadcasted_iota(jnp.int32, (PART, 128), 1)
        for j in range(3):
            cols = pl.ds(j * 128, 128)
            gradient = jnp.dot(returning[...], adjoint[:, pl.ds(j * 256, 256)], preferred_element_type=F32)
            for k in range(PS // PART):
                rows = pl.ds(k * PART, PART)
                gr, gi = gradient[k * PART : (k + 1) * PART, :128], gradient[k * PART : (k + 1) * PART, 128:]
                pr, pi = probe[0, rows, cols], probe[1, rows, cols]
                wr, wi = window[s % 2, 0, rows, cols], window[s % 2, 1, rows, cols]
                for p, term in ((0, pr * gr + pi * gi), (1, pr * gi - pi * gr)):
                    term = pltpu.roll(term, shift, axis=1)
                    past = turned[p, rows, :] if j else jnp.zeros_like(term)
                    total[p, block + j, pl.ds(top + k * PART, PART), :] += jnp.where(lanes >= shift, term, past)
                    if j < 2:
                        turned[p, rows, :] = term
                    else:
                        total[p, block + 3, pl.ds(top + k * PART, PART), :] += jnp.where(lanes < shift, term, 0.0)
                probe_sum[0, rows, cols] += wr * gr + wi * gi
                probe_sum[1, rows, cols] += wr * gi - wi * gr
                probe_sum[2, rows, cols] += wr * wr + wi * wi
        return carry

    lax.fori_loop(0, count, slot, 0)
    pairs = []
    for p in range(2):
        for j in range(4):
            cols = pl.ds(j * 128, 128)
            pairs.append((total.at[p, j + 2, pl.ds(HALF, TH), :], field.at[p, :, cols]))
    copies = [pltpu.make_async_copy(a, b, copied.at[k]) for k, (a, b) in enumerate(pairs)]
    for copy in copies:
        copy.start()
    for p in range(2):
        for j in range(EW // 128):
            cols = pl.ds(j % 2 * 128, 128)
            if 2 <= j < 6:
                cols = pl.ds((j - 2) * 128, 128)
                rim_above[p, :, cols] = total[p, j, pl.ds(0, HALF), :].astype(BF16)
                rim_below[p, :, cols] = total[p, j, pl.ds(HALF + TH, HALF), :].astype(BF16)
            else:
                rim = rim_before if j < 2 else rim_after
                rim[p, :, cols] = total[p, j].astype(BF16)
    for core in range(2):

        @pl.when(my_col % 2 == core)
        def _():
            for ref, half, kind in ((kept, core, BF16), (given, 1 - core, BF16)):
                for at in range(BLOCKS):
                    if at < USED:
                        found = half * USED + at
                        p, k, j = found // 72, found // 3 % 24, found % 3
                        ref[at] = probe_sum[p, pl.ds(k * 16, 16), pl.ds(j * 128, 128)].astype(kind)
                    else:
                        ref[at] = jnp.zeros((16, 128), kind)

    for copy in copies:
        copy.wait()


def total_kernel(pieces, out):
    total = pieces[0].astype(F32)
    for k in range(1, pieces.shape[0]):
        total = total + pieces[k].astype(F32)
    for k in range(out.shape[0]):
        out[k] = total.astype(BF16)


def object_kernel(center, field, from_before, from_after, across, from_above, from_below, weight, out):
    my_row = lax.axis_index("row")
    for k in range(TH // 64):
        rows = pl.ds(k * 64, 64)
        outer = pl.ds(HALF + k * 64, 64)
        for p in range(2):
            cells = field[p, rows, :]
            sides = [from_before[p, outer, :], from_after[p, outer, :]]
            cells = cells + jnp.concatenate(sides, axis=1).astype(F32)
            if k * 64 < HALF:
                near, far = from_above[p, rows, :].astype(F32), across[p, rows, :].astype(F32)
                cells = cells + jnp.where(my_row == EDGE, far, near)
            if k * 64 >= TH - HALF:
                there = pl.ds(k * 64 - TH + HALF, 64)
                near, far = from_below[p, there, :].astype(F32), across[p, there, :].astype(F32)
                cells = cells + jnp.where(my_row == EDGE - 1, far, near)
            out[p, rows, :] = center[p, rows, :] - cells * weight[rows, :]


def probe_kernel(half, other, probe, out, sums, planes):
    core = lax.axis_index("col") % 2
    sums[core] = half[...]
    sums[1 - core] = other[...]
    for found in range(2 * USED):
        p, k, j = found // 72, found // 3 % 24, found % 3
        planes[p, pl.ds(k * 16, 16), pl.ds(j * 128, 128)] = sums[found // USED, found % USED].astype(F32)
    floor = PROBE_REG * jnp.max(planes[2])
    square = jnp.zeros((STEP, PS), F32)
    for k in range(PS // STEP):
        rows = pl.ds(k * STEP, STEP)
        weight = 1.0 / (planes[2, rows, :] + floor)
        for p in range(2):
            direction = planes[p, rows, :] * weight
            planes[p, rows, :] = direction
            square = square + direction * direction
    spread = jnp.sqrt(jnp.sum(square) / (PS * PS) + EPSILON)
    for p in range(2):
        out[p] = probe[p] - PROBE_RATE * planes[p] / spread


SMEM = pl.BlockSpec(memory_space=pltpu.SMEM)
VMEM = pl.BlockSpec(memory_space=pltpu.VMEM)
ANY = pl.BlockSpec(memory_space=pl.ANY)


def params(mib):
    return pltpu.CompilerParams(vmem_limit_bytes=mib << 20)


def shifted(value, axis, step):
    size = lax.axis_size(axis)
    low, high = max(0, -step), min(size, size - step)
    return lax.ppermute(value, axis, [(k, k + step) for k in range(low, high)])


def slots_call(*arrays):
    like = jax.ShapeDtypeStruct
    forward = dft_blocks()
    return pl.pallas_call(
        main_kernel,
        out_shape=(
            like((2, TH, TW), F32),
            like((2, EH, 256), BF16),
            like((2, EH, 256), BF16),
            like((2, HALF, TW), BF16),
            like((2, HALF, TW), BF16),
            like((BLOCKS, 16, 128), BF16),
            like((BLOCKS, 16, 128), BF16),
        ),
        in_specs=[SMEM] * 2 + [ANY] * 11,
        out_specs=(ANY,) + (VMEM,) * 6,
        scratch_shapes=[
            pltpu.VMEM((2, EW // 128, EH, 128), F32),
            pltpu.VMEM((2, EW // 128, EH, 128), F32),
            pltpu.VMEM((2 * PS, PS), BF16),
            pltpu.VMEM((PS, 2 * PS), BF16),
            pltpu.VMEM((2 * PS, PS), BF16),
            pltpu.VMEM((PS, 2 * PS), BF16),
            pltpu.VMEM((2, PS, 128), F32),
            pltpu.VMEM((2, 2, PS, PS), F32),
            pltpu.VMEM((3, PS, PS), F32),
            pltpu.VMEM((2, PS, PS), F32),
            pltpu.VMEM((PMAX, PS, PS), BF16),
            pltpu.VMEM((2 * PS, 2 * PS), BF16),
            pltpu.VMEM((2 * PS, 2 * PS), BF16),
            pltpu.VMEM((2, HALF, TW), BF16),
            pltpu.VMEM((2, HALF, TW), BF16),
            pltpu.VMEM((2, TH, 256), BF16),
            pltpu.VMEM((2, TH, 256), BF16),
            pltpu.VMEM((2, PS, 256), BF16),
            pltpu.VMEM((2, PS, 256), BF16),
            pltpu.SemaphoreType.DMA((16,)),
            pltpu.SemaphoreType.DMA((PMAX,)),
        ],
        compiler_params=params(60),
        name="slots",
    )(*arrays, jnp.asarray(forward))


def across_edge(value):
    return lax.ppermute(value, "row", [(EDGE - 1, EDGE), (EDGE, EDGE - 1)])


def within_halves(value, step):
    rows = [k for k in range(lax.axis_size("row")) if k // EDGE == (k + step) // EDGE]
    return lax.ppermute(value, "row", [(k, k + step) for k in rows])


def on_device(object_field, probe_field, intensities, positions, tile_counts):
    like = jax.ShapeDtypeStruct
    my_row = lax.axis_index("row")
    where = positions.transpose(0, 2, 3, 1).reshape(-1, positions.shape[1])
    head, tail = object_field[:, :HALF, :].astype(BF16), object_field[:, TH - HALF :, :].astype(BF16)
    across = across_edge(jnp.where(my_row == EDGE, head, tail))
    above = within_halves(tail, 1)
    below = within_halves(head, -1)
    before = shifted(object_field[:, :, TW - 256 :].astype(BF16), "col", 1)
    after = shifted(object_field[:, :, :256].astype(BF16), "col", -1)
    weight = pl.pallas_call(
        illumination_kernel,
        out_shape=like((TH, TW), F32),
        in_specs=[SMEM, SMEM, VMEM],
        out_specs=VMEM,
        scratch_shapes=[pltpu.VMEM((CANVAS // 128, CANVAS, 128), F32), pltpu.VMEM((3, PS, 128), F32)],
        compiler_params=params(60),
        cost_estimate=pl.CostEstimate(flops=20_000_000, bytes_accessed=20_000_000, transcendentals=0),
        name="illumination",
    )(where, tile_counts, probe_field)
    across, above, below, weight = lax.optimization_barrier((across, above, below, weight))
    corners = jnp.concatenate(
        [jnp.where(my_row == EDGE, across, above), jnp.where(my_row == EDGE - 1, across, below)], axis=1
    )
    corners_before = shifted(corners[:, :, TW - 256 :], "col", 1)
    corners_after = shifted(corners[:, :, :256], "col", -1)
    field, rim_before, rim_after, rim_above, rim_below, kept, given = slots_call(
        where, tile_counts, object_field, across, above, below, before, after,
        corners_before, corners_after, probe_field, intensities.reshape(PMAX, PS, PS),
    )
    cols, rows = lax.axis_size("col"), lax.axis_size("row")
    device = np.arange(rows * cols).reshape(2, 4, 4, 4, 2)
    plane = device.transpose(0, 2, 4, 1, 3).reshape(-1, 16).tolist()
    line = device.transpose(1, 3, 4, 0, 2).reshape(-1, 8).tolist()
    partner = [(k, k ^ 1) for k in range(cols)]

    def exchanged(pieces, groups):
        return lax.all_to_all(pieces, ("row", "col"), 0, 0, axis_index_groups=groups)

    def total_of(pieces, times, flops):
        return pl.pallas_call(
            total_kernel,
            out_shape=like((times,) + pieces.shape[1:], BF16),
            in_specs=[VMEM],
            out_specs=VMEM,
            cost_estimate=pl.CostEstimate(flops=flops, bytes_accessed=0, transcendentals=0),
            name="total",
        )(pieces)

    arrived = lax.ppermute(given, "col", partner)
    mine = (kept.astype(F32) + arrived.astype(F32)).astype(BF16)
    mine, rim_before, rim_after = lax.optimization_barrier((mine, rim_before, rim_after))
    from_before = shifted(rim_after, "col", 1)
    from_after = shifted(rim_before, "col", -1)
    parts = exchanged(mine.reshape(16, -1, 16, 128), plane)
    sums = total_of(parts, 8, 10_000_000_000)
    parts = exchanged(sums, line)
    sides = jnp.concatenate([from_before, from_after], axis=2).astype(F32)
    up = (rim_above.astype(F32) + sides[:, :HALF]).astype(BF16)
    down = (rim_below.astype(F32) + sides[:, HALF + TH :]).astype(BF16)
    across = across_edge(jnp.where(my_row == EDGE, up, down))
    from_below = within_halves(up, -1)
    from_above = within_halves(down, 1)
    sums = total_of(parts, 16, 1_000_000_000)
    half = exchanged(sums, plane).reshape(BLOCKS, 16, 128)
    new_object = pl.pallas_call(
        object_kernel,
        out_shape=like((2, TH, TW), F32),
        in_specs=[VMEM] * 8,
        out_specs=VMEM,
        compiler_params=params(60),
        cost_estimate=pl.CostEstimate(flops=40_000_000_000, bytes_accessed=12_000_000, transcendentals=0),
        name="new_object",
    )(object_field, field, from_before, from_after, across, from_above, from_below, weight)
    half, new_object = lax.optimization_barrier((half, new_object))
    other = lax.ppermute(half, "col", partner)
    new_probe = pl.pallas_call(
        probe_kernel,
        out_shape=like((2, PS, PS), F32),
        in_specs=[VMEM] * 3,
        out_specs=VMEM,
        scratch_shapes=[pltpu.VMEM((2, BLOCKS, 16, 128), BF16), pltpu.VMEM((3, PS, PS), F32)],
        compiler_params=params(60),
        name="new_probe",
    )(half, other, probe_field)
    return (new_object, new_probe)


def solution(mesh):
    placed = (P(None, "row", "col"), P(), P("row", "col", None, None, None), P(), P())
    return jax.shard_map(
        on_device,
        mesh=mesh,
        in_specs=placed,
        out_specs=(P(None, "row", "col"), P()),
        check_vma=False,
    )
```

profile of v0, /device:TPU:57, one launch (start us, length us, event | category | flops | bytes accessed | tf_op | source)
XLA Modules:
  0.0 154.5 jit_solution(2922999800082809542)
XLA Ops:
  3.4 2.4 %collective-permute-start.2 = (bf16[2,192,512]{2,1,0:T(8,128)(2,1)}, bf16[2,192,512]{2,1,0:T(8,128)(2,1)S(1)}, u32[]{:S(2)}, u32[]{:S(2)}) collective-permute-start(bf16[2,192,512]{2,1,0:T(8,128)(2,1)} %get-tuple-element.39), channel_id=1, source_target_pairs={{32,0},{64,32},{96,64},{160,128},{192,160},{224,192},{33,1},{65,33... | collective-permute-start | bytes 1179656 | tf_op jit(solution)/shard_map/ppermute | solution.py:388
  5.8 6.5 %collective-permute-start = (bf16[2,192,512]{2,1,0:T(8,128)(2,1)}, bf16[2,192,512]{2,1,0:T(8,128)(2,1)S(1)}, u32[]{:S(2)}, u32[]{:S(2)}) collective-permute-start(bf16[2,192,512]{2,1,0:T(8,128)(2,1)} %get-tuple-element.40), channel_id=1, source_target_pairs={{96,128},{128,96},{97,129},{129,97},{98,130},{130,98},{99,131},{13... | collective-permute-start | bytes 1179656 | tf_op jit(solution)/shard_map/ppermute | solution.py:383
  13.7 2.9 %collective-permute-start.4 = (bf16[2,512,256]{2,1,0:T(8,128)(2,1)S(1)}, bf16[2,512,256]{2,1,0:T(8,128)(2,1)S(1)}, u32[]{:S(2)}, u32[]{:S(2)}) collective-permute-start(bf16[2,512,256]{2,1,0:T(8,128)(2,1)S(1)} %get-tuple-element.37), channel_id=1, source_target_pairs={{1,0},{2,1},{3,2},{4,3},{5,4},{6,5},{7,6},{8,7},{9,8},{10,9},{11,1... | collective-permute-start | bytes 1572872 | tf_op jit(solution)/shard_map/ppermute | solution.py:335
  16.5 3.0 %collective-permute-start.3 = (bf16[2,512,256]{2,1,0:T(8,128)(2,1)S(1)}, bf16[2,512,256]{2,1,0:T(8,128)(2,1)S(1)}, u32[]{:S(2)}, u32[]{:S(2)}) collective-permute-start(bf16[2,512,256]{2,1,0:T(8,128)(2,1)S(1)} %get-tuple-element.38), channel_id=1, source_target_pairs={{0,1},{1,2},{2,3},{3,4},{4,5},{5,6},{6,7},{7,8},{8,9},{9,10},{10,1... | collective-permute-start | bytes 1572872 | tf_op jit(solution)/shard_map/ppermute | solution.py:335
  19.6 6.5 %illumination.1.weight = f32[512,512]{1,0:T(8,128)} custom-call(s32[96,32]{1,0:T(8,128)} %bitcast.9, s32[8,32]{1,0:T(8,128)} %counts.3, f32[2,384,384]{2,1,0:T(8,128)} %probe.3), custom_call_target="tpu_custom_call" | custom-call | flops 20000000 | bytes 20000000 | tf_op jit(solution)/shard_map/illumination/pallas_call | solution.py:401
  26.1 5.9 %collective-permute-done.across_in = bf16[2,192,512]{2,1,0:T(8,128)(2,1)S(1)} collective-permute-done((bf16[2,192,512]{2,1,0:T(8,128)(2,1)}, bf16[2,192,512]{2,1,0:T(8,128)(2,1)S(1)}, u32[]{:S(2)}, u32[]{:S(2)}) %collective-permute-start) | collective-permute-done | bytes 393248 | tf_op jit(solution)/shard_map/ppermute | solution.py:383
  32.9 3.9 %collective-permute-start.6 = (bf16[2,384,256]{2,1,0:T(8,128)(2,1)S(1)}, bf16[2,384,256]{2,1,0:T(8,128)(2,1)S(1)}, u32[]{:S(2)}, u32[]{:S(2)}) collective-permute-start(bf16[2,384,256]{2,1,0:T(8,128)(2,1)S(1)} %get-tuple-element.42), channel_id=1, source_target_pairs={{1,0},{2,1},{3,2},{4,3},{5,4},{6,5},{7,6},{8,7},{9,8},{10,9},{11,1... | collective-permute-start | bytes 1179656 | tf_op jit(solution)/shard_map/ppermute | solution.py:335
  36.8 2.9 %collective-permute-start.5 = (bf16[2,384,256]{2,1,0:T(8,128)(2,1)S(1)}, bf16[2,384,256]{2,1,0:T(8,128)(2,1)S(1)}, u32[]{:S(2)}, u32[]{:S(2)}) collective-permute-start(bf16[2,384,256]{2,1,0:T(8,128)(2,1)S(1)} %get-tuple-element.43), channel_id=1, source_target_pairs={{0,1},{1,2},{2,3},{3,4},{4,5},{5,6},{6,7},{7,8},{8,9},{9,10},{10,1... | collective-permute-start | bytes 1179656 | tf_op jit(solution)/shard_map/ppermute | solution.py:335
  39.7 3.8 %collective-permute-done.6.corners_after_in = bf16[2,384,256]{2,1,0:T(8,128)(2,1)S(1)} collective-permute-done((bf16[2,384,256]{2,1,0:T(8,128)(2,1)S(1)}, bf16[2,384,256]{2,1,0:T(8,128)(2,1)S(1)}, u32[]{:S(2)}, u32[]{:S(2)}) %collective-permute-start.6) | collective-permute-done | bytes 393248 | tf_op jit(solution)/shard_map/ppermute | solution.py:335
  45.2 15.0 %slots.1 = (f32[2,512,512]{2,1,0:T(8,128)}, bf16[2,896,256]{2,1,0:T(8,128)(2,1)}, bf16[2,896,256]{2,1,0:T(8,128)(2,1)}, bf16[2,192,512]{2,1,0:T(8,128)(2,1)}, bf...) custom-call(s32[96,32]{1,0:T(8,128)} %bitcast.10, s32[8,32]{1,0:T(8,128)} %counts.3, ...), custom_call_target="tpu_custom_call" | custom-call | tf_op jit(solution)/shard_map/slots/pallas_call | solution.py:341
  60.2 3.8 %collective-permute-start.7 = (bf16[112,16,128]{2,1,0:T(8,128)(2,1)}, bf16[112,16,128]{2,1,0:T(8,128)(2,1)S(1)}, u32[]{:S(2)}, u32[]{:S(2)}) collective-permute-start(bf16[112,16,128]{2,1,0:T(8,128)(2,1)} %get-tuple-element.22), channel_id=1, source_target_pairs={{0,1},{1,0},{2,3},{3,2},{4,5},{5,4},{6,7},{7,6},{8,9},{9,8},{10,11... | collective-permute-start | bytes 1376264 | tf_op jit(solution)/shard_map/ppermute | solution.py:440
  65.6 1.9 %add_convert_fusion = bf16[112,16,128]{2,1,0:T(8,128)(2,1)} fusion(bf16[112,16,128]{2,1,0:T(8,128)(2,1)S(1)} %collective-permute-done.7, bf16[112,16,128]{2,1,0:T(8,128)(2,1)} %get-tuple-element.21), kind=kLoop, calls=%fused_computation | loop fusion | flops 917504 | bytes 1376256 | tf_op jit(solution)/shard_map/convert_element_type | solution.py:441
  67.5 15.0 %all-to-all-start = ((bf16[16,7,16,128]{3,2,1,0:T(8,128)(2,1)}), bf16[16,7,16,128]{3,2,1,0:T(8,128)(2,1)S(1)}, u32[]{:S(2)}, u32[]{:S(2)}) async-start(bf16[16,7,16,128]{3,2,1,0:T(8,128)(2,1)} %bitcast.4), calls=%async_computation | async-start | bytes 917504 | tf_op jit(solution)/shard_map/all_to_all | solution.py:428
  82.5 3.8 %collective-permute-start.8 = (bf16[2,896,256]{2,1,0:T(8,128)(2,1)}, bf16[2,896,256]{2,1,0:T(8,128)(2,1)S(1)}, u32[]{:S(2)}, u32[]{:S(2)}) collective-permute-start(bf16[2,896,256]{2,1,0:T(8,128)(2,1)} %get-tuple-element.27), channel_id=1, source_target_pairs={{0,1},{1,2},{2,3},{3,4},{4,5},{5,6},{6,7},{7,8},{8,9},{9,10},{10,1... | collective-permute-start | bytes 2752520 | tf_op jit(solution)/shard_map/ppermute | solution.py:335
  86.4 1.9 %collective-permute-start.9 = (bf16[2,896,256]{2,1,0:T(8,128)(2,1)}, bf16[2,896,256]{2,1,0:T(8,128)(2,1)S(1)}, u32[]{:S(2)}, u32[]{:S(2)}) collective-permute-start(bf16[2,896,256]{2,1,0:T(8,128)(2,1)} %get-tuple-element.28), channel_id=1, source_target_pairs={{1,0},{2,1},{3,2},{4,3},{5,4},{6,5},{7,6},{8,7},{9,8},{10,9},{11,1... | collective-permute-start | bytes 2752520 | tf_op jit(solution)/shard_map/ppermute | solution.py:335
  88.3 12.4 %all-to-all-done.pieces = bf16[16,7,16,128]{3,2,1,0:T(8,128)(2,1)S(1)} async-done(((bf16[16,7,16,128]{3,2,1,0:T(8,128)(2,1)}), bf16[16,7,16,128]{3,2,1,0:T(8,128)(2,1)S(1)}, u32[]{:S(2)}, u32[]{:S(2)}) %all-to-all-start) | async-done | bytes 458784 | tf_op jit(solution)/shard_map/all_to_all | solution.py:428
  103.3 5.6 %all-to-all-start.1 = ((bf16[8,7,16,128]{3,2,1,0:T(8,128)(2,1)}), bf16[8,7,16,128]{3,2,1,0:T(8,128)(2,1)}, u32[]{:S(2)}, u32[]{:S(2)}) async-start(bf16[8,7,16,128]{3,2,1,0:T(8,128)(2,1)} %total.2), calls=%async_computation.1 | async-start | bytes 458752 | tf_op jit(solution)/shard_map/all_to_all | solution.py:428
  110.3 6.1 %collective-permute-start.10 = (bf16[2,192,512]{2,1,0:T(8,128)(2,1)}, bf16[2,192,512]{2,1,0:T(8,128)(2,1)S(1)}, u32[]{:S(2)}, u32[]{:S(2)}) collective-permute-start(bf16[2,192,512]{2,1,0:T(8,128)(2,1)} %get-tuple-element.34), channel_id=1, source_target_pairs={{96,128},{128,96},{97,129},{129,97},{98,130},{130,98},{99,131},{13... | collective-permute-start | bytes 1179656 | tf_op jit(solution)/shard_map/ppermute | solution.py:383
  117.7 4.0 %collective-permute-start.12 = (bf16[2,192,512]{2,1,0:T(8,128)(2,1)S(1)}, bf16[2,192,512]{2,1,0:T(8,128)(2,1)S(1)}, u32[]{:S(2)}, u32[]{:S(2)}) collective-permute-start(bf16[2,192,512]{2,1,0:T(8,128)(2,1)S(1)} %get-tuple-element.36), channel_id=1, source_target_pairs={{32,0},{64,32},{96,64},{160,128},{192,160},{224,192},{33,1},{65,33... | collective-permute-start | bytes 1179656 | tf_op jit(solution)/shard_map/ppermute | solution.py:388
  123.5 4.0 %all-to-all-start.2 = ((bf16[16,7,16,128]{3,2,1,0:T(8,128)(2,1)}), bf16[16,7,16,128]{3,2,1,0:T(8,128)(2,1)S(1)}, u32[]{:S(2)}, u32[]{:S(2)}) async-start(bf16[16,7,16,128]{3,2,1,0:T(8,128)(2,1)} %total.3), calls=%async_computation.2 | async-start | bytes 917504 | tf_op jit(solution)/shard_map/all_to_all | solution.py:428
  127.5 12.4 %collective-permute-done.10.across = bf16[2,192,512]{2,1,0:T(8,128)(2,1)S(1)} collective-permute-done((bf16[2,192,512]{2,1,0:T(8,128)(2,1)}, bf16[2,192,512]{2,1,0:T(8,128)(2,1)S(1)}, u32[]{:S(2)}, u32[]{:S(2)}) %collective-permute-start.10) | collective-permute-done | bytes 393248 | tf_op jit(solution)/shard_map/ppermute | solution.py:383
  141.0 5.2 %new_object.1 = f32[2,512,512]{2,1,0:T(8,128)} custom-call(f32[2,512,512]{2,1,0:T(8,128)} %center.3, f32[2,512,512]{2,1,0:T(8,128)} %get-tuple-element.26.field, bf16[2,896,256]{2,1,0:T(8,128)(2,1)} %copy-done.4, bf16[2,896,256]{2,1,0:T(8,128)(2,1)} %copy-done.5, bf16[2,192,512]{2,1,0:T(8,128)(2,1)} %copy-done.14, bf16[2,192,512]{2,1,0:T(8,128)(2,1)} %copy-done.15, ...), custom_call_target="tpu_custom_call" | custom-call | flops 40000000000 | bytes 12000000 | tf_op jit(solution)/shard_map/new_object/pallas_call | solution.py:456
  146.1 2.6 %collective-permute-start.13 = (bf16[112,16,128]{2,1,0:T(8,128)(2,1)S(1)}, bf16[112,16,128]{2,1,0:T(8,128)(2,1)S(1)}, u32[]{:S(2)}, u32[]{:S(2)}) collective-permute-start(bf16[112,16,128]{2,1,0:T(8,128)(2,1)S(1)} %bitcast.6), channel_id=1, source_target_pairs={{0,1},{1,0},{2,3},{3,2},{4,5},{5,4},{6,7},{7,6},{8,9},{9,8},{10,11... | collective-permute-start | bytes 1376264 | tf_op jit(solution)/shard_map/ppermute | solution.py:466
  151.0 3.5 %new_probe.1 = f32[2,384,384]{2,1,0:T(8,128)} custom-call(bf16[112,16,128]{2,1,0:T(8,128)(2,1)} %bitcast.7, bf16[112,16,128]{2,1,0:T(8,128)(2,1)} %copy-done.8, f32[2,384,384]{2,1,0:T(8,128)} %probe.3), custom_call_target="tpu_custom_call" | custom-call | tf_op jit(solution)/shard_map/new_probe/pallas_call | solution.py:467
  (57 shorter events, 18.5 us)
Async XLA Ops:
  3.4 22.7 %collective-permute-start.2 = (bf16[2,192,512]{2,1,0:T(8,128)(2,1)}, bf16[2,192,512]{2,1,0:T(8,128)(2,1)S(1)}, u32[]{:S(2)}, u32[]{:S(2)}) collective-permute-start(bf16[2,192,512]{2,1,0:T(8,128)(2,1)} %get-tuple-element.39), channel_id=1, source_target_pairs={{32,0},{64,32},{96,64},{160,128},{192,160},{224,192},{33,1},{65,33... | collective-permute-start | bytes 1179656 | tf_op jit(solution)/shard_map/ppermute | solution.py:388
  5.8 26.2 %collective-permute-start = (bf16[2,192,512]{2,1,0:T(8,128)(2,1)}, bf16[2,192,512]{2,1,0:T(8,128)(2,1)S(1)}, u32[]{:S(2)}, u32[]{:S(2)}) collective-permute-start(bf16[2,192,512]{2,1,0:T(8,128)(2,1)} %get-tuple-element.40), channel_id=1, source_target_pairs={{96,128},{128,96},{97,129},{129,97},{98,130},{130,98},{99,131},{13... | collective-permute-start | bytes 1179656 | tf_op jit(solution)/shard_map/ppermute | solution.py:383
  12.3 19.7 %collective-permute-start.1 = (bf16[2,192,512]{2,1,0:T(8,128)(2,1)}, bf16[2,192,512]{2,1,0:T(8,128)(2,1)S(1)}, u32[]{:S(2)}, u32[]{:S(2)}) collective-permute-start(bf16[2,192,512]{2,1,0:T(8,128)(2,1)} %get-tuple-element.41), channel_id=1, source_target_pairs={{0,32},{32,64},{64,96},{128,160},{160,192},{192,224},{1,33},{33,65... | collective-permute-start | bytes 1179656 | tf_op jit(solution)/shard_map/ppermute | solution.py:388
  13.7 26.0 %collective-permute-start.4 = (bf16[2,512,256]{2,1,0:T(8,128)(2,1)S(1)}, bf16[2,512,256]{2,1,0:T(8,128)(2,1)S(1)}, u32[]{:S(2)}, u32[]{:S(2)}) collective-permute-start(bf16[2,512,256]{2,1,0:T(8,128)(2,1)S(1)} %get-tuple-element.37), channel_id=1, source_target_pairs={{1,0},{2,1},{3,2},{4,3},{5,4},{6,5},{7,6},{8,7},{9,8},{10,9},{11,1... | collective-permute-start | bytes 1572872 | tf_op jit(solution)/shard_map/ppermute | solution.py:335
  16.5 23.2 %collective-permute-start.3 = (bf16[2,512,256]{2,1,0:T(8,128)(2,1)S(1)}, bf16[2,512,256]{2,1,0:T(8,128)(2,1)S(1)}, u32[]{:S(2)}, u32[]{:S(2)}) collective-permute-start(bf16[2,512,256]{2,1,0:T(8,128)(2,1)S(1)} %get-tuple-element.38), channel_id=1, source_target_pairs={{0,1},{1,2},{2,3},{3,4},{4,5},{5,6},{6,7},{7,8},{8,9},{9,10},{10,1... | collective-permute-start | bytes 1572872 | tf_op jit(solution)/shard_map/ppermute | solution.py:335
  26.1 6.1 %copy-start.1 = (bf16[2,192,512]{2,1,0:T(8,128)(2,1)}, bf16[2,192,512]{2,1,0:T(8,128)(2,1)S(1)}, u32[]{:S(2)}) copy-start(bf16[2,192,512]{2,1,0:T(8,128)(2,1)S(1)} %collective-permute-done.2.below_in) | copy-start | bytes 1179652
  32.9 10.6 %collective-permute-start.6 = (bf16[2,384,256]{2,1,0:T(8,128)(2,1)S(1)}, bf16[2,384,256]{2,1,0:T(8,128)(2,1)S(1)}, u32[]{:S(2)}, u32[]{:S(2)}) collective-permute-start(bf16[2,384,256]{2,1,0:T(8,128)(2,1)S(1)} %get-tuple-element.42), channel_id=1, source_target_pairs={{1,0},{2,1},{3,2},{4,3},{5,4},{6,5},{7,6},{8,7},{9,8},{10,9},{11,1... | collective-permute-start | bytes 1179656 | tf_op jit(solution)/shard_map/ppermute | solution.py:335
  36.8 7.6 %collective-permute-start.5 = (bf16[2,384,256]{2,1,0:T(8,128)(2,1)S(1)}, bf16[2,384,256]{2,1,0:T(8,128)(2,1)S(1)}, u32[]{:S(2)}, u32[]{:S(2)}) collective-permute-start(bf16[2,384,256]{2,1,0:T(8,128)(2,1)S(1)} %get-tuple-element.43), channel_id=1, source_target_pairs={{0,1},{1,2},{2,3},{3,4},{4,5},{5,6},{6,7},{7,8},{8,9},{9,10},{10,1... | collective-permute-start | bytes 1179656 | tf_op jit(solution)/shard_map/ppermute | solution.py:335
  39.7 4.7 %copy-start.6 = (bf16[2,512,256]{2,1,0:T(8,128)(2,1)}, bf16[2,512,256]{2,1,0:T(8,128)(2,1)S(1)}, u32[]{:S(2)}) copy-start(bf16[2,512,256]{2,1,0:T(8,128)(2,1)S(1)} %collective-permute-done.4.after_in) | copy-start | bytes 1572868
  39.7 4.7 %copy-start.7 = (bf16[2,512,256]{2,1,0:T(8,128)(2,1)}, bf16[2,512,256]{2,1,0:T(8,128)(2,1)S(1)}, u32[]{:S(2)}) copy-start(bf16[2,512,256]{2,1,0:T(8,128)(2,1)S(1)} %collective-permute-done.3.before_in) | copy-start | bytes 1572868
  60.2 5.5 %collective-permute-start.7 = (bf16[112,16,128]{2,1,0:T(8,128)(2,1)}, bf16[112,16,128]{2,1,0:T(8,128)(2,1)S(1)}, u32[]{:S(2)}, u32[]{:S(2)}) collective-permute-start(bf16[112,16,128]{2,1,0:T(8,128)(2,1)} %get-tuple-element.22), channel_id=1, source_target_pairs={{0,1},{1,0},{2,3},{3,2},{4,5},{5,4},{6,7},{7,6},{8,9},{9,8},{10,11... | collective-permute-start | bytes 1376264 | tf_op jit(solution)/shard_map/ppermute | solution.py:440
  67.5 33.2 %all-to-all-start = ((bf16[16,7,16,128]{3,2,1,0:T(8,128)(2,1)}), bf16[16,7,16,128]{3,2,1,0:T(8,128)(2,1)S(1)}, u32[]{:S(2)}, u32[]{:S(2)}) async-start(bf16[16,7,16,128]{3,2,1,0:T(8,128)(2,1)} %bitcast.4), calls=%async_computation | async-start | bytes 917504 | tf_op jit(solution)/shard_map/all_to_all | solution.py:428
  82.5 26.5 %copy-start.12 = (bf16[2,192,512]{2,1,0:T(8,128)(2,1)S(1)}, bf16[2,192,512]{2,1,0:T(8,128)(2,1)}, u32[]{:S(2)}) copy-start(bf16[2,192,512]{2,1,0:T(8,128)(2,1)} %get-tuple-element.29) | copy-start | bytes 1179652
  82.5 26.5 %copy-start.13 = (bf16[2,192,512]{2,1,0:T(8,128)(2,1)S(1)}, bf16[2,192,512]{2,1,0:T(8,128)(2,1)}, u32[]{:S(2)}) copy-start(bf16[2,192,512]{2,1,0:T(8,128)(2,1)} %get-tuple-element.30) | copy-start | bytes 1179652
  82.5 26.4 %collective-permute-start.8 = (bf16[2,896,256]{2,1,0:T(8,128)(2,1)}, bf16[2,896,256]{2,1,0:T(8,128)(2,1)S(1)}, u32[]{:S(2)}, u32[]{:S(2)}) collective-permute-start(bf16[2,896,256]{2,1,0:T(8,128)(2,1)} %get-tuple-element.27), channel_id=1, source_target_pairs={{0,1},{1,2},{2,3},{3,4},{4,5},{5,6},{6,7},{7,8},{8,9},{9,10},{10,1... | collective-permute-start | bytes 2752520 | tf_op jit(solution)/shard_map/ppermute | solution.py:335
  86.4 22.6 %collective-permute-start.9 = (bf16[2,896,256]{2,1,0:T(8,128)(2,1)}, bf16[2,896,256]{2,1,0:T(8,128)(2,1)S(1)}, u32[]{:S(2)}, u32[]{:S(2)}) collective-permute-start(bf16[2,896,256]{2,1,0:T(8,128)(2,1)} %get-tuple-element.28), channel_id=1, source_target_pairs={{1,0},{2,1},{3,2},{4,3},{5,4},{6,5},{7,6},{8,7},{9,8},{10,9},{11,1... | collective-permute-start | bytes 2752520 | tf_op jit(solution)/shard_map/ppermute | solution.py:335
  103.3 18.4 %all-to-all-start.1 = ((bf16[8,7,16,128]{3,2,1,0:T(8,128)(2,1)}), bf16[8,7,16,128]{3,2,1,0:T(8,128)(2,1)}, u32[]{:S(2)}, u32[]{:S(2)}) async-start(bf16[8,7,16,128]{3,2,1,0:T(8,128)(2,1)} %total.2), calls=%async_computation.1 | async-start | bytes 458752 | tf_op jit(solution)/shard_map/all_to_all | solution.py:428
  109.0 1.3 copy-start.5
  110.3 29.6 %collective-permute-start.10 = (bf16[2,192,512]{2,1,0:T(8,128)(2,1)}, bf16[2,192,512]{2,1,0:T(8,128)(2,1)S(1)}, u32[]{:S(2)}, u32[]{:S(2)}) collective-permute-start(bf16[2,192,512]{2,1,0:T(8,128)(2,1)} %get-tuple-element.34), channel_id=1, source_target_pairs={{96,128},{128,96},{97,129},{129,97},{98,130},{130,98},{99,131},{13... | collective-permute-start | bytes 1179656 | tf_op jit(solution)/shard_map/ppermute | solution.py:383
  116.4 23.5 %collective-permute-start.11 = (bf16[2,192,512]{2,1,0:T(8,128)(2,1)S(1)}, bf16[2,192,512]{2,1,0:T(8,128)(2,1)S(1)}, u32[]{:S(2)}, u32[]{:S(2)}) collective-permute-start(bf16[2,192,512]{2,1,0:T(8,128)(2,1)S(1)} %get-tuple-element.35), channel_id=1, source_target_pairs={{0,32},{32,64},{64,96},{128,160},{160,192},{192,224},{1,33},{33,65... | collective-permute-start | bytes 1179656 | tf_op jit(solution)/shard_map/ppermute | solution.py:388
  117.7 22.2 %collective-permute-start.12 = (bf16[2,192,512]{2,1,0:T(8,128)(2,1)S(1)}, bf16[2,192,512]{2,1,0:T(8,128)(2,1)S(1)}, u32[]{:S(2)}, u32[]{:S(2)}) collective-permute-start(bf16[2,192,512]{2,1,0:T(8,128)(2,1)S(1)} %get-tuple-element.36), channel_id=1, source_target_pairs={{32,0},{64,32},{96,64},{160,128},{192,160},{224,192},{33,1},{65,33... | collective-permute-start | bytes 1179656 | tf_op jit(solution)/shard_map/ppermute | solution.py:388
  123.5 22.6 %all-to-all-start.2 = ((bf16[16,7,16,128]{3,2,1,0:T(8,128)(2,1)}), bf16[16,7,16,128]{3,2,1,0:T(8,128)(2,1)S(1)}, u32[]{:S(2)}, u32[]{:S(2)}) async-start(bf16[16,7,16,128]{3,2,1,0:T(8,128)(2,1)} %total.3), calls=%async_computation.2 | async-start | bytes 917504 | tf_op jit(solution)/shard_map/all_to_all | solution.py:428
  146.1 4.1 %copy-start = (bf16[16,7,16,128]{3,2,1,0:T(8,128)(2,1)}, bf16[16,7,16,128]{3,2,1,0:T(8,128)(2,1)S(1)}, u32[]{:S(2)}) copy-start(bf16[16,7,16,128]{3,2,1,0:T(8,128)(2,1)S(1)} %all-to-all-done.2) | copy-start | bytes 1376260
  146.1 4.1 %collective-permute-start.13 = (bf16[112,16,128]{2,1,0:T(8,128)(2,1)S(1)}, bf16[112,16,128]{2,1,0:T(8,128)(2,1)S(1)}, u32[]{:S(2)}, u32[]{:S(2)}) collective-permute-start(bf16[112,16,128]{2,1,0:T(8,128)(2,1)S(1)} %bitcast.6), channel_id=1, source_target_pairs={{0,1},{1,0},{2,3},{3,2},{4,5},{5,4},{6,7},{7,6},{8,9},{9,8},{10,11... | collective-permute-start | bytes 1376264 | tf_op jit(solution)/shard_map/ppermute | solution.py:466
  (10 other events, 8.8 us)
where the time goes:
time: 155 us; the launch traced here: 154 us
  starting transfers between devices  71 us (46%)
  waiting for transfers between devices  38.6 us (25%)
  Pallas kernels  33.7 us (22%)
  other arithmetic  6.04 us (4%)
  local copies, waits for them, and re-layouts  4.31 us (3%)
    all_to_all x3, starting transfers between devices, exchanged(): lax.all_to_all(pieces, ('row', 'col'), 0, 0, axis_index_groups=groups)  24.6 us
    ppermute x6, starting transfers between devices, shifted(): return lax.ppermute(value, axis, [(k, k + step) for k in range(low, high)])  18.4 us
    ppermute x2, waiting for transfers between devices, across_edge(): return lax.ppermute(value, 'row', [(EDGE - 1, EDGE), (EDGE, EDGE - 1)])  18.3 us
    pallas_call x1, Pallas kernels, slots_call(): pl.pallas_call(main_kernel, out_shape=(like((2, TH, TW), F32), like((2, E...  15 us
    ppermute x2, starting transfers between devices, across_edge(): return lax.ppermute(value, 'row', [(EDGE - 1, EDGE), (EDGE, EDGE - 1)])  12.6 us
    all_to_all x3, waiting for transfers between devices, exchanged(): lax.all_to_all(pieces, ('row', 'col'), 0, 0, axis_index_groups=groups)  12.5 us
    ppermute x4, starting transfers between devices, within_halves(): return lax.ppermute(value, 'row', [(k, k + step) for k in rows])  8.97 us
    pallas_call x1, Pallas kernels, on_device(): pl.pallas_call(illumination_kernel, out_shape=like((TH, TW), F32), in_spe...  6.53 us
  transfers between devices with their start and end apart: 17, of which 7 were waited for; matrix products, arithmetic and copies ran while one was open for 1% of the time, Pallas kernels for 10%

commit v1 on v0

--- a/solution.py
+++ b/solution.py
@@ -280,23 +280,43 @@
         out[k] = total.astype(BF16)
 
 
-def object_kernel(center, field, from_before, from_after, across, from_above, from_below, weight, out):
-    my_row = lax.axis_index("row")
+def cut_kernel(cells, out, piece, copied):
+    first = jnp.where(lax.axis_index("row") == EDGE, 0, TH - HALF)
+    copy = pltpu.make_async_copy(cells.at[:, pl.ds(pl.multiple_of(first, 64), HALF), :], piece, copied)
+    copy.start()
+    copy.wait()
+    out[...] = piece[...].astype(BF16)
+
+
+def object_kernel(center, field, from_before, from_after, weight, out):
     for k in range(TH // 64):
         rows = pl.ds(k * 64, 64)
         outer = pl.ds(HALF + k * 64, 64)
         for p in range(2):
-            cells = field[p, rows, :]
             sides = [from_before[p, outer, :], from_after[p, outer, :]]
-            cells = cells + jnp.concatenate(sides, axis=1).astype(F32)
-            if k * 64 < HALF:
-                near, far = from_above[p, rows, :].astype(F32), across[p, rows, :].astype(F32)
-                cells = cells + jnp.where(my_row == EDGE, far, near)
-            if k * 64 >= TH - HALF:
-                there = pl.ds(k * 64 - TH + HALF, 64)
-                near, far = from_below[p, there, :].astype(F32), across[p, there, :].astype(F32)
-                cells = cells + jnp.where(my_row == EDGE - 1, far, near)
+            cells = field[p, rows, :] + jnp.concatenate(sides, axis=1).astype(F32)
             out[p, rows, :] = center[p, rows, :] - cells * weight[rows, :]
+
+
+def rims_kernel(base, weight_in, across, from_above, from_below, out, cells, weight, arrived, left):
+    my_row = lax.axis_index("row")
+    places = (pl.ds(0, HALF), pl.ds(TH - HALF, HALF))
+    inward, outward = [], []
+    for k, rows in enumerate(places):
+        inward.append(pltpu.make_async_copy(base.at[:, rows, :], cells.at[k], arrived.at[k]))
+        inward.append(pltpu.make_async_copy(weight_in.at[rows, :], weight.at[k], arrived.at[2 + k]))
+        outward.append(pltpu.make_async_copy(cells.at[k], out.at[:, rows, :], left.at[k]))
+    for copy in inward:
+        copy.start()
+    for k, (near, edge) in enumerate(((from_above, EDGE), (from_below, EDGE - 1))):
+        inward[2 * k].wait()
+        inward[2 * k + 1].wait()
+        for p in range(2):
+            rim = jnp.where(my_row == edge, across[p].astype(F32), near[p].astype(F32))
+            cells[k, p] = cells[k, p] - rim * weight[k]
+        outward[k].start()
+    for copy in outward:
+        copy.wait()
 
 
 def probe_kernel(half, other, probe, out, sums, planes):
@@ -393,7 +413,17 @@
     my_row = lax.axis_index("row")
     where = positions.transpose(0, 2, 3, 1).reshape(-1, positions.shape[1])
     head, tail = object_field[:, :HALF, :].astype(BF16), object_field[:, TH - HALF :, :].astype(BF16)
-    across = across_edge(jnp.where(my_row == EDGE, head, tail))
+    piece = pl.pallas_call(
+        cut_kernel,
+        out_shape=like((2, HALF, TW), BF16),
+        in_specs=[ANY],
+        out_specs=VMEM,
+        scratch_shapes=[pltpu.VMEM((2, HALF, TW), F32), pltpu.SemaphoreType.DMA],
+        compiler_params=params(60),
+        cost_estimate=pl.CostEstimate(flops=400_000, bytes_accessed=1_200_000, transcendentals=0),
+        name="cut",
+    )(object_field)
+    across = across_edge(piece)
     above = within_halves(tail, 1)
     below = within_halves(head, -1)
     before = shifted(object_field[:, :, TW - 256 :].astype(BF16), "col", 1)
@@ -433,6 +463,7 @@
             out_shape=like((times,) + pieces.shape[1:], BF16),
             in_specs=[VMEM],
             out_specs=VMEM,
+            compiler_params=params(8),
             cost_estimate=pl.CostEstimate(flops=flops, bytes_accessed=0, transcendentals=0),
             name="total",
         )(pieces)
@@ -456,12 +487,28 @@
     new_object = pl.pallas_call(
         object_kernel,
         out_shape=like((2, TH, TW), F32),
-        in_specs=[VMEM] * 8,
+        in_specs=[VMEM] * 5,
         out_specs=VMEM,
         compiler_params=params(60),
-        cost_estimate=pl.CostEstimate(flops=40_000_000_000, bytes_accessed=12_000_000, transcendentals=0),
+        cost_estimate=pl.CostEstimate(flops=4_000_000, bytes_accessed=12_000_000, transcendentals=0),
         name="new_object",
-    )(object_field, field, from_before, from_after, across, from_above, from_below, weight)
+    )(object_field, field, from_before, from_after, weight)
+    new_object = pl.pallas_call(
+        rims_kernel,
+        out_shape=like((2, TH, TW), F32),
+        in_specs=[ANY, ANY, VMEM, VMEM, VMEM],
+        out_specs=ANY,
+        scratch_shapes=[
+            pltpu.VMEM((2, 2, HALF, TW), F32),
+            pltpu.VMEM((2, HALF, TW), F32),
+            pltpu.SemaphoreType.DMA((4,)),
+            pltpu.SemaphoreType.DMA((2,)),
+        ],
+        input_output_aliases={0: 0},
+        compiler_params=params(16),
+        cost_estimate=pl.CostEstimate(flops=40_000_000_000, bytes_accessed=4_000_000, transcendentals=0),
+        name="rims",
+    )(new_object, weight, across, from_above, from_below)
     half, new_object = lax.optimization_barrier((half, new_object))
     other = lax.ppermute(half, "col", partner)
     new_probe = pl.pallas_call(
@@ -470,7 +517,7 @@
         in_specs=[VMEM] * 3,
         out_specs=VMEM,
         scratch_shapes=[pltpu.VMEM((2, BLOCKS, 16, 128), BF16), pltpu.VMEM((3, PS, PS), F32)],
-        compiler_params=params(60),
+        compiler_params=params(24),
         name="new_probe",
     )(half, other, probe_field)
     return (new_object, new_probe)

time: 155 us -> 149 us (0.961)
  waiting for transfers between devices: 38.6 us -> 30.9 us
  Pallas kernels: 33.7 us -> 38.6 us
  local copies, waits for them, and re-layouts: 4.31 us -> 1.66 us
  other arithmetic: 6.04 us -> 3.56 us
    ppermute x2, waiting for transfers between devices: 18.3 us -> 10.6 us  [across_edge(): return lax.ppermute(value, 'row', [(EDGE - 1, EDGE), (EDGE, EDGE - 1)])]
    pallas_call x0 -> x2, Pallas kernels: none -> 5.57 us  [the longest x1 3.48 us: on_device(): pl.pallas_call(rims_kernel, out_shape=like((2, TH, TW), F32), in_specs=[A...]
    all_to_all x3, starting transfers between devices: 24.6 us -> 28.9 us  [exchanged(): lax.all_to_all(pieces, ('row', 'col'), 0, 0, axis_index_groups=groups)]
    ppermute x1, starting transfers between devices: 3.8 us -> 0.09 us  [on_device(): arrived = lax.ppermute(given, 'col', partner)]
    unnamed x34 -> x28, local copies, waits for them, and re-layouts: 4.24 us -> 0.75 us
    pallas_call x1, Pallas kernels: 15 us -> 18.1 us  [slots_call(): pl.pallas_call(main_kernel, out_shape=(like((2, TH, TW), F32), like((2, E...]
    pallas_call x2, Pallas kernels: 3.54 us -> 1.58 us  [total_of(): pl.pallas_call(total_kernel, out_shape=like((times,) + pieces.shape[1:],...]
    another operation x1, other arithmetic: 1.73 us -> 0.13 us
  transfers between devices with their start and end apart: 17 -> 17, of which waited for: 7 -> 7; matrix products, arithmetic and copies ran while one was open for 1% -> 2% of each run, Pallas kernels for 10% -> 11%
where the time goes in v1:
time: 149 us; the launch traced here: 148 us
  starting transfers between devices  72.2 us (48%)
  Pallas kernels  38.6 us (26%)
  waiting for transfers between devices  30.9 us (21%)
  other arithmetic  3.56 us (2%)
  local copies, waits for them, and re-layouts  1.66 us (1%)
    all_to_all x3, starting transfers between devices, exchanged(): lax.all_to_all(pieces, ('row', 'col'), 0, 0, axis_index_groups=groups)  28.9 us
    ppermute x6, starting transfers between devices, shifted(): return lax.ppermute(value, axis, [(k, k + step) for k in range(low, high)])  18.3 us
    pallas_call x1, Pallas kernels, slots_call(): pl.pallas_call(main_kernel, out_shape=(like((2, TH, TW), F32), like((2, E...  18.1 us
    ppermute x2, starting transfers between devices, across_edge(): return lax.ppermute(value, 'row', [(EDGE - 1, EDGE), (EDGE, EDGE - 1)])  13.6 us
    all_to_all x3, waiting for transfers between devices, exchanged(): lax.all_to_all(pieces, ('row', 'col'), 0, 0, axis_index_groups=groups)  12.2 us
    ppermute x2, waiting for transfers between devices, across_edge(): return lax.ppermute(value, 'row', [(EDGE - 1, EDGE), (EDGE, EDGE - 1)])  10.6 us
    ppermute x4, starting transfers between devices, within_halves(): return lax.ppermute(value, 'row', [(k, k + step) for k in rows])  8.66 us
    pallas_call x1, Pallas kernels, on_device(): pl.pallas_call(illumination_kernel, out_shape=like((TH, TW), F32), in_spe...  6.68 us
  transfers between devices with their start and end apart: 17, of which 7 were waited for; matrix products, arithmetic and copies ran while one was open for 2% of the time, Pallas kernels for 11%

profile of v1, /device:TPU:57, one launch (start us, length us, event | category | flops | bytes accessed | tf_op | source)
XLA Modules:
  0.0 147.9 jit_solution(10246096283740446704)
XLA Ops:
  0.6 2.1 %cut.1 = bf16[2,192,512]{2,1,0:T(8,128)(2,1)} custom-call(f32[2,512,512]{2,1,0:T(8,128)} %center.3), custom_call_target="tpu_custom_call" | custom-call | flops 400000 | bytes 1200000 | tf_op jit(solution)/shard_map/cut/pallas_call | solution.py:416
  2.7 7.6 %collective-permute-start = (bf16[2,192,512]{2,1,0:T(8,128)(2,1)}, bf16[2,192,512]{2,1,0:T(8,128)(2,1)S(1)}, u32[]{:S(2)}, u32[]{:S(2)}) collective-permute-start(bf16[2,192,512]{2,1,0:T(8,128)(2,1)} %cut.1), channel_id=1, source_target_pairs={{96,128},{128,96},{97,129},{129,97},{98,130},{130,98},{99,131},{13... | collective-permute-start | bytes 1179656 | tf_op jit(solution)/shard_map/ppermute | solution.py:403
  14.0 2.9 %collective-permute-start.4 = (bf16[2,512,256]{2,1,0:T(8,128)(2,1)}, bf16[2,512,256]{2,1,0:T(8,128)(2,1)S(1)}, u32[]{:S(2)}, u32[]{:S(2)}) collective-permute-start(bf16[2,512,256]{2,1,0:T(8,128)(2,1)} %get-tuple-element.37), channel_id=1, source_target_pairs={{1,0},{2,1},{3,2},{4,3},{5,4},{6,5},{7,6},{8,7},{9,8},{10,9},{11,1... | collective-permute-start | bytes 1572872 | tf_op jit(solution)/shard_map/ppermute | solution.py:355
  16.9 3.0 %collective-permute-start.3 = (bf16[2,512,256]{2,1,0:T(8,128)(2,1)S(1)}, bf16[2,512,256]{2,1,0:T(8,128)(2,1)S(1)}, u32[]{:S(2)}, u32[]{:S(2)}) collective-permute-start(bf16[2,512,256]{2,1,0:T(8,128)(2,1)S(1)} %get-tuple-element.38), channel_id=1, source_target_pairs={{0,1},{1,2},{2,3},{3,4},{4,5},{5,6},{6,7},{7,8},{8,9},{9,10},{10,1... | collective-permute-start | bytes 1572872 | tf_op jit(solution)/shard_map/ppermute | solution.py:355
  19.9 6.7 %illumination.1.weight.weight_in = f32[512,512]{1,0:T(8,128)} custom-call(s32[96,32]{1,0:T(8,128)} %bitcast.9, s32[8,32]{1,0:T(8,128)} %counts.3, f32[2,384,384]{2,1,0:T(8,128)} %probe.3), custom_call_target="tpu_custom_call" | custom-call | flops 20000000 | bytes 20000000 | tf_op jit(solution)/shard_map/illumination/pallas_call | solution.py:431
  26.6 2.7 %collective-permute-done.across_in = bf16[2,192,512]{2,1,0:T(8,128)(2,1)S(1)} collective-permute-done((bf16[2,192,512]{2,1,0:T(8,128)(2,1)}, bf16[2,192,512]{2,1,0:T(8,128)(2,1)S(1)}, u32[]{:S(2)}, u32[]{:S(2)}) %collective-permute-start) | collective-permute-done | bytes 393248 | tf_op jit(solution)/shard_map/ppermute | solution.py:403
  29.4 3.6 %collective-permute-start.6 = (bf16[2,384,256]{2,1,0:T(8,128)(2,1)S(1)}, bf16[2,384,256]{2,1,0:T(8,128)(2,1)S(1)}, u32[]{:S(2)}, u32[]{:S(2)}) collective-permute-start(bf16[2,384,256]{2,1,0:T(8,128)(2,1)S(1)} %get-tuple-element.41), channel_id=1, source_target_pairs={{1,0},{2,1},{3,2},{4,3},{5,4},{6,5},{7,6},{8,7},{9,8},{10,9},{11,1... | collective-permute-start | bytes 1179656 | tf_op jit(solution)/shard_map/ppermute | solution.py:355
  33.0 2.9 %collective-permute-start.5 = (bf16[2,384,256]{2,1,0:T(8,128)(2,1)S(1)}, bf16[2,384,256]{2,1,0:T(8,128)(2,1)S(1)}, u32[]{:S(2)}, u32[]{:S(2)}) collective-permute-start(bf16[2,384,256]{2,1,0:T(8,128)(2,1)S(1)} %get-tuple-element.42), channel_id=1, source_target_pairs={{0,1},{1,2},{2,3},{3,4},{4,5},{5,6},{6,7},{7,8},{8,9},{9,10},{10,1... | collective-permute-start | bytes 1179656 | tf_op jit(solution)/shard_map/ppermute | solution.py:355
  36.0 3.5 %collective-permute-done.6.corners_after_in = bf16[2,384,256]{2,1,0:T(8,128)(2,1)S(1)} collective-permute-done((bf16[2,384,256]{2,1,0:T(8,128)(2,1)S(1)}, bf16[2,384,256]{2,1,0:T(8,128)(2,1)S(1)}, u32[]{:S(2)}, u32[]{:S(2)}) %collective-permute-start.6) | collective-permute-done | bytes 393248 | tf_op jit(solution)/shard_map/ppermute | solution.py:355
  41.4 18.1 %slots.1 = (f32[2,512,512]{2,1,0:T(8,128)}, bf16[2,896,256]{2,1,0:T(8,128)(2,1)}, bf16[2,896,256]{2,1,0:T(8,128)(2,1)}, bf16[2,192,512]{2,1,0:T(8,128)(2,1)}, bf...) custom-call(s32[96,32]{1,0:T(8,128)} %bitcast.10, s32[8,32]{1,0:T(8,128)} %counts.3, ...), custom_call_target="tpu_custom_call" | custom-call | tf_op jit(solution)/shard_map/slots/pallas_call | solution.py:361
  59.6 2.0 %collective-permute-done.7 = bf16[112,16,128]{2,1,0:T(8,128)(2,1)S(1)} collective-permute-done((bf16[112,16,128]{2,1,0:T(8,128)(2,1)}, bf16[112,16,128]{2,1,0:T(8,128)(2,1)S(1)}, u32[]{:S(2)}, u32[]{:S(2)}) %collective-permute-start.7) | collective-permute-done | bytes 458784 | tf_op jit(solution)/shard_map/ppermute | solution.py:471
  63.5 18.2 %all-to-all-start = ((bf16[16,7,16,128]{3,2,1,0:T(8,128)(2,1)}), bf16[16,7,16,128]{3,2,1,0:T(8,128)(2,1)S(1)}, u32[]{:S(2)}, u32[]{:S(2)}) async-start(bf16[16,7,16,128]{3,2,1,0:T(8,128)(2,1)} %bitcast.4), calls=%async_computation | async-start | bytes 917504 | tf_op jit(solution)/shard_map/all_to_all | solution.py:458
  81.8 4.0 %collective-permute-start.8 = (bf16[2,896,256]{2,1,0:T(8,128)(2,1)}, bf16[2,896,256]{2,1,0:T(8,128)(2,1)S(1)}, u32[]{:S(2)}, u32[]{:S(2)}) collective-permute-start(bf16[2,896,256]{2,1,0:T(8,128)(2,1)} %get-tuple-element.27), channel_id=1, source_target_pairs={{0,1},{1,2},{2,3},{3,4},{4,5},{5,6},{6,7},{7,8},{8,9},{9,10},{10,1... | collective-permute-start | bytes 2752520 | tf_op jit(solution)/shard_map/ppermute | solution.py:355
  85.9 1.9 %collective-permute-start.9 = (bf16[2,896,256]{2,1,0:T(8,128)(2,1)}, bf16[2,896,256]{2,1,0:T(8,128)(2,1)S(1)}, u32[]{:S(2)}, u32[]{:S(2)}) collective-permute-start(bf16[2,896,256]{2,1,0:T(8,128)(2,1)} %get-tuple-element.28), channel_id=1, source_target_pairs={{1,0},{2,1},{3,2},{4,3},{5,4},{6,5},{7,6},{8,7},{9,8},{10,9},{11,1... | collective-permute-start | bytes 2752520 | tf_op jit(solution)/shard_map/ppermute | solution.py:355
  87.8 12.2 %all-to-all-done.pieces = bf16[16,7,16,128]{3,2,1,0:T(8,128)(2,1)S(1)} async-done(((bf16[16,7,16,128]{3,2,1,0:T(8,128)(2,1)}), bf16[16,7,16,128]{3,2,1,0:T(8,128)(2,1)S(1)}, u32[]{:S(2)}, u32[]{:S(2)}) %all-to-all-start) | async-done | bytes 458784 | tf_op jit(solution)/shard_map/all_to_all | solution.py:458
  100.8 6.7 %all-to-all-start.1 = ((bf16[8,7,16,128]{3,2,1,0:T(8,128)(2,1)}), bf16[8,7,16,128]{3,2,1,0:T(8,128)(2,1)S(1)}, u32[]{:S(2)}, u32[]{:S(2)}) async-start(bf16[8,7,16,128]{3,2,1,0:T(8,128)(2,1)} %total.2), calls=%async_computation.1 | async-start | bytes 458752 | tf_op jit(solution)/shard_map/all_to_all | solution.py:458
  108.8 6.0 %collective-permute-start.10 = (bf16[2,192,512]{2,1,0:T(8,128)(2,1)}, bf16[2,192,512]{2,1,0:T(8,128)(2,1)S(1)}, u32[]{:S(2)}, u32[]{:S(2)}) collective-permute-start(bf16[2,192,512]{2,1,0:T(8,128)(2,1)} %get-tuple-element.34), channel_id=1, source_target_pairs={{96,128},{128,96},{97,129},{129,97},{98,130},{130,98},{99,131},{13... | collective-permute-start | bytes 1179656 | tf_op jit(solution)/shard_map/ppermute | solution.py:403
  116.2 4.8 %collective-permute-start.12 = (bf16[2,192,512]{2,1,0:T(8,128)(2,1)}, bf16[2,192,512]{2,1,0:T(8,128)(2,1)}, u32[]{:S(2)}, u32[]{:S(2)}) collective-permute-start(bf16[2,192,512]{2,1,0:T(8,128)(2,1)} %get-tuple-element.36), channel_id=1, source_target_pairs={{32,0},{64,32},{96,64},{160,128},{192,160},{224,192},{33,1},{65,33... | collective-permute-start | bytes 1179656 | tf_op jit(solution)/shard_map/ppermute | solution.py:408
  121.8 4.0 %all-to-all-start.2 = ((bf16[16,7,16,128]{3,2,1,0:T(8,128)(2,1)}), bf16[16,7,16,128]{3,2,1,0:T(8,128)(2,1)S(1)}, u32[]{:S(2)}, u32[]{:S(2)}) async-start(bf16[16,7,16,128]{3,2,1,0:T(8,128)(2,1)} %total.3), calls=%async_computation.2 | async-start | bytes 917504 | tf_op jit(solution)/shard_map/all_to_all | solution.py:458
  125.7 4.7 %new_object.1.base = f32[2,512,512]{2,1,0:T(8,128)} custom-call(f32[2,512,512]{2,1,0:T(8,128)} %center.3, f32[2,512,512]{2,1,0:T(8,128)} %get-tuple-element.26.field, bf16[2,896,256]{2,1,0:T(8,128)(2,1)} %copy-done.3, bf16[2,896,256]{2,1,0:T(8,128)(2,1)} %copy-done.4, f32[512,512]{1,0:T(8,128)} %illumination.1.weight.weight_in), custom_call_target="tpu_custom_call" | custom-call | flops 4000000 | bytes 12000000 | tf_op jit(solution)/shard_map/new_object/pallas_call | solution.py:487
  130.5 7.9 %collective-permute-done.10.across = bf16[2,192,512]{2,1,0:T(8,128)(2,1)S(1)} collective-permute-done((bf16[2,192,512]{2,1,0:T(8,128)(2,1)}, bf16[2,192,512]{2,1,0:T(8,128)(2,1)S(1)}, u32[]{:S(2)}, u32[]{:S(2)}) %collective-permute-start.10) | collective-permute-done | bytes 393248 | tf_op jit(solution)/shard_map/ppermute | solution.py:403
  138.4 3.5 %rims.1 = f32[2,512,512]{2,1,0:T(8,128)} custom-call(f32[2,512,512]{2,1,0:T(8,128)} %new_object.1.base, f32[512,512]{1,0:T(8,128)S(1)} %copy-done.1, bf16[2,192,512]{2,1,0:T(8,128)(2,1)S(1)} %collective-permute-done.10.across, bf16[2,192,512]{2,1,0:T(8,128)(2,1)S(1)} %collective-permute-done.11.from_above, ...), custom_call_target="tpu_custom_call", output_to_operand_aliasing={{}: (0, {})} | custom-call | flops 40000000000 | bytes 4000000 | tf_op jit(solution)/shard_map/rims/pallas_call | solution.py:496
  141.9 2.6 %collective-permute-start.13 = (bf16[112,16,128]{2,1,0:T(8,128)(2,1)S(1)}, bf16[112,16,128]{2,1,0:T(8,128)(2,1)S(1)}, u32[]{:S(2)}, u32[]{:S(2)}) collective-permute-start(bf16[112,16,128]{2,1,0:T(8,128)(2,1)S(1)} %bitcast.6), channel_id=1, source_target_pairs={{0,1},{1,0},{2,3},{3,2},{4,5},{5,4},{6,7},{7,6},{8,9},{9,8},{10,11... | collective-permute-start | bytes 1376264 | tf_op jit(solution)/shard_map/ppermute | solution.py:513
  146.0 1.9 %new_probe.1 = f32[2,384,384]{2,1,0:T(8,128)} custom-call(bf16[112,16,128]{2,1,0:T(8,128)(2,1)S(1)} %bitcast.7, bf16[112,16,128]{2,1,0:T(8,128)(2,1)S(1)} %collective-permute-done.13.other, f32[2,384,384]{2,1,0:T(8,128)S(1)} %copy-done), custom_call_target="tpu_custom_call" | custom-call | tf_op jit(solution)/shard_map/new_probe/pallas_call | solution.py:514
  (53 shorter events, 13.4 us)
Async XLA Ops:
  2.7 26.5 %collective-permute-start = (bf16[2,192,512]{2,1,0:T(8,128)(2,1)}, bf16[2,192,512]{2,1,0:T(8,128)(2,1)S(1)}, u32[]{:S(2)}, u32[]{:S(2)}) collective-permute-start(bf16[2,192,512]{2,1,0:T(8,128)(2,1)} %cut.1), channel_id=1, source_target_pairs={{96,128},{128,96},{97,129},{129,97},{98,130},{130,98},{99,131},{13... | collective-permute-start | bytes 1179656 | tf_op jit(solution)/shard_map/ppermute | solution.py:403
  10.5 18.7 %collective-permute-start.2 = (bf16[2,192,512]{2,1,0:T(8,128)(2,1)S(1)}, bf16[2,192,512]{2,1,0:T(8,128)(2,1)S(1)}, u32[]{:S(2)}, u32[]{:S(2)}) collective-permute-start(bf16[2,192,512]{2,1,0:T(8,128)(2,1)S(1)} %get-tuple-element.39), channel_id=1, source_target_pairs={{32,0},{64,32},{96,64},{160,128},{192,160},{224,192},{33,1},{65,33... | collective-permute-start | bytes 1179656 | tf_op jit(solution)/shard_map/ppermute | solution.py:408
  11.9 17.4 %collective-permute-start.1 = (bf16[2,192,512]{2,1,0:T(8,128)(2,1)S(1)}, bf16[2,192,512]{2,1,0:T(8,128)(2,1)S(1)}, u32[]{:S(2)}, u32[]{:S(2)}) collective-permute-start(bf16[2,192,512]{2,1,0:T(8,128)(2,1)S(1)} %get-tuple-element.40), channel_id=1, source_target_pairs={{0,32},{32,64},{64,96},{128,160},{160,192},{192,224},{1,33},{33,65... | collective-permute-start | bytes 1179656 | tf_op jit(solution)/shard_map/ppermute | solution.py:408
  14.0 21.9 %collective-permute-start.4 = (bf16[2,512,256]{2,1,0:T(8,128)(2,1)}, bf16[2,512,256]{2,1,0:T(8,128)(2,1)S(1)}, u32[]{:S(2)}, u32[]{:S(2)}) collective-permute-start(bf16[2,512,256]{2,1,0:T(8,128)(2,1)} %get-tuple-element.37), channel_id=1, source_target_pairs={{1,0},{2,1},{3,2},{4,3},{5,4},{6,5},{7,6},{8,7},{9,8},{10,9},{11,1... | collective-permute-start | bytes 1572872 | tf_op jit(solution)/shard_map/ppermute | solution.py:355
  16.9 19.1 %collective-permute-start.3 = (bf16[2,512,256]{2,1,0:T(8,128)(2,1)S(1)}, bf16[2,512,256]{2,1,0:T(8,128)(2,1)S(1)}, u32[]{:S(2)}, u32[]{:S(2)}) collective-permute-start(bf16[2,512,256]{2,1,0:T(8,128)(2,1)S(1)} %get-tuple-element.38), channel_id=1, source_target_pairs={{0,1},{1,2},{2,3},{3,4},{4,5},{5,6},{6,7},{7,8},{8,9},{9,10},{10,1... | collective-permute-start | bytes 1572872 | tf_op jit(solution)/shard_map/ppermute | solution.py:355
  29.3 11.4 %copy-start.5 = (bf16[2,192,512]{2,1,0:T(8,128)(2,1)}, bf16[2,192,512]{2,1,0:T(8,128)(2,1)S(1)}, u32[]{:S(2)}) copy-start(bf16[2,192,512]{2,1,0:T(8,128)(2,1)S(1)} %collective-permute-done.across_in) | copy-start | bytes 1179652
  29.4 10.0 %collective-permute-start.6 = (bf16[2,384,256]{2,1,0:T(8,128)(2,1)S(1)}, bf16[2,384,256]{2,1,0:T(8,128)(2,1)S(1)}, u32[]{:S(2)}, u32[]{:S(2)}) collective-permute-start(bf16[2,384,256]{2,1,0:T(8,128)(2,1)S(1)} %get-tuple-element.41), channel_id=1, source_target_pairs={{1,0},{2,1},{3,2},{4,3},{5,4},{6,5},{7,6},{8,7},{9,8},{10,9},{11,1... | collective-permute-start | bytes 1179656 | tf_op jit(solution)/shard_map/ppermute | solution.py:355
  33.0 7.6 %collective-permute-start.5 = (bf16[2,384,256]{2,1,0:T(8,128)(2,1)S(1)}, bf16[2,384,256]{2,1,0:T(8,128)(2,1)S(1)}, u32[]{:S(2)}, u32[]{:S(2)}) collective-permute-start(bf16[2,384,256]{2,1,0:T(8,128)(2,1)S(1)} %get-tuple-element.42), channel_id=1, source_target_pairs={{0,1},{1,2},{2,3},{3,4},{4,5},{5,6},{6,7},{7,8},{8,9},{9,10},{10,1... | collective-permute-start | bytes 1179656 | tf_op jit(solution)/shard_map/ppermute | solution.py:355
  59.5 2.1 %collective-permute-start.7 = (bf16[112,16,128]{2,1,0:T(8,128)(2,1)}, bf16[112,16,128]{2,1,0:T(8,128)(2,1)S(1)}, u32[]{:S(2)}, u32[]{:S(2)}) collective-permute-start(bf16[112,16,128]{2,1,0:T(8,128)(2,1)} %get-tuple-element.22), channel_id=1, source_target_pairs={{0,1},{1,0},{2,3},{3,2},{4,5},{5,4},{6,7},{7,6},{8,9},{9,8},{10,11... | collective-permute-start | bytes 1376264 | tf_op jit(solution)/shard_map/ppermute | solution.py:471
  63.5 36.4 %all-to-all-start = ((bf16[16,7,16,128]{3,2,1,0:T(8,128)(2,1)}), bf16[16,7,16,128]{3,2,1,0:T(8,128)(2,1)S(1)}, u32[]{:S(2)}, u32[]{:S(2)}) async-start(bf16[16,7,16,128]{3,2,1,0:T(8,128)(2,1)} %bitcast.4), calls=%async_computation | async-start | bytes 917504 | tf_op jit(solution)/shard_map/all_to_all | solution.py:458
  81.8 25.7 %copy-start.12 = (bf16[2,192,512]{2,1,0:T(8,128)(2,1)S(1)}, bf16[2,192,512]{2,1,0:T(8,128)(2,1)}, u32[]{:S(2)}) copy-start(bf16[2,192,512]{2,1,0:T(8,128)(2,1)} %get-tuple-element.30) | copy-start | bytes 1179652
  81.8 25.7 %copy-start.13 = (bf16[2,192,512]{2,1,0:T(8,128)(2,1)S(1)}, bf16[2,192,512]{2,1,0:T(8,128)(2,1)}, u32[]{:S(2)}) copy-start(bf16[2,192,512]{2,1,0:T(8,128)(2,1)} %get-tuple-element.31) | copy-start | bytes 1179652
  81.8 25.6 %collective-permute-start.8 = (bf16[2,896,256]{2,1,0:T(8,128)(2,1)}, bf16[2,896,256]{2,1,0:T(8,128)(2,1)S(1)}, u32[]{:S(2)}, u32[]{:S(2)}) collective-permute-start(bf16[2,896,256]{2,1,0:T(8,128)(2,1)} %get-tuple-element.27), channel_id=1, source_target_pairs={{0,1},{1,2},{2,3},{3,4},{4,5},{5,6},{6,7},{7,8},{8,9},{9,10},{10,1... | collective-permute-start | bytes 2752520 | tf_op jit(solution)/shard_map/ppermute | solution.py:355
  85.9 21.6 %collective-permute-start.9 = (bf16[2,896,256]{2,1,0:T(8,128)(2,1)}, bf16[2,896,256]{2,1,0:T(8,128)(2,1)S(1)}, u32[]{:S(2)}, u32[]{:S(2)}) collective-permute-start(bf16[2,896,256]{2,1,0:T(8,128)(2,1)} %get-tuple-element.28), channel_id=1, source_target_pairs={{1,0},{2,1},{3,2},{4,3},{5,4},{6,5},{7,6},{8,7},{9,8},{10,9},{11,1... | collective-permute-start | bytes 2752520 | tf_op jit(solution)/shard_map/ppermute | solution.py:355
  100.8 20.2 %all-to-all-start.1 = ((bf16[8,7,16,128]{3,2,1,0:T(8,128)(2,1)}), bf16[8,7,16,128]{3,2,1,0:T(8,128)(2,1)S(1)}, u32[]{:S(2)}, u32[]{:S(2)}) async-start(bf16[8,7,16,128]{3,2,1,0:T(8,128)(2,1)} %total.2), calls=%async_computation.1 | async-start | bytes 458752 | tf_op jit(solution)/shard_map/all_to_all | solution.py:458
  107.4 14.3 %copy-start.3 = (bf16[2,896,256]{2,1,0:T(8,128)(2,1)}, bf16[2,896,256]{2,1,0:T(8,128)(2,1)S(1)}, u32[]{:S(2)}) copy-start(bf16[2,896,256]{2,1,0:T(8,128)(2,1)S(1)} %collective-permute-done.8.from_before) | copy-start | bytes 2752516
  107.4 14.3 %copy-start.4 = (bf16[2,896,256]{2,1,0:T(8,128)(2,1)}, bf16[2,896,256]{2,1,0:T(8,128)(2,1)S(1)}, u32[]{:S(2)}) copy-start(bf16[2,896,256]{2,1,0:T(8,128)(2,1)S(1)} %collective-permute-done.9.from_after) | copy-start | bytes 2752516
  108.8 29.5 %collective-permute-start.10 = (bf16[2,192,512]{2,1,0:T(8,128)(2,1)}, bf16[2,192,512]{2,1,0:T(8,128)(2,1)S(1)}, u32[]{:S(2)}, u32[]{:S(2)}) collective-permute-start(bf16[2,192,512]{2,1,0:T(8,128)(2,1)} %get-tuple-element.34), channel_id=1, source_target_pairs={{96,128},{128,96},{97,129},{129,97},{98,130},{130,98},{99,131},{13... | collective-permute-start | bytes 1179656 | tf_op jit(solution)/shard_map/ppermute | solution.py:403
  114.9 23.5 %collective-permute-start.11 = (bf16[2,192,512]{2,1,0:T(8,128)(2,1)}, bf16[2,192,512]{2,1,0:T(8,128)(2,1)S(1)}, u32[]{:S(2)}, u32[]{:S(2)}) collective-permute-start(bf16[2,192,512]{2,1,0:T(8,128)(2,1)} %get-tuple-element.35), channel_id=1, source_target_pairs={{0,32},{32,64},{64,96},{128,160},{160,192},{192,224},{1,33},{33,65... | collective-permute-start | bytes 1179656 | tf_op jit(solution)/shard_map/ppermute | solution.py:408
  116.2 22.2 %collective-permute-start.12 = (bf16[2,192,512]{2,1,0:T(8,128)(2,1)}, bf16[2,192,512]{2,1,0:T(8,128)(2,1)}, u32[]{:S(2)}, u32[]{:S(2)}) collective-permute-start(bf16[2,192,512]{2,1,0:T(8,128)(2,1)} %get-tuple-element.36), channel_id=1, source_target_pairs={{32,0},{64,32},{96,64},{160,128},{192,160},{224,192},{33,1},{65,33... | collective-permute-start | bytes 1179656 | tf_op jit(solution)/shard_map/ppermute | solution.py:408
  121.8 20.1 %all-to-all-start.2 = ((bf16[16,7,16,128]{3,2,1,0:T(8,128)(2,1)}), bf16[16,7,16,128]{3,2,1,0:T(8,128)(2,1)S(1)}, u32[]{:S(2)}, u32[]{:S(2)}) async-start(bf16[16,7,16,128]{3,2,1,0:T(8,128)(2,1)} %total.3), calls=%async_computation.2 | async-start | bytes 917504 | tf_op jit(solution)/shard_map/all_to_all | solution.py:458
  125.7 12.6 %copy-start.1 = (f32[512,512]{1,0:T(8,128)S(1)}, f32[512,512]{1,0:T(8,128)}, u32[]{:S(2)}) copy-start(f32[512,512]{1,0:T(8,128)} %illumination.1.weight.weight_in) | copy-start | bytes 3145732
  130.5 15.5 %copy-start = (f32[2,384,384]{2,1,0:T(8,128)S(1)}, f32[2,384,384]{2,1,0:T(8,128)}, u32[]{:S(2)}) copy-start(f32[2,384,384]{2,1,0:T(8,128)} %probe.3) | copy-start | bytes 3538948
  141.9 4.1 %collective-permute-start.13 = (bf16[112,16,128]{2,1,0:T(8,128)(2,1)S(1)}, bf16[112,16,128]{2,1,0:T(8,128)(2,1)S(1)}, u32[]{:S(2)}, u32[]{:S(2)}) collective-permute-start(bf16[112,16,128]{2,1,0:T(8,128)(2,1)S(1)} %bitcast.6), channel_id=1, source_target_pairs={{0,1},{1,0},{2,3},{3,2},{4,5},{5,4},{6,7},{7,6},{8,9},{9,8},{10,11... | collective-permute-start | bytes 1376264 | tf_op jit(solution)/shard_map/ppermute | solution.py:513
  (7 other events, 43.8 us)

commit v2 on v1

--- a/solution.py
+++ b/solution.py
@@ -361,13 +361,13 @@
     return pl.pallas_call(
         main_kernel,
         out_shape=(
-            like((2, TH, TW), F32),
-            like((2, EH, 256), BF16),
-            like((2, EH, 256), BF16),
-            like((2, HALF, TW), BF16),
-            like((2, HALF, TW), BF16),
+            pltpu.HBM((2, TH, TW), F32),
+            pltpu.HBM((2, EH, 256), BF16),
+            pltpu.HBM((2, EH, 256), BF16),
+            pltpu.HBM((2, HALF, TW), BF16),
+            pltpu.HBM((2, HALF, TW), BF16),
             like((BLOCKS, 16, 128), BF16),
-            like((BLOCKS, 16, 128), BF16),
+            pltpu.HBM((BLOCKS, 16, 128), BF16),
         ),
         in_specs=[SMEM] * 2 + [ANY] * 11,
         out_specs=(ANY,) + (VMEM,) * 6,
@@ -394,7 +394,7 @@
             pltpu.SemaphoreType.DMA((16,)),
             pltpu.SemaphoreType.DMA((PMAX,)),
         ],
-        compiler_params=params(60),
+        compiler_params=params(38),
         name="slots",
     )(*arrays, jnp.asarray(forward))
 

time: 149 us -> 150 us (level)
  Pallas kernels: 38.6 us -> 36.2 us
  local copies, waits for them, and re-layouts: 1.66 us -> 3.29 us
  transfers between devices with their start and end apart: 17 -> 17, of which waited for: 7 -> 7; matrix products, arithmetic and copies ran while one was open for 2% -> 4% of each run, Pallas kernels for 11% -> 10%
where the time goes in v2:
time: 150 us; the launch traced here: 148 us
  starting transfers between devices  72.8 us (49%)
  Pallas kernels  36.2 us (24%)
  waiting for transfers between devices  29.9 us (20%)
  other arithmetic  4.76 us (3%)
  local copies, waits for them, and re-layouts  3.29 us (2%)
    all_to_all x3, starting transfers between devices, exchanged(): lax.all_to_all(pieces, ('row', 'col'), 0, 0, axis_index_groups=groups)  28 us
    ppermute x6, starting transfers between devices, shifted(): return lax.ppermute(value, axis, [(k, k + step) for k in range(low, high)])  18.3 us
    pallas_call x1, Pallas kernels, slots_call(): pl.pallas_call(main_kernel, out_shape=(pltpu.HBM((2, TH, TW), F32), pltpu...  17.1 us
    ppermute x2, starting transfers between devices, across_edge(): return lax.ppermute(value, 'row', [(EDGE - 1, EDGE), (EDGE, EDGE - 1)])  14.3 us
    all_to_all x3, waiting for transfers between devices, exchanged(): lax.all_to_all(pieces, ('row', 'col'), 0, 0, axis_index_groups=groups)  12.2 us
    ppermute x2, waiting for transfers between devices, across_edge(): return lax.ppermute(value, 'row', [(EDGE - 1, EDGE), (EDGE, EDGE - 1)])  9.55 us
    ppermute x4, starting transfers between devices, within_halves(): return lax.ppermute(value, 'row', [(k, k + step) for k in rows])  9.35 us
    pallas_call x1, Pallas kernels, on_device(): pl.pallas_call(illumination_kernel, out_shape=like((TH, TW), F32), in_spe...  5.3 us
  transfers between devices with their start and end apart: 17, of which 7 were waited for; matrix products, arithmetic and copies ran while one was open for 4% of the time, Pallas kernels for 10%

profile of v2, /device:TPU:57, one launch (start us, length us, event | category | flops | bytes accessed | tf_op | source)
XLA Modules:
  0.0 147.9 jit_solution(15668495055552018939)
XLA Ops:
  0.6 2.1 %cut.1 = bf16[2,192,512]{2,1,0:T(8,128)(2,1)} custom-call(f32[2,512,512]{2,1,0:T(8,128)} %center.3), custom_call_target="tpu_custom_call" | custom-call | flops 400000 | bytes 1200000 | tf_op jit(solution)/shard_map/cut/pallas_call | solution.py:416
  2.7 7.6 %collective-permute-start = (bf16[2,192,512]{2,1,0:T(8,128)(2,1)}, bf16[2,192,512]{2,1,0:T(8,128)(2,1)}, u32[]{:S(2)}, u32[]{:S(2)}) collective-permute-start(bf16[2,192,512]{2,1,0:T(8,128)(2,1)} %cut.1), channel_id=1, source_target_pairs={{96,128},{128,96},{97,129},{129,97},{98,130},{130,98},{99,131},{13... | collective-permute-start | bytes 1179656 | tf_op jit(solution)/shard_map/ppermute | solution.py:403
  11.4 2.0 %collective-permute-start.2 = (bf16[2,192,512]{2,1,0:T(8,128)(2,1)}, bf16[2,192,512]{2,1,0:T(8,128)(2,1)}, u32[]{:S(2)}, u32[]{:S(2)}) collective-permute-start(bf16[2,192,512]{2,1,0:T(8,128)(2,1)} %get-tuple-element.39), channel_id=1, source_target_pairs={{32,0},{64,32},{96,64},{160,128},{192,160},{224,192},{33,1},{65,33... | collective-permute-start | bytes 1179656 | tf_op jit(solution)/shard_map/ppermute | solution.py:408
  15.8 2.9 %collective-permute-start.4 = (bf16[2,512,256]{2,1,0:T(8,128)(2,1)}, bf16[2,512,256]{2,1,0:T(8,128)(2,1)}, u32[]{:S(2)}, u32[]{:S(2)}) collective-permute-start(bf16[2,512,256]{2,1,0:T(8,128)(2,1)} %get-tuple-element.37), channel_id=1, source_target_pairs={{1,0},{2,1},{3,2},{4,3},{5,4},{6,5},{7,6},{8,7},{9,8},{10,9},{11,1... | collective-permute-start | bytes 1572872 | tf_op jit(solution)/shard_map/ppermute | solution.py:355
  18.6 3.0 %collective-permute-start.3 = (bf16[2,512,256]{2,1,0:T(8,128)(2,1)}, bf16[2,512,256]{2,1,0:T(8,128)(2,1)}, u32[]{:S(2)}, u32[]{:S(2)}) collective-permute-start(bf16[2,512,256]{2,1,0:T(8,128)(2,1)} %get-tuple-element.38), channel_id=1, source_target_pairs={{0,1},{1,2},{2,3},{3,4},{4,5},{5,6},{6,7},{7,8},{8,9},{9,10},{10,1... | collective-permute-start | bytes 1572872 | tf_op jit(solution)/shard_map/ppermute | solution.py:355
  21.7 5.3 %illumination.1.weight.weight_in = f32[512,512]{1,0:T(8,128)} custom-call(s32[96,32]{1,0:T(8,128)} %bitcast.9, s32[8,32]{1,0:T(8,128)} %counts.3, f32[2,384,384]{2,1,0:T(8,128)} %probe.3), custom_call_target="tpu_custom_call" | custom-call | flops 20000000 | bytes 20000000 | tf_op jit(solution)/shard_map/illumination/pallas_call | solution.py:431
  27.0 2.4 %collective-permute-done.across_in = bf16[2,192,512]{2,1,0:T(8,128)(2,1)} collective-permute-done((bf16[2,192,512]{2,1,0:T(8,128)(2,1)}, bf16[2,192,512]{2,1,0:T(8,128)(2,1)}, u32[]{:S(2)}, u32[]{:S(2)}) %collective-permute-start) | collective-permute-done | bytes 393248 | tf_op jit(solution)/shard_map/ppermute | solution.py:403
  30.6 3.7 %collective-permute-start.6 = (bf16[2,384,256]{2,1,0:T(8,128)(2,1)S(1)}, bf16[2,384,256]{2,1,0:T(8,128)(2,1)S(1)}, u32[]{:S(2)}, u32[]{:S(2)}) collective-permute-start(bf16[2,384,256]{2,1,0:T(8,128)(2,1)S(1)} %get-tuple-element.41), channel_id=1, source_target_pairs={{1,0},{2,1},{3,2},{4,3},{5,4},{6,5},{7,6},{8,7},{9,8},{10,9},{11,1... | collective-permute-start | bytes 1179656 | tf_op jit(solution)/shard_map/ppermute | solution.py:355
  34.3 2.8 %collective-permute-start.5 = (bf16[2,384,256]{2,1,0:T(8,128)(2,1)S(1)}, bf16[2,384,256]{2,1,0:T(8,128)(2,1)S(1)}, u32[]{:S(2)}, u32[]{:S(2)}) collective-permute-start(bf16[2,384,256]{2,1,0:T(8,128)(2,1)S(1)} %get-tuple-element.42), channel_id=1, source_target_pairs={{0,1},{1,2},{2,3},{3,4},{4,5},{5,6},{6,7},{7,8},{8,9},{9,10},{10,1... | collective-permute-start | bytes 1179656 | tf_op jit(solution)/shard_map/ppermute | solution.py:355
  37.1 3.5 %collective-permute-done.6.corners_after_in = bf16[2,384,256]{2,1,0:T(8,128)(2,1)S(1)} collective-permute-done((bf16[2,384,256]{2,1,0:T(8,128)(2,1)S(1)}, bf16[2,384,256]{2,1,0:T(8,128)(2,1)S(1)}, u32[]{:S(2)}, u32[]{:S(2)}) %collective-permute-start.6) | collective-permute-done | bytes 393248 | tf_op jit(solution)/shard_map/ppermute | solution.py:355
  43.1 17.1 %slots.1 = (f32[2,512,512]{2,1,0:T(8,128)}, bf16[2,896,256]{2,1,0:T(8,128)(2,1)}, bf16[2,896,256]{2,1,0:T(8,128)(2,1)}, bf16[2,192,512]{2,1,0:T(8,128)(2,1)}, bf...) custom-call(s32[96,32]{1,0:T(8,128)S(1)} %bitcast.10, ...), custom_call_target="tpu_custom_call" | custom-call | tf_op jit(solution)/shard_map/slots/pallas_call | solution.py:361
  60.3 2.0 %collective-permute-done.7 = bf16[112,16,128]{2,1,0:T(8,128)(2,1)S(1)} collective-permute-done((bf16[112,16,128]{2,1,0:T(8,128)(2,1)}, bf16[112,16,128]{2,1,0:T(8,128)(2,1)S(1)}, u32[]{:S(2)}, u32[]{:S(2)}) %collective-permute-start.7) | collective-permute-done | bytes 458784 | tf_op jit(solution)/shard_map/ppermute | solution.py:471
  63.2 18.2 %all-to-all-start = ((bf16[16,7,16,128]{3,2,1,0:T(8,128)(2,1)}), bf16[16,7,16,128]{3,2,1,0:T(8,128)(2,1)S(1)}, u32[]{:S(2)}, u32[]{:S(2)}) async-start(bf16[16,7,16,128]{3,2,1,0:T(8,128)(2,1)} %bitcast.4), calls=%async_computation | async-start | bytes 917504 | tf_op jit(solution)/shard_map/all_to_all | solution.py:458
  81.5 4.0 %collective-permute-start.8 = (bf16[2,896,256]{2,1,0:T(8,128)(2,1)}, bf16[2,896,256]{2,1,0:T(8,128)(2,1)S(1)}, u32[]{:S(2)}, u32[]{:S(2)}) collective-permute-start(bf16[2,896,256]{2,1,0:T(8,128)(2,1)} %get-tuple-element.27), channel_id=1, source_target_pairs={{0,1},{1,2},{2,3},{3,4},{4,5},{5,6},{6,7},{7,8},{8,9},{9,10},{10,1... | collective-permute-start | bytes 2752520 | tf_op jit(solution)/shard_map/ppermute | solution.py:355
  87.4 12.2 %all-to-all-done.pieces = bf16[16,7,16,128]{3,2,1,0:T(8,128)(2,1)S(1)} async-done(((bf16[16,7,16,128]{3,2,1,0:T(8,128)(2,1)}), bf16[16,7,16,128]{3,2,1,0:T(8,128)(2,1)S(1)}, u32[]{:S(2)}, u32[]{:S(2)}) %all-to-all-start) | async-done | bytes 458784 | tf_op jit(solution)/shard_map/all_to_all | solution.py:458
  100.4 5.8 %all-to-all-start.1 = ((bf16[8,7,16,128]{3,2,1,0:T(8,128)(2,1)}), bf16[8,7,16,128]{3,2,1,0:T(8,128)(2,1)S(1)}, u32[]{:S(2)}, u32[]{:S(2)}) async-start(bf16[8,7,16,128]{3,2,1,0:T(8,128)(2,1)} %total.2), calls=%async_computation.1 | async-start | bytes 458752 | tf_op jit(solution)/shard_map/all_to_all | solution.py:458
  106.2 2.5 %broadcast_select_fusion.1 = (bf16[2,192,512]{2,1,0:T(8,128)(2,1)}, bf16[2,192,512]{2,1,0:T(8,128)(2,1)}, bf16[2,192,512]{2,1,0:T(8,128)(2,1)}) fusion(pred[]{:T(512)S(6)} %eq.7, bf16[2,896,256]{2,1,0:T(8,128)(2,1)} %collective-permute-done.9.from_after, bf16[2,896,256]{2,1,0:T(8,128)(2,1)S(1)} %collective-permute-done.8.from_before, ...), kind=kLoop, calls=%fused_computation.10 | loop fusion | flops 2949120 | bytes 3801089 | tf_op jit(solution)/shard_map/jit(_where)/select_n | solution.py:482
  108.7 6.8 %collective-permute-start.10 = (bf16[2,192,512]{2,1,0:T(8,128)(2,1)}, bf16[2,192,512]{2,1,0:T(8,128)(2,1)S(1)}, u32[]{:S(2)}, u32[]{:S(2)}) collective-permute-start(bf16[2,192,512]{2,1,0:T(8,128)(2,1)} %get-tuple-element.34), channel_id=1, source_target_pairs={{96,128},{128,96},{97,129},{129,97},{98,130},{130,98},{99,131},{13... | collective-permute-start | bytes 1179656 | tf_op jit(solution)/shard_map/ppermute | solution.py:403
  116.8 4.7 %collective-permute-start.12 = (bf16[2,192,512]{2,1,0:T(8,128)(2,1)}, bf16[2,192,512]{2,1,0:T(8,128)(2,1)}, u32[]{:S(2)}, u32[]{:S(2)}) collective-permute-start(bf16[2,192,512]{2,1,0:T(8,128)(2,1)} %get-tuple-element.36), channel_id=1, source_target_pairs={{32,0},{64,32},{96,64},{160,128},{192,160},{224,192},{33,1},{65,33... | collective-permute-start | bytes 1179656 | tf_op jit(solution)/shard_map/ppermute | solution.py:408
  122.3 4.0 %all-to-all-start.2 = ((bf16[16,7,16,128]{3,2,1,0:T(8,128)(2,1)}), bf16[16,7,16,128]{3,2,1,0:T(8,128)(2,1)S(1)}, u32[]{:S(2)}, u32[]{:S(2)}) async-start(bf16[16,7,16,128]{3,2,1,0:T(8,128)(2,1)} %total.3), calls=%async_computation.2 | async-start | bytes 917504 | tf_op jit(solution)/shard_map/all_to_all | solution.py:458
  126.3 4.7 %new_object.1.base = f32[2,512,512]{2,1,0:T(8,128)} custom-call(f32[2,512,512]{2,1,0:T(8,128)} %center.3, f32[2,512,512]{2,1,0:T(8,128)} %get-tuple-element.26.field, bf16[2,896,256]{2,1,0:T(8,128)(2,1)} %copy-done.7, bf16[2,896,256]{2,1,0:T(8,128)(2,1)} %collective-permute-done.9.from_after, f32[512,512]{1,0:T(8,128)} %illumination.1.weight.weight_in), custom_call_target="tpu_custom_call" | custom-call | flops 4000000 | bytes 12000000 | tf_op jit(solution)/shard_map/new_object/pallas_call | solution.py:487
  131.0 7.2 %collective-permute-done.10.across = bf16[2,192,512]{2,1,0:T(8,128)(2,1)S(1)} collective-permute-done((bf16[2,192,512]{2,1,0:T(8,128)(2,1)}, bf16[2,192,512]{2,1,0:T(8,128)(2,1)S(1)}, u32[]{:S(2)}, u32[]{:S(2)}) %collective-permute-start.10) | collective-permute-done | bytes 393248 | tf_op jit(solution)/shard_map/ppermute | solution.py:403
  138.2 3.5 %rims.1 = f32[2,512,512]{2,1,0:T(8,128)} custom-call(f32[2,512,512]{2,1,0:T(8,128)} %new_object.1.base, f32[512,512]{1,0:T(8,128)S(1)} %copy-done.2, bf16[2,192,512]{2,1,0:T(8,128)(2,1)S(1)} %collective-permute-done.10.across, bf16[2,192,512]{2,1,0:T(8,128)(2,1)S(1)} %collective-permute-done.11.from_above, ...), custom_call_target="tpu_custom_call", output_to_operand_aliasing={{}: (0, {})} | custom-call | flops 40000000000 | bytes 4000000 | tf_op jit(solution)/shard_map/rims/pallas_call | solution.py:496
  141.7 2.7 %collective-permute-start.13 = (bf16[112,16,128]{2,1,0:T(8,128)(2,1)S(1)}, bf16[112,16,128]{2,1,0:T(8,128)(2,1)S(1)}, u32[]{:S(2)}, u32[]{:S(2)}) collective-permute-start(bf16[112,16,128]{2,1,0:T(8,128)(2,1)S(1)} %bitcast.6), channel_id=1, source_target_pairs={{0,1},{1,0},{2,3},{3,2},{4,5},{5,4},{6,7},{7,6},{8,9},{9,8},{10,11... | collective-permute-start | bytes 1376264 | tf_op jit(solution)/shard_map/ppermute | solution.py:513
  (45 shorter events, 16.3 us)
Async XLA Ops:
  2.7 26.6 %collective-permute-start = (bf16[2,192,512]{2,1,0:T(8,128)(2,1)}, bf16[2,192,512]{2,1,0:T(8,128)(2,1)}, u32[]{:S(2)}, u32[]{:S(2)}) collective-permute-start(bf16[2,192,512]{2,1,0:T(8,128)(2,1)} %cut.1), channel_id=1, source_target_pairs={{96,128},{128,96},{97,129},{129,97},{98,130},{130,98},{99,131},{13... | collective-permute-start | bytes 1179656 | tf_op jit(solution)/shard_map/ppermute | solution.py:403
  11.4 17.9 %collective-permute-start.2 = (bf16[2,192,512]{2,1,0:T(8,128)(2,1)}, bf16[2,192,512]{2,1,0:T(8,128)(2,1)}, u32[]{:S(2)}, u32[]{:S(2)}) collective-permute-start(bf16[2,192,512]{2,1,0:T(8,128)(2,1)} %get-tuple-element.39), channel_id=1, source_target_pairs={{32,0},{64,32},{96,64},{160,128},{192,160},{224,192},{33,1},{65,33... | collective-permute-start | bytes 1179656 | tf_op jit(solution)/shard_map/ppermute | solution.py:408
  13.5 15.9 %collective-permute-start.1 = (bf16[2,192,512]{2,1,0:T(8,128)(2,1)}, bf16[2,192,512]{2,1,0:T(8,128)(2,1)}, u32[]{:S(2)}, u32[]{:S(2)}) collective-permute-start(bf16[2,192,512]{2,1,0:T(8,128)(2,1)} %get-tuple-element.40), channel_id=1, source_target_pairs={{0,32},{32,64},{64,96},{128,160},{160,192},{192,224},{1,33},{33,65... | collective-permute-start | bytes 1179656 | tf_op jit(solution)/shard_map/ppermute | solution.py:408
  15.8 21.3 %collective-permute-start.4 = (bf16[2,512,256]{2,1,0:T(8,128)(2,1)}, bf16[2,512,256]{2,1,0:T(8,128)(2,1)}, u32[]{:S(2)}, u32[]{:S(2)}) collective-permute-start(bf16[2,512,256]{2,1,0:T(8,128)(2,1)} %get-tuple-element.37), channel_id=1, source_target_pairs={{1,0},{2,1},{3,2},{4,3},{5,4},{6,5},{7,6},{8,7},{9,8},{10,9},{11,1... | collective-permute-start | bytes 1572872 | tf_op jit(solution)/shard_map/ppermute | solution.py:355
  18.6 18.5 %collective-permute-start.3 = (bf16[2,512,256]{2,1,0:T(8,128)(2,1)}, bf16[2,512,256]{2,1,0:T(8,128)(2,1)}, u32[]{:S(2)}, u32[]{:S(2)}) collective-permute-start(bf16[2,512,256]{2,1,0:T(8,128)(2,1)} %get-tuple-element.38), channel_id=1, source_target_pairs={{0,1},{1,2},{2,3},{3,4},{4,5},{5,6},{6,7},{7,8},{8,9},{9,10},{10,1... | collective-permute-start | bytes 1572872 | tf_op jit(solution)/shard_map/ppermute | solution.py:355
  27.0 14.8 %copy-start.1 = (f32[2,384,384]{2,1,0:T(8,128)S(1)}, f32[2,384,384]{2,1,0:T(8,128)}, u32[]{:S(2)}) copy-start(f32[2,384,384]{2,1,0:T(8,128)} %probe.3) | copy-start | bytes 3538948
  27.0 14.8 %copy-start.3 = (bf16[1,1,6,384,384]{4,3,2,1,0:T(8,128)(2,1)S(1)}, bf16[1,1,6,384,384]{4,3,2,1,0:T(8,128)(2,1)}, u32[]{:S(2)}) copy-start(bf16[1,1,6,384,384]{4,3,2,1,0:T(8,128)(2,1)} %param.8) | copy-start | bytes 5308420
  27.0 14.8 %copy-start.5 = (s32[8,32,6,2]{1,3,2,0:T(2,128)S(1)}, s32[8,32,6,2]{1,3,2,0:T(2,128)}, u32[]{:S(2)}) copy-start(s32[8,32,6,2]{1,3,2,0:T(2,128)} %param.9) | copy-start | bytes 36868
  27.0 14.8 %copy-start.6 = (s32[8,32]{1,0:T(8,128)S(1)}, s32[8,32]{1,0:T(8,128)}, u32[]{:S(2)}) copy-start(s32[8,32]{1,0:T(8,128)} %counts.3) | copy-start | bytes 3076
  30.6 10.0 %collective-permute-start.6 = (bf16[2,384,256]{2,1,0:T(8,128)(2,1)S(1)}, bf16[2,384,256]{2,1,0:T(8,128)(2,1)S(1)}, u32[]{:S(2)}, u32[]{:S(2)}) collective-permute-start(bf16[2,384,256]{2,1,0:T(8,128)(2,1)S(1)} %get-tuple-element.41), channel_id=1, source_target_pairs={{1,0},{2,1},{3,2},{4,3},{5,4},{6,5},{7,6},{8,7},{9,8},{10,9},{11,1... | collective-permute-start | bytes 1179656 | tf_op jit(solution)/shard_map/ppermute | solution.py:355
  34.3 7.5 %collective-permute-start.5 = (bf16[2,384,256]{2,1,0:T(8,128)(2,1)S(1)}, bf16[2,384,256]{2,1,0:T(8,128)(2,1)S(1)}, u32[]{:S(2)}, u32[]{:S(2)}) collective-permute-start(bf16[2,384,256]{2,1,0:T(8,128)(2,1)S(1)} %get-tuple-element.42), channel_id=1, source_target_pairs={{0,1},{1,2},{2,3},{3,4},{4,5},{5,6},{6,7},{7,8},{8,9},{9,10},{10,1... | collective-permute-start | bytes 1179656 | tf_op jit(solution)/shard_map/ppermute | solution.py:355
  60.2 2.1 %collective-permute-start.7 = (bf16[112,16,128]{2,1,0:T(8,128)(2,1)}, bf16[112,16,128]{2,1,0:T(8,128)(2,1)S(1)}, u32[]{:S(2)}, u32[]{:S(2)}) collective-permute-start(bf16[112,16,128]{2,1,0:T(8,128)(2,1)} %get-tuple-element.22), channel_id=1, source_target_pairs={{0,1},{1,0},{2,3},{3,2},{4,5},{5,4},{6,7},{7,6},{8,9},{9,8},{10,11... | collective-permute-start | bytes 1376264 | tf_op jit(solution)/shard_map/ppermute | solution.py:471
  63.2 36.4 %all-to-all-start = ((bf16[16,7,16,128]{3,2,1,0:T(8,128)(2,1)}), bf16[16,7,16,128]{3,2,1,0:T(8,128)(2,1)S(1)}, u32[]{:S(2)}, u32[]{:S(2)}) async-start(bf16[16,7,16,128]{3,2,1,0:T(8,128)(2,1)} %bitcast.4), calls=%async_computation | async-start | bytes 917504 | tf_op jit(solution)/shard_map/all_to_all | solution.py:458
  81.4 24.8 %copy-start.8 = (bf16[2,192,512]{2,1,0:T(8,128)(2,1)S(1)}, bf16[2,192,512]{2,1,0:T(8,128)(2,1)}, u32[]{:S(2)}) copy-start(bf16[2,192,512]{2,1,0:T(8,128)(2,1)} %get-tuple-element.30) | copy-start | bytes 1179652
  81.4 24.8 %copy-start.9 = (bf16[2,192,512]{2,1,0:T(8,128)(2,1)S(1)}, bf16[2,192,512]{2,1,0:T(8,128)(2,1)}, u32[]{:S(2)}) copy-start(bf16[2,192,512]{2,1,0:T(8,128)(2,1)} %get-tuple-element.31) | copy-start | bytes 1179652
  81.5 24.8 %collective-permute-start.8 = (bf16[2,896,256]{2,1,0:T(8,128)(2,1)}, bf16[2,896,256]{2,1,0:T(8,128)(2,1)S(1)}, u32[]{:S(2)}, u32[]{:S(2)}) collective-permute-start(bf16[2,896,256]{2,1,0:T(8,128)(2,1)} %get-tuple-element.27), channel_id=1, source_target_pairs={{0,1},{1,2},{2,3},{3,4},{4,5},{5,6},{6,7},{7,8},{8,9},{9,10},{10,1... | collective-permute-start | bytes 2752520 | tf_op jit(solution)/shard_map/ppermute | solution.py:355
  85.5 20.7 %collective-permute-start.9 = (bf16[2,896,256]{2,1,0:T(8,128)(2,1)}, bf16[2,896,256]{2,1,0:T(8,128)(2,1)}, u32[]{:S(2)}, u32[]{:S(2)}) collective-permute-start(bf16[2,896,256]{2,1,0:T(8,128)(2,1)} %get-tuple-element.28), channel_id=1, source_target_pairs={{1,0},{2,1},{3,2},{4,3},{5,4},{6,5},{7,6},{8,7},{9,8},{10,9},{11,1... | collective-permute-start | bytes 2752520 | tf_op jit(solution)/shard_map/ppermute | solution.py:355
  100.4 21.1 %all-to-all-start.1 = ((bf16[8,7,16,128]{3,2,1,0:T(8,128)(2,1)}), bf16[8,7,16,128]{3,2,1,0:T(8,128)(2,1)S(1)}, u32[]{:S(2)}, u32[]{:S(2)}) async-start(bf16[8,7,16,128]{3,2,1,0:T(8,128)(2,1)} %total.2), calls=%async_computation.1 | async-start | bytes 458752 | tf_op jit(solution)/shard_map/all_to_all | solution.py:458
  108.7 29.5 %collective-permute-start.10 = (bf16[2,192,512]{2,1,0:T(8,128)(2,1)}, bf16[2,192,512]{2,1,0:T(8,128)(2,1)S(1)}, u32[]{:S(2)}, u32[]{:S(2)}) collective-permute-start(bf16[2,192,512]{2,1,0:T(8,128)(2,1)} %get-tuple-element.34), channel_id=1, source_target_pairs={{96,128},{128,96},{97,129},{129,97},{98,130},{130,98},{99,131},{13... | collective-permute-start | bytes 1179656 | tf_op jit(solution)/shard_map/ppermute | solution.py:403
  115.5 22.7 %collective-permute-start.11 = (bf16[2,192,512]{2,1,0:T(8,128)(2,1)}, bf16[2,192,512]{2,1,0:T(8,128)(2,1)S(1)}, u32[]{:S(2)}, u32[]{:S(2)}) collective-permute-start(bf16[2,192,512]{2,1,0:T(8,128)(2,1)} %get-tuple-element.35), channel_id=1, source_target_pairs={{0,32},{32,64},{64,96},{128,160},{160,192},{192,224},{1,33},{33,65... | collective-permute-start | bytes 1179656 | tf_op jit(solution)/shard_map/ppermute | solution.py:408
  116.8 21.4 %collective-permute-start.12 = (bf16[2,192,512]{2,1,0:T(8,128)(2,1)}, bf16[2,192,512]{2,1,0:T(8,128)(2,1)}, u32[]{:S(2)}, u32[]{:S(2)}) collective-permute-start(bf16[2,192,512]{2,1,0:T(8,128)(2,1)} %get-tuple-element.36), channel_id=1, source_target_pairs={{32,0},{64,32},{96,64},{160,128},{192,160},{224,192},{33,1},{65,33... | collective-permute-start | bytes 1179656 | tf_op jit(solution)/shard_map/ppermute | solution.py:408
  122.3 19.4 %all-to-all-start.2 = ((bf16[16,7,16,128]{3,2,1,0:T(8,128)(2,1)}), bf16[16,7,16,128]{3,2,1,0:T(8,128)(2,1)S(1)}, u32[]{:S(2)}, u32[]{:S(2)}) async-start(bf16[16,7,16,128]{3,2,1,0:T(8,128)(2,1)} %total.3), calls=%async_computation.2 | async-start | bytes 917504 | tf_op jit(solution)/shard_map/all_to_all | solution.py:458
  126.3 11.9 %copy-start.2 = (f32[512,512]{1,0:T(8,128)S(1)}, f32[512,512]{1,0:T(8,128)}, u32[]{:S(2)}) copy-start(f32[512,512]{1,0:T(8,128)} %illumination.1.weight.weight_in) | copy-start | bytes 3145732
  141.7 4.2 %collective-permute-start.13 = (bf16[112,16,128]{2,1,0:T(8,128)(2,1)S(1)}, bf16[112,16,128]{2,1,0:T(8,128)(2,1)S(1)}, u32[]{:S(2)}, u32[]{:S(2)}) collective-permute-start(bf16[112,16,128]{2,1,0:T(8,128)(2,1)S(1)} %bitcast.6), channel_id=1, source_target_pairs={{0,1},{1,0},{2,3},{3,2},{4,5},{5,4},{6,7},{7,6},{8,9},{9,8},{10,11... | collective-permute-start | bytes 1376264 | tf_op jit(solution)/shard_map/ppermute | solution.py:513
  (3 other events, 13.5 us)

commit v3 on v1

--- a/solution.py
+++ b/solution.py
@@ -156,17 +156,19 @@
     for copy in copies[:6]:
         copy.wait()
     for p in range(2):
-        for j in range(EW // 128):
-            if 2 <= j < 6:
-                cols = pl.ds((j - 2) * 128, 128)
-                over, under, low = above, below, 0
-            else:
-                cols = pl.ds(j % 2 * 128, 128)
-                middle, over = (before, corners_before) if j < 2 else (after, corners_after)
-                under, low = over, HALF
-                extended[p, j, pl.ds(HALF, TH), :] = middle[p, :, cols].astype(F32)
-            extended[p, j, pl.ds(0, HALF), :] = over[p, pl.ds(0, HALF), cols].astype(F32)
-            extended[p, j, pl.ds(HALF + TH, HALF), :] = under[p, pl.ds(low, HALF), cols].astype(F32)
+        for j in range(2, 6):
+            cols = pl.ds((j - 2) * 128, 128)
+            extended[p, j, pl.ds(0, HALF), :] = above[p, :, cols].astype(F32)
+            extended[p, j, pl.ds(HALF + TH, HALF), :] = below[p, :, cols].astype(F32)
+        for middle, corners, whole, part in ((before, corners_before, 1, 0), (after, corners_after, 6, 7)):
+            extended[p, whole, pl.ds(0, HALF), :] = corners[p, pl.ds(0, HALF), :].astype(F32)
+            extended[p, whole, pl.ds(HALF, TH), :] = middle[p, pl.ds(0, TH), :].astype(F32)
+            extended[p, whole, pl.ds(HALF + TH, HALF), :] = corners[p, pl.ds(HALF, HALF), :].astype(F32)
+            for piece, rows, top, low in ((corners, HALF, 0, HALF + TH), (middle, TH // 2, HALF, HALF + TH // 2)):
+                found = piece[p, pl.ds(2 * rows, rows), :].astype(F32)
+                turned_half = pltpu.roll(found, 64, axis=1)
+                extended[p, part, pl.ds(top, rows), :] = found if part else turned_half
+                extended[p, part, pl.ds(low, rows), :] = turned_half if part else found
     for copy in copies[6:]:
         copy.wait()
     for k in range(2):
@@ -245,16 +247,20 @@
     copies = [pltpu.make_async_copy(a, b, copied.at[k]) for k, (a, b) in enumerate(pairs)]
     for copy in copies:
         copy.start()
-    for p in range(2):
-        for j in range(EW // 128):
-            cols = pl.ds(j % 2 * 128, 128)
-            if 2 <= j < 6:
-                cols = pl.ds((j - 2) * 128, 128)
-                rim_above[p, :, cols] = total[p, j, pl.ds(0, HALF), :].astype(BF16)
-                rim_below[p, :, cols] = total[p, j, pl.ds(HALF + TH, HALF), :].astype(BF16)
+    lanes = lax.broadcasted_iota(jnp.int32, (EH // 2, 128), 1)
+    for p in range(2):
+        for j in range(2, 6):
+            cols = pl.ds((j - 2) * 128, 128)
+            rim_above[p, :, cols] = total[p, j, pl.ds(0, HALF), :].astype(BF16)
+            rim_below[p, :, cols] = total[p, j, pl.ds(HALF + TH, HALF), :].astype(BF16)
+        for rim, whole, part in ((rim_before, 1, 0), (rim_after, 6, 7)):
+            rim[p, pl.ds(0, EH), :] = total[p, whole].astype(BF16)
+            upper, lower = total[p, part, pl.ds(0, EH // 2), :], total[p, part, pl.ds(EH // 2, EH // 2), :]
+            if part:
+                lower = pltpu.roll(lower, 64, axis=1)
             else:
-                rim = rim_before if j < 2 else rim_after
-                rim[p, :, cols] = total[p, j].astype(BF16)
+                upper = pltpu.roll(upper, 64, axis=1)
+            rim[p, pl.ds(EH, EH // 2), :] = jnp.where(lanes < 64, upper, lower).astype(BF16)
     for core in range(2):
 
         @pl.when(my_col % 2 == core)
@@ -288,13 +294,88 @@
     out[...] = piece[...].astype(BF16)
 
 
-def object_kernel(center, field, from_before, from_after, weight, out):
+def beside(upper, lower, from_upper_lanes):
+    lanes = lax.broadcasted_iota(jnp.int32, upper.shape, 1)
+    if from_upper_lanes:
+        return jnp.where(lanes < 64, pltpu.roll(upper, 64, axis=1), lower)
+    return jnp.where(lanes < 64, upper, pltpu.roll(lower, 64, axis=1))
+
+
+def pieces_kernel(cells, head, tail, last, first):
+    half = TH // 2
+    for p in range(2):
+        head[p] = cells[p, pl.ds(0, HALF), :].astype(BF16)
+        tail[p] = cells[p, pl.ds(TH - HALF, HALF), :].astype(BF16)
+        for out, whole, part in ((last, 384, 256), (first, 0, 128)):
+            out[p, pl.ds(0, TH), :] = cells[p, :, pl.ds(whole, 128)].astype(BF16)
+            upper, lower = cells[p, pl.ds(0, half), pl.ds(part, 128)], cells[p, pl.ds(half, half), pl.ds(part, 128)]
+            out[p, pl.ds(TH, half), :] = beside(upper, lower, part == 256).astype(BF16)
+
+
+def corners_kernel(across, above, below, last, first):
+    my_row = lax.axis_index("row")
+    for p in range(2):
+        for out, whole, part in ((last, 384, 256), (first, 0, 128)):
+
+            def block(at):
+                cols = pl.ds(at, 128)
+                far = across[p, :, cols].astype(F32)
+                top = jnp.where(my_row == EDGE, far, above[p, :, cols].astype(F32))
+                return top, jnp.where(my_row == EDGE - 1, far, below[p, :, cols].astype(F32))
+
+            top, bottom = block(whole)
+            out[p, pl.ds(0, HALF), :] = top.astype(BF16)
+            out[p, pl.ds(HALF, HALF), :] = bottom.astype(BF16)
+            out[p, pl.ds(2 * HALF, HALF), :] = beside(*block(part), part == 256).astype(BF16)
+
+
+def merge_kernel(from_before, from_after, rim_above, rim_below, swap, up, down):
+    my_row = lax.axis_index("row")
+    lanes = lax.broadcasted_iota(jnp.int32, (HALF, 128), 1)
+    for p in range(2):
+        sums = []
+        for rim, rows, halves, lower in (
+            (rim_above, pl.ds(0, HALF), pl.ds(EH, HALF), False),
+            (rim_below, pl.ds(EH - HALF, HALF), pl.ds(EH * 3 // 2 - HALF, HALF), True),
+        ):
+            left, right = from_before[p, halves, :].astype(F32), from_after[p, halves, :].astype(F32)
+            if lower:
+                left = pltpu.roll(left, 64, axis=1)
+            else:
+                right = pltpu.roll(right, 64, axis=1)
+            blocks = [
+                from_before[p, rows, :].astype(F32),
+                jnp.where(lanes < 64, left, 0.0),
+                jnp.where(lanes >= 64, right, 0.0),
+                from_after[p, rows, :].astype(F32),
+            ]
+            sums.append(rim[p].astype(F32) + jnp.concatenate(blocks, axis=1))
+        up[p] = sums[0].astype(BF16)
+        down[p] = sums[1].astype(BF16)
+        swap[p] = jnp.where(my_row == EDGE, sums[0], sums[1]).astype(BF16)
+
+
+def object_kernel(center, field, from_before, from_after, weight, earlier, out):
+    del earlier
+    lanes = lax.broadcasted_iota(jnp.int32, (64, 128), 1)
     for k in range(TH // 64):
         rows = pl.ds(k * 64, 64)
         outer = pl.ds(HALF + k * 64, 64)
+        upper = HALF + k * 64 < EH // 2
+        halves = pl.ds(EH + (HALF + k * 64) % (EH // 2), 64)
         for p in range(2):
-            sides = [from_before[p, outer, :], from_after[p, outer, :]]
-            cells = field[p, rows, :] + jnp.concatenate(sides, axis=1).astype(F32)
+            left, right = from_before[p, halves, :].astype(F32), from_after[p, halves, :].astype(F32)
+            if upper:
+                right = pltpu.roll(right, 64, axis=1)
+            else:
+                left = pltpu.roll(left, 64, axis=1)
+            sides = [
+                from_before[p, outer, :].astype(F32),
+                jnp.where(lanes < 64, left, 0.0),
+                jnp.where(lanes >= 64, right, 0.0),
+                from_after[p, outer, :].astype(F32),
+            ]
+            cells = field[p, rows, :] + jnp.concatenate(sides, axis=1)
             out[p, rows, :] = center[p, rows, :] - cells * weight[rows, :]
 
 
@@ -362,8 +443,8 @@
         main_kernel,
         out_shape=(
             like((2, TH, TW), F32),
-            like((2, EH, 256), BF16),
-            like((2, EH, 256), BF16),
+            like((2, EH * 3 // 2, 128), BF16),
+            like((2, EH * 3 // 2, 128), BF16),
             like((2, HALF, TW), BF16),
             like((2, HALF, TW), BF16),
             like((BLOCKS, 16, 128), BF16),
@@ -387,10 +468,10 @@
             pltpu.VMEM((2 * PS, 2 * PS), BF16),
             pltpu.VMEM((2, HALF, TW), BF16),
             pltpu.VMEM((2, HALF, TW), BF16),
-            pltpu.VMEM((2, TH, 256), BF16),
-            pltpu.VMEM((2, TH, 256), BF16),
-            pltpu.VMEM((2, PS, 256), BF16),
-            pltpu.VMEM((2, PS, 256), BF16),
+            pltpu.VMEM((2, TH * 3 // 2, 128), BF16),
+            pltpu.VMEM((2, TH * 3 // 2, 128), BF16),
+            pltpu.VMEM((2, PS * 3 // 2, 128), BF16),
+            pltpu.VMEM((2, PS * 3 // 2, 128), BF16),
             pltpu.SemaphoreType.DMA((16,)),
             pltpu.SemaphoreType.DMA((PMAX,)),
         ],
@@ -412,7 +493,6 @@
     like = jax.ShapeDtypeStruct
     my_row = lax.axis_index("row")
     where = positions.transpose(0, 2, 3, 1).reshape(-1, positions.shape[1])
-    head, tail = object_field[:, :HALF, :].astype(BF16), object_field[:, TH - HALF :, :].astype(BF16)
     piece = pl.pallas_call(
         cut_kernel,
         out_shape=like((2, HALF, TW), BF16),
@@ -424,10 +504,21 @@
         name="cut",
     )(object_field)
     across = across_edge(piece)
+    strip = like((2, TH * 3 // 2, 128), BF16)
+    piece, object_cells = lax.optimization_barrier((piece, object_field))
+    head, tail, last, first = pl.pallas_call(
+        pieces_kernel,
+        out_shape=(like((2, HALF, TW), BF16),) * 2 + (strip,) * 2,
+        in_specs=[VMEM],
+        out_specs=(VMEM,) * 4,
+        compiler_params=params(60),
+        cost_estimate=pl.CostEstimate(flops=2_000_000, bytes_accessed=4_000_000, transcendentals=0),
+        name="pieces",
+    )(object_cells)
     above = within_halves(tail, 1)
     below = within_halves(head, -1)
-    before = shifted(object_field[:, :, TW - 256 :].astype(BF16), "col", 1)
-    after = shifted(object_field[:, :, :256].astype(BF16), "col", -1)
+    before = shifted(last, "col", 1)
+    after = shifted(first, "col", -1)
     weight = pl.pallas_call(
         illumination_kernel,
         out_shape=like((TH, TW), F32),
@@ -439,11 +530,17 @@
         name="illumination",
     )(where, tile_counts, probe_field)
     across, above, below, weight = lax.optimization_barrier((across, above, below, weight))
-    corners = jnp.concatenate(
-        [jnp.where(my_row == EDGE, across, above), jnp.where(my_row == EDGE - 1, across, below)], axis=1
-    )
-    corners_before = shifted(corners[:, :, TW - 256 :], "col", 1)
-    corners_after = shifted(corners[:, :, :256], "col", -1)
+    last, first = pl.pallas_call(
+        corners_kernel,
+        out_shape=(like((2, PS * 3 // 2, 128), BF16),) * 2,
+        in_specs=[VMEM] * 3,
+        out_specs=(VMEM,) * 2,
+        compiler_params=params(16),
+        cost_estimate=pl.CostEstimate(flops=1_000_000, bytes_accessed=2_000_000, transcendentals=0),
+        name="corners",
+    )(across, above, below)
+    corners_before = shifted(last, "col", 1)
+    corners_after = shifted(first, "col", -1)
     field, rim_before, rim_after, rim_above, rim_below, kept, given = slots_call(
         where, tile_counts, object_field, across, above, below, before, after,
         corners_before, corners_after, probe_field, intensities.reshape(PMAX, PS, PS),
@@ -476,10 +573,16 @@
     parts = exchanged(mine.reshape(16, -1, 16, 128), plane)
     sums = total_of(parts, 8, 10_000_000_000)
     parts = exchanged(sums, line)
-    sides = jnp.concatenate([from_before, from_after], axis=2).astype(F32)
-    up = (rim_above.astype(F32) + sides[:, :HALF]).astype(BF16)
-    down = (rim_below.astype(F32) + sides[:, HALF + TH :]).astype(BF16)
-    across = across_edge(jnp.where(my_row == EDGE, up, down))
+    swap, up, down = pl.pallas_call(
+        merge_kernel,
+        out_shape=(like((2, HALF, TW), BF16),) * 3,
+        in_specs=[VMEM] * 4,
+        out_specs=(VMEM,) * 3,
+        compiler_params=params(24),
+        cost_estimate=pl.CostEstimate(flops=1_000_000, bytes_accessed=2_000_000, transcendentals=0),
+        name="merge",
+    )(from_before, from_after, rim_above, rim_below)
+    across = across_edge(swap)
     from_below = within_halves(up, -1)
     from_above = within_halves(down, 1)
     sums = total_of(parts, 16, 1_000_000_000)
@@ -487,12 +590,12 @@
     new_object = pl.pallas_call(
         object_kernel,
         out_shape=like((2, TH, TW), F32),
-        in_specs=[VMEM] * 5,
+        in_specs=[VMEM] * 5 + [ANY],
         out_specs=VMEM,
         compiler_params=params(60),
         cost_estimate=pl.CostEstimate(flops=4_000_000, bytes_accessed=12_000_000, transcendentals=0),
         name="new_object",
-    )(object_field, field, from_before, from_after, weight)
+    )(object_field, field, from_before, from_after, weight, sums)
     new_object = pl.pallas_call(
         rims_kernel,
         out_shape=like((2, TH, TW), F32),

time: 149 us -> 145 us (0.973); the launches traced: 148 us -> 147 us
  starting transfers between devices: 72.2 us -> 76.5 us
  waiting for transfers between devices: 30.9 us -> 28.1 us
  other arithmetic: 3.56 us -> 1.91 us
    pallas_call x0 -> x3, Pallas kernels: none -> 4.43 us  [the longest x1 2.89 us: on_device(): pl.pallas_call(pieces_kernel, out_shape=(like((2, HALF, TW), BF16),) * 2...]
    pallas_call x1, Pallas kernels: 18.1 us -> 14.6 us  [slots_call(): pl.pallas_call(main_kernel, out_shape=(like((2, TH, TW), F32), like((2, E...]
    ppermute x4, starting transfers between devices: 8.66 us -> 11.3 us  [within_halves(): return lax.ppermute(value, 'row', [(k, k + step) for k in rows])]
    all_to_all x3, starting transfers between devices: 28.9 us -> 31.5 us  [exchanged(): lax.all_to_all(pieces, ('row', 'col'), 0, 0, axis_index_groups=groups)]
    all_to_all x3, waiting for transfers between devices: 12.2 us -> 9.99 us  [exchanged(): lax.all_to_all(pieces, ('row', 'col'), 0, 0, axis_index_groups=groups)]
  transfers between devices with their start and end apart: 17 -> 17, of which waited for: 7 -> 6; matrix products, arithmetic and copies ran while one was open for 2% -> 0% of each run, Pallas kernels for 11% -> 14%
where the time goes in v3:
time: 145 us; the launch traced here: 147 us
  starting transfers between devices  76.5 us (53%)
  Pallas kernels  38.5 us (27%)
  waiting for transfers between devices  28.1 us (19%)
  other arithmetic  1.91 us (1%)
    all_to_all x3, starting transfers between devices, exchanged(): lax.all_to_all(pieces, ('row', 'col'), 0, 0, axis_index_groups=groups)  31.5 us
    ppermute x6, starting transfers between devices, shifted(): return lax.ppermute(value, axis, [(k, k + step) for k in range(low, high)])  18.5 us
    pallas_call x1, Pallas kernels, slots_call(): pl.pallas_call(main_kernel, out_shape=(like((2, TH, TW), F32), like((2, E...  14.6 us
    ppermute x2, starting transfers between devices, across_edge(): return lax.ppermute(value, 'row', [(EDGE - 1, EDGE), (EDGE, EDGE - 1)])  13 us
    ppermute x4, starting transfers between devices, within_halves(): return lax.ppermute(value, 'row', [(k, k + step) for k in rows])  11.3 us
    all_to_all x3, waiting for transfers between devices, exchanged(): lax.all_to_all(pieces, ('row', 'col'), 0, 0, axis_index_groups=groups)  9.99 us
    ppermute x2, waiting for transfers between devices, across_edge(): return lax.ppermute(value, 'row', [(EDGE - 1, EDGE), (EDGE, EDGE - 1)])  9.18 us
    pallas_call x1, Pallas kernels, on_device(): pl.pallas_call(illumination_kernel, out_shape=like((TH, TW), F32), in_spe...  5.52 us
  transfers between devices with their start and end apart: 17, of which 6 were waited for; matrix products, arithmetic and copies ran while one was open for 0% of the time, Pallas kernels for 14%

profile of v3, /device:TPU:57, one launch (start us, length us, event | category | flops | bytes accessed | tf_op | source)
XLA Modules:
  0.0 146.7 jit_solution(14650357717127628915)
XLA Ops:
  0.6 1.9 %cut.1 = bf16[2,192,512]{2,1,0:T(8,128)(2,1)} custom-call(f32[2,512,512]{2,1,0:T(8,128)} %center.3), custom_call_target="tpu_custom_call" | custom-call | flops 400000 | bytes 1200000 | tf_op jit(solution)/shard_map/cut/pallas_call | solution.py:496
  2.6 7.6 %collective-permute-start = (bf16[2,192,512]{2,1,0:T(8,128)(2,1)}, bf16[2,192,512]{2,1,0:T(8,128)(2,1)S(1)}, u32[]{:S(2)}, u32[]{:S(2)}) collective-permute-start(bf16[2,192,512]{2,1,0:T(8,128)(2,1)} %cut.1), channel_id=1, source_target_pairs={{96,128},{128,96},{97,129},{129,97},{98,130},{130,98},{99,131},{13... | collective-permute-start | bytes 1179656 | tf_op jit(solution)/shard_map/ppermute | solution.py:484
  10.2 2.9 %pieces.1 = (bf16[2,192,512]{2,1,0:T(8,128)(2,1)}, bf16[2,192,512]{2,1,0:T(8,128)(2,1)}, bf16[2,768,128]{2,1,0:T(8,128)(2,1)}, bf16[2,768,128]{2,1,0:T(8,128)(2,1)}) custom-call(f32[2,512,512]{2,1,0:T(8,128)} %center.3), custom_call_target="tpu_custom_call" | custom-call | flops 2000000 | bytes 4000000 | tf_op jit(solution)/shard_map/pieces/pallas_call | solution.py:509
  14.3 4.0 %collective-permute-start.2 = (bf16[2,192,512]{2,1,0:T(8,128)(2,1)}, bf16[2,192,512]{2,1,0:T(8,128)(2,1)S(1)}, u32[]{:S(2)}, u32[]{:S(2)}) collective-permute-start(bf16[2,192,512]{2,1,0:T(8,128)(2,1)} %get-tuple-element.30), channel_id=1, source_target_pairs={{32,0},{64,32},{96,64},{160,128},{192,160},{224,192},{33,1},{65,33... | collective-permute-start | bytes 1179656 | tf_op jit(solution)/shard_map/ppermute | solution.py:489
  18.4 4.5 %collective-permute-start.3 = (bf16[2,768,128]{2,1,0:T(8,128)(2,1)}, bf16[2,768,128]{2,1,0:T(8,128)(2,1)S(1)}, u32[]{:S(2)}, u32[]{:S(2)}) collective-permute-start(bf16[2,768,128]{2,1,0:T(8,128)(2,1)} %get-tuple-element.34), channel_id=1, source_target_pairs={{0,1},{1,2},{2,3},{3,4},{4,5},{5,6},{6,7},{7,8},{8,9},{9,10},{10,1... | collective-permute-start | bytes 1179656 | tf_op jit(solution)/shard_map/ppermute | solution.py:436
  22.9 1.9 %collective-permute-start.4 = (bf16[2,768,128]{2,1,0:T(8,128)(2,1)}, bf16[2,768,128]{2,1,0:T(8,128)(2,1)S(1)}, u32[]{:S(2)}, u32[]{:S(2)}) collective-permute-start(bf16[2,768,128]{2,1,0:T(8,128)(2,1)} %get-tuple-element.35), channel_id=1, source_target_pairs={{1,0},{2,1},{3,2},{4,3},{5,4},{6,5},{7,6},{8,7},{9,8},{10,9},{11,1... | collective-permute-start | bytes 1179656 | tf_op jit(solution)/shard_map/ppermute | solution.py:436
  24.8 5.5 %illumination.1.weight.weight_in = f32[512,512]{1,0:T(8,128)} custom-call(s32[96,32]{1,0:T(8,128)} %bitcast.9, s32[8,32]{1,0:T(8,128)} %counts.3, f32[2,384,384]{2,1,0:T(8,128)} %probe.3), custom_call_target="tpu_custom_call" | custom-call | flops 20000000 | bytes 20000000 | tf_op jit(solution)/shard_map/illumination/pallas_call | solution.py:522
  30.6 3.5 %collective-permute-start.5 = (bf16[2,576,128]{2,1,0:T(8,128)(2,1)S(1)}, bf16[2,576,128]{2,1,0:T(8,128)(2,1)S(1)}, u32[]{:S(2)}, u32[]{:S(2)}) collective-permute-start(bf16[2,576,128]{2,1,0:T(8,128)(2,1)S(1)} %get-tuple-element.36), channel_id=1, source_target_pairs={{0,1},{1,2},{2,3},{3,4},{4,5},{5,6},{6,7},{7,8},{8,9},{9,10},{10,1... | collective-permute-start | bytes 884744 | tf_op jit(solution)/shard_map/ppermute | solution.py:436
  34.1 2.8 %collective-permute-start.6 = (bf16[2,576,128]{2,1,0:T(8,128)(2,1)S(1)}, bf16[2,576,128]{2,1,0:T(8,128)(2,1)S(1)}, u32[]{:S(2)}, u32[]{:S(2)}) collective-permute-start(bf16[2,576,128]{2,1,0:T(8,128)(2,1)S(1)} %get-tuple-element.37), channel_id=1, source_target_pairs={{1,0},{2,1},{3,2},{4,3},{5,4},{6,5},{7,6},{8,7},{9,8},{10,9},{11,1... | collective-permute-start | bytes 884744 | tf_op jit(solution)/shard_map/ppermute | solution.py:436
  37.8 4.7 %collective-permute-done.6.corners_after_in = bf16[2,576,128]{2,1,0:T(8,128)(2,1)S(1)} collective-permute-done((bf16[2,576,128]{2,1,0:T(8,128)(2,1)S(1)}, bf16[2,576,128]{2,1,0:T(8,128)(2,1)S(1)}, u32[]{:S(2)}, u32[]{:S(2)}) %collective-permute-start.6) | collective-permute-done | bytes 294944 | tf_op jit(solution)/shard_map/ppermute | solution.py:436
  43.1 14.6 %slots.1 = (f32[2,512,512]{2,1,0:T(8,128)}, bf16[2,1344,128]{2,1,0:T(8,128)(2,1)}, bf16[2,1344,128]{2,1,0:T(8,128)(2,1)}, bf16[2,192,512]{2,1,0:T(8,128)(2,1)}, ...) custom-call(s32[96,32]{1,0:T(8,128)} %bitcast.10, s32[8,32]{1,0:T(8,128)} %counts.3, ...), custom_call_target="tpu_custom_call" | custom-call | tf_op jit(solution)/shard_map/slots/pallas_call | solution.py:442
  57.9 2.0 %collective-permute-done.7 = bf16[112,16,128]{2,1,0:T(8,128)(2,1)S(1)} collective-permute-done((bf16[112,16,128]{2,1,0:T(8,128)(2,1)}, bf16[112,16,128]{2,1,0:T(8,128)(2,1)S(1)}, u32[]{:S(2)}, u32[]{:S(2)}) %collective-permute-start.7) | collective-permute-done | bytes 458784 | tf_op jit(solution)/shard_map/ppermute | solution.py:568
  61.8 24.2 %all-to-all-start = ((bf16[16,7,16,128]{3,2,1,0:T(8,128)(2,1)}), bf16[16,7,16,128]{3,2,1,0:T(8,128)(2,1)S(1)}, u32[]{:S(2)}, u32[]{:S(2)}) async-start(bf16[16,7,16,128]{3,2,1,0:T(8,128)(2,1)} %bitcast.4), calls=%async_computation | async-start | bytes 917504 | tf_op jit(solution)/shard_map/all_to_all | solution.py:555
  86.0 3.8 %collective-permute-start.8 = (bf16[2,1344,128]{2,1,0:T(8,128)(2,1)}, bf16[2,1344,128]{2,1,0:T(8,128)(2,1)S(1)}, u32[]{:S(2)}, u32[]{:S(2)}) collective-permute-start(bf16[2,1344,128]{2,1,0:T(8,128)(2,1)} %get-tuple-element.44), channel_id=1, source_target_pairs={{0,1},{1,2},{2,3},{3,4},{4,5},{5,6},{6,7},{7,8},{8,9},{9,10},{10,1... | collective-permute-start | bytes 2064392 | tf_op jit(solution)/shard_map/ppermute | solution.py:436
  91.8 10.0 %all-to-all-done.pieces = bf16[16,7,16,128]{3,2,1,0:T(8,128)(2,1)S(1)} async-done(((bf16[16,7,16,128]{3,2,1,0:T(8,128)(2,1)}), bf16[16,7,16,128]{3,2,1,0:T(8,128)(2,1)S(1)}, u32[]{:S(2)}, u32[]{:S(2)}) %all-to-all-start) | async-done | bytes 458784 | tf_op jit(solution)/shard_map/all_to_all | solution.py:555
  102.5 3.4 %all-to-all-start.1 = ((bf16[8,7,16,128]{3,2,1,0:T(8,128)(2,1)}), bf16[8,7,16,128]{3,2,1,0:T(8,128)(2,1)S(1)}, u32[]{:S(2)}, u32[]{:S(2)}) async-start(bf16[8,7,16,128]{3,2,1,0:T(8,128)(2,1)} %total.2), calls=%async_computation.1 | async-start | bytes 458752 | tf_op jit(solution)/shard_map/all_to_all | solution.py:555
  107.2 5.5 %collective-permute-start.10 = (bf16[2,192,512]{2,1,0:T(8,128)(2,1)}, bf16[2,192,512]{2,1,0:T(8,128)(2,1)}, u32[]{:S(2)}, u32[]{:S(2)}) collective-permute-start(bf16[2,192,512]{2,1,0:T(8,128)(2,1)} %get-tuple-element.49), channel_id=1, source_target_pairs={{96,128},{128,96},{97,129},{129,97},{98,130},{130,98},{99,131},{13... | collective-permute-start | bytes 1179656 | tf_op jit(solution)/shard_map/ppermute | solution.py:484
  114.0 4.7 %collective-permute-start.12 = (bf16[2,192,512]{2,1,0:T(8,128)(2,1)S(1)}, bf16[2,192,512]{2,1,0:T(8,128)(2,1)}, u32[]{:S(2)}, u32[]{:S(2)}) collective-permute-start(bf16[2,192,512]{2,1,0:T(8,128)(2,1)S(1)} %get-tuple-element.51), channel_id=1, source_target_pairs={{32,0},{64,32},{96,64},{160,128},{192,160},{224,192},{33,1},{65,33... | collective-permute-start | bytes 1179656 | tf_op jit(solution)/shard_map/ppermute | solution.py:489
  119.6 4.0 %all-to-all-start.2 = ((bf16[16,7,16,128]{3,2,1,0:T(8,128)(2,1)}), bf16[16,7,16,128]{3,2,1,0:T(8,128)(2,1)S(1)}, u32[]{:S(2)}, u32[]{:S(2)}) async-start(bf16[16,7,16,128]{3,2,1,0:T(8,128)(2,1)} %total.3.earlier), calls=%async_computation.2 | async-start | bytes 917504 | tf_op jit(solution)/shard_map/all_to_all | solution.py:555
  123.5 4.8 %new_object.1.base = f32[2,512,512]{2,1,0:T(8,128)} custom-call(f32[2,512,512]{2,1,0:T(8,128)} %center.3, f32[2,512,512]{2,1,0:T(8,128)} %get-tuple-element.43.field, bf16[2,1344,128]{2,1,0:T(8,128)(2,1)} %copy-done.2, bf16[2,1344,128]{2,1,0:T(8,128)(2,1)} %copy-done.3, f32[512,512]{1,0:T(8,128)} %illumination.1.weight.weight_in, ...), custom_call_target="tpu_custom_call" | custom-call | flops 4000000 | bytes 12000000 | tf_op jit(solution)/shard_map/new_object/pallas_call | solution.py:590
  128.3 9.2 %collective-permute-done.10.across = bf16[2,192,512]{2,1,0:T(8,128)(2,1)} collective-permute-done((bf16[2,192,512]{2,1,0:T(8,128)(2,1)}, bf16[2,192,512]{2,1,0:T(8,128)(2,1)}, u32[]{:S(2)}, u32[]{:S(2)}) %collective-permute-start.10) | collective-permute-done | bytes 393248 | tf_op jit(solution)/shard_map/ppermute | solution.py:484
  137.5 3.7 %rims.1 = f32[2,512,512]{2,1,0:T(8,128)} custom-call(f32[2,512,512]{2,1,0:T(8,128)} %new_object.1.base, f32[512,512]{1,0:T(8,128)S(1)} %copy-done.1, bf16[2,192,512]{2,1,0:T(8,128)(2,1)} %collective-permute-done.10.across, bf16[2,192,512]{2,1,0:T(8,128)(2,1)} %collective-permute-done.11.from_above, ...), custom_call_target="tpu_custom_call", output_to_operand_aliasing={{}: (0, {})} | custom-call | flops 40000000000 | bytes 4000000 | tf_op jit(solution)/shard_map/rims/pallas_call | solution.py:599
  141.2 2.0 %collective-permute-start.13 = (bf16[112,16,128]{2,1,0:T(8,128)(2,1)S(1)}, bf16[112,16,128]{2,1,0:T(8,128)(2,1)S(1)}, u32[]{:S(2)}, u32[]{:S(2)}) collective-permute-start(bf16[112,16,128]{2,1,0:T(8,128)(2,1)S(1)} %bitcast.6), channel_id=1, source_target_pairs={{0,1},{1,0},{2,3},{3,2},{4,5},{5,4},{6,7},{7,6},{8,9},{9,8},{10,11... | collective-permute-start | bytes 1376264 | tf_op jit(solution)/shard_map/ppermute | solution.py:616
  144.7 1.9 %new_probe.1 = f32[2,384,384]{2,1,0:T(8,128)} custom-call(bf16[112,16,128]{2,1,0:T(8,128)(2,1)S(1)} %bitcast.7, bf16[112,16,128]{2,1,0:T(8,128)(2,1)S(1)} %collective-permute-done.13.other, f32[2,384,384]{2,1,0:T(8,128)S(1)} %copy-done), custom_call_target="tpu_custom_call" | custom-call | tf_op jit(solution)/shard_map/new_probe/pallas_call | solution.py:617
  (48 shorter events, 12.5 us)
Async XLA Ops:
  2.6 27.8 %collective-permute-start = (bf16[2,192,512]{2,1,0:T(8,128)(2,1)}, bf16[2,192,512]{2,1,0:T(8,128)(2,1)S(1)}, u32[]{:S(2)}, u32[]{:S(2)}) collective-permute-start(bf16[2,192,512]{2,1,0:T(8,128)(2,1)} %cut.1), channel_id=1, source_target_pairs={{96,128},{128,96},{97,129},{129,97},{98,130},{130,98},{99,131},{13... | collective-permute-start | bytes 1179656 | tf_op jit(solution)/shard_map/ppermute | solution.py:484
  13.0 17.3 %collective-permute-start.1 = (bf16[2,192,512]{2,1,0:T(8,128)(2,1)}, bf16[2,192,512]{2,1,0:T(8,128)(2,1)S(1)}, u32[]{:S(2)}, u32[]{:S(2)}) collective-permute-start(bf16[2,192,512]{2,1,0:T(8,128)(2,1)} %get-tuple-element.29), channel_id=1, source_target_pairs={{0,32},{32,64},{64,96},{128,160},{160,192},{192,224},{1,33},{33,65... | collective-permute-start | bytes 1179656 | tf_op jit(solution)/shard_map/ppermute | solution.py:489
  14.3 16.0 %collective-permute-start.2 = (bf16[2,192,512]{2,1,0:T(8,128)(2,1)}, bf16[2,192,512]{2,1,0:T(8,128)(2,1)S(1)}, u32[]{:S(2)}, u32[]{:S(2)}) collective-permute-start(bf16[2,192,512]{2,1,0:T(8,128)(2,1)} %get-tuple-element.30), channel_id=1, source_target_pairs={{32,0},{64,32},{96,64},{160,128},{192,160},{224,192},{33,1},{65,33... | collective-permute-start | bytes 1179656 | tf_op jit(solution)/shard_map/ppermute | solution.py:489
  18.4 18.6 %collective-permute-start.3 = (bf16[2,768,128]{2,1,0:T(8,128)(2,1)}, bf16[2,768,128]{2,1,0:T(8,128)(2,1)S(1)}, u32[]{:S(2)}, u32[]{:S(2)}) collective-permute-start(bf16[2,768,128]{2,1,0:T(8,128)(2,1)} %get-tuple-element.34), channel_id=1, source_target_pairs={{0,1},{1,2},{2,3},{3,4},{4,5},{5,6},{6,7},{7,8},{8,9},{9,10},{10,1... | collective-permute-start | bytes 1179656 | tf_op jit(solution)/shard_map/ppermute | solution.py:436
  22.9 14.1 %collective-permute-start.4 = (bf16[2,768,128]{2,1,0:T(8,128)(2,1)}, bf16[2,768,128]{2,1,0:T(8,128)(2,1)S(1)}, u32[]{:S(2)}, u32[]{:S(2)}) collective-permute-start(bf16[2,768,128]{2,1,0:T(8,128)(2,1)} %get-tuple-element.35), channel_id=1, source_target_pairs={{1,0},{2,1},{3,2},{4,3},{5,4},{6,5},{7,6},{8,7},{9,8},{10,9},{11,1... | collective-permute-start | bytes 1179656 | tf_op jit(solution)/shard_map/ppermute | solution.py:436
  30.3 12.1 %copy-start.4 = (bf16[2,192,512]{2,1,0:T(8,128)(2,1)}, bf16[2,192,512]{2,1,0:T(8,128)(2,1)S(1)}, u32[]{:S(2)}) copy-start(bf16[2,192,512]{2,1,0:T(8,128)(2,1)S(1)} %collective-permute-done.across.across_in) | copy-start | bytes 1179652
  30.6 7.1 %collective-permute-start.5 = (bf16[2,576,128]{2,1,0:T(8,128)(2,1)S(1)}, bf16[2,576,128]{2,1,0:T(8,128)(2,1)S(1)}, u32[]{:S(2)}, u32[]{:S(2)}) collective-permute-start(bf16[2,576,128]{2,1,0:T(8,128)(2,1)S(1)} %get-tuple-element.36), channel_id=1, source_target_pairs={{0,1},{1,2},{2,3},{3,4},{4,5},{5,6},{6,7},{7,8},{8,9},{9,10},{10,1... | collective-permute-start | bytes 884744 | tf_op jit(solution)/shard_map/ppermute | solution.py:436
  34.1 8.3 %collective-permute-start.6 = (bf16[2,576,128]{2,1,0:T(8,128)(2,1)S(1)}, bf16[2,576,128]{2,1,0:T(8,128)(2,1)S(1)}, u32[]{:S(2)}, u32[]{:S(2)}) collective-permute-start(bf16[2,576,128]{2,1,0:T(8,128)(2,1)S(1)} %get-tuple-element.37), channel_id=1, source_target_pairs={{1,0},{2,1},{3,2},{4,3},{5,4},{6,5},{7,6},{8,7},{9,8},{10,9},{11,1... | collective-permute-start | bytes 884744 | tf_op jit(solution)/shard_map/ppermute | solution.py:436
  57.8 2.1 %collective-permute-start.7 = (bf16[112,16,128]{2,1,0:T(8,128)(2,1)}, bf16[112,16,128]{2,1,0:T(8,128)(2,1)S(1)}, u32[]{:S(2)}, u32[]{:S(2)}) collective-permute-start(bf16[112,16,128]{2,1,0:T(8,128)(2,1)} %get-tuple-element.39), channel_id=1, source_target_pairs={{0,1},{1,0},{2,3},{3,2},{4,5},{5,4},{6,7},{7,6},{8,9},{9,8},{10,11... | collective-permute-start | bytes 1376264 | tf_op jit(solution)/shard_map/ppermute | solution.py:568
  61.8 40.0 %all-to-all-start = ((bf16[16,7,16,128]{3,2,1,0:T(8,128)(2,1)}), bf16[16,7,16,128]{3,2,1,0:T(8,128)(2,1)S(1)}, u32[]{:S(2)}, u32[]{:S(2)}) async-start(bf16[16,7,16,128]{3,2,1,0:T(8,128)(2,1)} %bitcast.4), calls=%async_computation | async-start | bytes 917504 | tf_op jit(solution)/shard_map/all_to_all | solution.py:555
  86.0 19.9 %copy-start.7 = (bf16[2,192,512]{2,1,0:T(8,128)(2,1)S(1)}, bf16[2,192,512]{2,1,0:T(8,128)(2,1)}, u32[]{:S(2)}) copy-start(bf16[2,192,512]{2,1,0:T(8,128)(2,1)} %get-tuple-element.47.rim_above) | copy-start | bytes 1179652
  86.0 19.9 %copy-start.8 = (bf16[2,192,512]{2,1,0:T(8,128)(2,1)S(1)}, bf16[2,192,512]{2,1,0:T(8,128)(2,1)}, u32[]{:S(2)}) copy-start(bf16[2,192,512]{2,1,0:T(8,128)(2,1)} %get-tuple-element.48.rim_below) | copy-start | bytes 1179652
  86.0 19.9 %collective-permute-start.8 = (bf16[2,1344,128]{2,1,0:T(8,128)(2,1)}, bf16[2,1344,128]{2,1,0:T(8,128)(2,1)S(1)}, u32[]{:S(2)}, u32[]{:S(2)}) collective-permute-start(bf16[2,1344,128]{2,1,0:T(8,128)(2,1)} %get-tuple-element.44), channel_id=1, source_target_pairs={{0,1},{1,2},{2,3},{3,4},{4,5},{5,6},{6,7},{7,8},{8,9},{9,10},{10,1... | collective-permute-start | bytes 2064392 | tf_op jit(solution)/shard_map/ppermute | solution.py:436
  89.8 16.0 %collective-permute-start.9 = (bf16[2,1344,128]{2,1,0:T(8,128)(2,1)}, bf16[2,1344,128]{2,1,0:T(8,128)(2,1)S(1)}, u32[]{:S(2)}, u32[]{:S(2)}) collective-permute-start(bf16[2,1344,128]{2,1,0:T(8,128)(2,1)} %get-tuple-element.45), channel_id=1, source_target_pairs={{1,0},{2,1},{3,2},{4,3},{5,4},{6,5},{7,6},{8,7},{9,8},{10,9},{11,1... | collective-permute-start | bytes 2064392 | tf_op jit(solution)/shard_map/ppermute | solution.py:436
  102.5 16.2 %all-to-all-start.1 = ((bf16[8,7,16,128]{3,2,1,0:T(8,128)(2,1)}), bf16[8,7,16,128]{3,2,1,0:T(8,128)(2,1)S(1)}, u32[]{:S(2)}, u32[]{:S(2)}) async-start(bf16[8,7,16,128]{3,2,1,0:T(8,128)(2,1)} %total.2), calls=%async_computation.1 | async-start | bytes 458752 | tf_op jit(solution)/shard_map/all_to_all | solution.py:555
  105.9 13.7 %copy-start.2 = (bf16[2,1344,128]{2,1,0:T(8,128)(2,1)}, bf16[2,1344,128]{2,1,0:T(8,128)(2,1)S(1)}, u32[]{:S(2)}) copy-start(bf16[2,1344,128]{2,1,0:T(8,128)(2,1)S(1)} %collective-permute-done.8.from_before) | copy-start | bytes 2064388
  105.9 13.7 %copy-start.3 = (bf16[2,1344,128]{2,1,0:T(8,128)(2,1)}, bf16[2,1344,128]{2,1,0:T(8,128)(2,1)S(1)}, u32[]{:S(2)}) copy-start(bf16[2,1344,128]{2,1,0:T(8,128)(2,1)S(1)} %collective-permute-done.9.from_after) | copy-start | bytes 2064388
  107.2 30.3 %collective-permute-start.10 = (bf16[2,192,512]{2,1,0:T(8,128)(2,1)}, bf16[2,192,512]{2,1,0:T(8,128)(2,1)}, u32[]{:S(2)}, u32[]{:S(2)}) collective-permute-start(bf16[2,192,512]{2,1,0:T(8,128)(2,1)} %get-tuple-element.49), channel_id=1, source_target_pairs={{96,128},{128,96},{97,129},{129,97},{98,130},{130,98},{99,131},{13... | collective-permute-start | bytes 1179656 | tf_op jit(solution)/shard_map/ppermute | solution.py:484
  112.7 24.8 %collective-permute-start.11 = (bf16[2,192,512]{2,1,0:T(8,128)(2,1)}, bf16[2,192,512]{2,1,0:T(8,128)(2,1)}, u32[]{:S(2)}, u32[]{:S(2)}) collective-permute-start(bf16[2,192,512]{2,1,0:T(8,128)(2,1)} %get-tuple-element.50), channel_id=1, source_target_pairs={{0,32},{32,64},{64,96},{128,160},{160,192},{192,224},{1,33},{33,65... | collective-permute-start | bytes 1179656 | tf_op jit(solution)/shard_map/ppermute | solution.py:489
  114.0 23.5 %collective-permute-start.12 = (bf16[2,192,512]{2,1,0:T(8,128)(2,1)S(1)}, bf16[2,192,512]{2,1,0:T(8,128)(2,1)}, u32[]{:S(2)}, u32[]{:S(2)}) collective-permute-start(bf16[2,192,512]{2,1,0:T(8,128)(2,1)S(1)} %get-tuple-element.51), channel_id=1, source_target_pairs={{32,0},{64,32},{96,64},{160,128},{192,160},{224,192},{33,1},{65,33... | collective-permute-start | bytes 1179656 | tf_op jit(solution)/shard_map/ppermute | solution.py:489
  119.6 21.7 %all-to-all-start.2 = ((bf16[16,7,16,128]{3,2,1,0:T(8,128)(2,1)}), bf16[16,7,16,128]{3,2,1,0:T(8,128)(2,1)S(1)}, u32[]{:S(2)}, u32[]{:S(2)}) async-start(bf16[16,7,16,128]{3,2,1,0:T(8,128)(2,1)} %total.3.earlier), calls=%async_computation.2 | async-start | bytes 917504 | tf_op jit(solution)/shard_map/all_to_all | solution.py:555
  123.5 14.0 %copy-start.1 = (f32[512,512]{1,0:T(8,128)S(1)}, f32[512,512]{1,0:T(8,128)}, u32[]{:S(2)}) copy-start(f32[512,512]{1,0:T(8,128)} %illumination.1.weight.weight_in) | copy-start | bytes 3145732
  128.3 16.4 %copy-start = (f32[2,384,384]{2,1,0:T(8,128)S(1)}, f32[2,384,384]{2,1,0:T(8,128)}, u32[]{:S(2)}) copy-start(f32[2,384,384]{2,1,0:T(8,128)} %probe.3) | copy-start | bytes 3538948
  141.2 3.5 %collective-permute-start.13 = (bf16[112,16,128]{2,1,0:T(8,128)(2,1)S(1)}, bf16[112,16,128]{2,1,0:T(8,128)(2,1)S(1)}, u32[]{:S(2)}, u32[]{:S(2)}) collective-permute-start(bf16[112,16,128]{2,1,0:T(8,128)(2,1)S(1)} %bitcast.6), channel_id=1, source_target_pairs={{0,1},{1,0},{2,3},{3,2},{4,5},{5,4},{6,7},{7,6},{8,9},{9,8},{10,11... | collective-permute-start | bytes 1376264 | tf_op jit(solution)/shard_map/ppermute | solution.py:616
  (6 other events, 40.6 us)

commit v4 on v3

--- a/solution.py
+++ b/solution.py
@@ -72,11 +72,15 @@
     return [jnp.where(keep, turned[k], turned[k + 1]) for k in range(3)]
 
 
-def illumination_kernel(positions, counts, probe, out, canvas, power):
-    my_row, my_col = lax.axis_index("row"), lax.axis_index("col")
+def power_kernel(probe, power):
     for j in range(3):
         cols = pl.ds(j * 128, 128)
         power[j] = probe[0, :, cols] * probe[0, :, cols] + probe[1, :, cols] * probe[1, :, cols]
+
+
+def illumination_kernel(positions, counts, power, earlier, out, canvas):
+    del earlier
+    my_row, my_col = lax.axis_index("row"), lax.axis_index("col")
     first, last = PS // 128, (PS + TW) // 128
     for j in range(first, last):
         canvas[j, pl.ds(PS, TH), :] = jnp.zeros((TH, 128), F32)
@@ -519,17 +523,16 @@
     below = within_halves(head, -1)
     before = shifted(last, "col", 1)
     after = shifted(first, "col", -1)
-    weight = pl.pallas_call(
-        illumination_kernel,
-        out_shape=like((TH, TW), F32),
-        in_specs=[SMEM, SMEM, VMEM],
+    power = pl.pallas_call(
+        power_kernel,
+        out_shape=like((3, PS, 128), F32),
+        in_specs=[VMEM],
         out_specs=VMEM,
-        scratch_shapes=[pltpu.VMEM((CANVAS // 128, CANVAS, 128), F32), pltpu.VMEM((3, PS, 128), F32)],
         compiler_params=params(60),
         cost_estimate=pl.CostEstimate(flops=20_000_000, bytes_accessed=20_000_000, transcendentals=0),
-        name="illumination",
-    )(where, tile_counts, probe_field)
-    across, above, below, weight = lax.optimization_barrier((across, above, below, weight))
+        name="power",
+    )(probe_field)
+    across, above, below, power = lax.optimization_barrier((across, above, below, power))
     last, first = pl.pallas_call(
         corners_kernel,
         out_shape=(like((2, PS * 3 // 2, 128), BF16),) * 2,
@@ -587,6 +590,16 @@
     from_above = within_halves(down, 1)
     sums = total_of(parts, 16, 1_000_000_000)
     half = exchanged(sums, plane).reshape(BLOCKS, 16, 128)
+    weight = pl.pallas_call(
+        illumination_kernel,
+        out_shape=like((TH, TW), F32),
+        in_specs=[SMEM, SMEM, VMEM, ANY],
+        out_specs=VMEM,
+        scratch_shapes=[pltpu.VMEM((CANVAS // 128, CANVAS, 128), F32)],
+        compiler_params=params(60),
+        cost_estimate=pl.CostEstimate(flops=20_000_000, bytes_accessed=20_000_000, transcendentals=0),
+        name="illumination",
+    )(where, tile_counts, power, sums)
     new_object = pl.pallas_call(
         object_kernel,
         out_shape=like((2, TH, TW), F32),

time: 145 us -> 145 us (level)
  the two profiles are of different devices: /device:TPU:57 before, /device:TPU:21 now
where the time goes in v4:
time: 145 us; the launch traced here: 143 us
  starting transfers between devices  88.5 us (61%)
  Pallas kernels  39.4 us (27%)
  waiting for transfers between devices  11.9 us (8%)
  other arithmetic  1.91 us (1%)
    ppermute x4, starting transfers between devices, within_halves(): return lax.ppermute(value, 'row', [(k, k + step) for k in rows])  25.1 us
    all_to_all x3, starting transfers between devices, exchanged(): lax.all_to_all(pieces, ('row', 'col'), 0, 0, axis_index_groups=groups)  24.7 us
    ppermute x6, starting transfers between devices, shifted(): return lax.ppermute(value, axis, [(k, k + step) for k in range(low, high)])  18.3 us
    ppermute x1, starting transfers between devices, on_device(): arrived = lax.ppermute(given, 'col', partner)  14.7 us
    pallas_call x1, Pallas kernels, slots_call(): pl.pallas_call(main_kernel, out_shape=(like((2, TH, TW), F32), like((2, E...  11.5 us
    pallas_call x1, Pallas kernels, on_device(): pl.pallas_call(illumination_kernel, out_shape=like((TH, TW), F32), in_spe...  7.31 us
    ppermute x6, waiting for transfers between devices, shifted(): return lax.ppermute(value, axis, [(k, k + step) for k in range(low, high)])  6.08 us
    pallas_call x1, Pallas kernels, on_device(): pl.pallas_call(object_kernel, out_shape=like((2, TH, TW), F32), in_specs=...  4.78 us
  transfers between devices with their start and end apart: 17, of which 6 were waited for; matrix products, arithmetic and copies ran while one was open for 0% of the time, Pallas kernels for 17%

profile of v4, /device:TPU:21, one launch (start us, length us, event | category | flops | bytes accessed | tf_op | source)
XLA Modules:
  0.0 143.3 jit_solution(10097577229871796925)
XLA Ops:
  0.6 1.9 %cut.1 = bf16[2,192,512]{2,1,0:T(8,128)(2,1)} custom-call(f32[2,512,512]{2,1,0:T(8,128)} %center.3), custom_call_target="tpu_custom_call" | custom-call | flops 400000 | bytes 1200000 | tf_op jit(solution)/shard_map/cut/pallas_call | solution.py:500
  3.3 2.9 %pieces.1 = (bf16[2,192,512]{2,1,0:T(8,128)(2,1)}, bf16[2,192,512]{2,1,0:T(8,128)(2,1)}, bf16[2,768,128]{2,1,0:T(8,128)(2,1)}, bf16[2,768,128]{2,1,0:T(8,128)(2,1)}) custom-call(f32[2,512,512]{2,1,0:T(8,128)} %center.3), custom_call_target="tpu_custom_call" | custom-call | flops 2000000 | bytes 4000000 | tf_op jit(solution)/shard_map/pieces/pallas_call | solution.py:513
  6.1 10.7 %collective-permute-start.1 = (bf16[2,192,512]{2,1,0:T(8,128)(2,1)}, bf16[2,192,512]{2,1,0:T(8,128)(2,1)S(1)}, u32[]{:S(2)}, u32[]{:S(2)}) collective-permute-start(bf16[2,192,512]{2,1,0:T(8,128)(2,1)} %get-tuple-element.29), channel_id=1, source_target_pairs={{0,32},{32,64},{64,96},{128,160},{160,192},{192,224},{1,33},{33,65... | collective-permute-start | bytes 1179656 | tf_op jit(solution)/shard_map/ppermute | solution.py:493
  16.8 1.9 %collective-permute-start.2 = (bf16[2,192,512]{2,1,0:T(8,128)(2,1)}, bf16[2,192,512]{2,1,0:T(8,128)(2,1)S(1)}, u32[]{:S(2)}, u32[]{:S(2)}) collective-permute-start(bf16[2,192,512]{2,1,0:T(8,128)(2,1)} %get-tuple-element.30), channel_id=1, source_target_pairs={{32,0},{64,32},{96,64},{160,128},{192,160},{224,192},{33,1},{65,33... | collective-permute-start | bytes 1179656 | tf_op jit(solution)/shard_map/ppermute | solution.py:493
  18.8 3.9 %collective-permute-start.3 = (bf16[2,768,128]{2,1,0:T(8,128)(2,1)}, bf16[2,768,128]{2,1,0:T(8,128)(2,1)S(1)}, u32[]{:S(2)}, u32[]{:S(2)}) collective-permute-start(bf16[2,768,128]{2,1,0:T(8,128)(2,1)} %get-tuple-element.34), channel_id=1, source_target_pairs={{0,1},{1,2},{2,3},{3,4},{4,5},{5,6},{6,7},{7,8},{8,9},{9,10},{10,1... | collective-permute-start | bytes 1179656 | tf_op jit(solution)/shard_map/ppermute | solution.py:440
  22.7 1.9 %collective-permute-start.4 = (bf16[2,768,128]{2,1,0:T(8,128)(2,1)}, bf16[2,768,128]{2,1,0:T(8,128)(2,1)S(1)}, u32[]{:S(2)}, u32[]{:S(2)}) collective-permute-start(bf16[2,768,128]{2,1,0:T(8,128)(2,1)} %get-tuple-element.35), channel_id=1, source_target_pairs={{1,0},{2,1},{3,2},{4,3},{5,4},{6,5},{7,6},{8,7},{9,8},{10,9},{11,1... | collective-permute-start | bytes 1179656 | tf_op jit(solution)/shard_map/ppermute | solution.py:440
  24.6 2.2 %power.1 = f32[3,384,128]{2,1,0:T(8,128)} custom-call(f32[2,384,384]{2,1,0:T(8,128)} %probe.3), custom_call_target="tpu_custom_call" | custom-call | flops 20000000 | bytes 20000000 | tf_op jit(solution)/shard_map/power/pallas_call | solution.py:526
  28.5 4.9 %collective-permute-start.5 = (bf16[2,576,128]{2,1,0:T(8,128)(2,1)S(1)}, bf16[2,576,128]{2,1,0:T(8,128)(2,1)S(1)}, u32[]{:S(2)}, u32[]{:S(2)}) collective-permute-start(bf16[2,576,128]{2,1,0:T(8,128)(2,1)S(1)} %get-tuple-element.36), channel_id=1, source_target_pairs={{0,1},{1,2},{2,3},{3,4},{4,5},{5,6},{6,7},{7,8},{8,9},{9,10},{10,1... | collective-permute-start | bytes 884744 | tf_op jit(solution)/shard_map/ppermute | solution.py:440
  33.4 1.9 %collective-permute-start.6 = (bf16[2,576,128]{2,1,0:T(8,128)(2,1)S(1)}, bf16[2,576,128]{2,1,0:T(8,128)(2,1)S(1)}, u32[]{:S(2)}, u32[]{:S(2)}) collective-permute-start(bf16[2,576,128]{2,1,0:T(8,128)(2,1)S(1)} %get-tuple-element.37), channel_id=1, source_target_pairs={{1,0},{2,1},{3,2},{4,3},{5,4},{6,5},{7,6},{8,7},{9,8},{10,9},{11,1... | collective-permute-start | bytes 884744 | tf_op jit(solution)/shard_map/ppermute | solution.py:440
  37.1 4.4 %collective-permute-done.6.corners_after_in = bf16[2,576,128]{2,1,0:T(8,128)(2,1)S(1)} collective-permute-done((bf16[2,576,128]{2,1,0:T(8,128)(2,1)S(1)}, bf16[2,576,128]{2,1,0:T(8,128)(2,1)S(1)}, u32[]{:S(2)}, u32[]{:S(2)}) %collective-permute-start.6) | collective-permute-done | bytes 294944 | tf_op jit(solution)/shard_map/ppermute | solution.py:440
  42.2 11.5 %slots.1 = (f32[2,512,512]{2,1,0:T(8,128)}, bf16[2,1344,128]{2,1,0:T(8,128)(2,1)}, bf16[2,1344,128]{2,1,0:T(8,128)(2,1)}, bf16[2,192,512]{2,1,0:T(8,128)(2,1)}, ...) custom-call(s32[96,32]{1,0:T(8,128)} %bitcast.9, s32[8,32]{1,0:T(8,128)} %counts.3, ...), custom_call_target="tpu_custom_call" | custom-call | tf_op jit(solution)/shard_map/slots/pallas_call | solution.py:446
  53.7 14.7 %collective-permute-start.7 = (bf16[112,16,128]{2,1,0:T(8,128)(2,1)}, bf16[112,16,128]{2,1,0:T(8,128)(2,1)S(1)}, u32[]{:S(2)}, u32[]{:S(2)}) collective-permute-start(bf16[112,16,128]{2,1,0:T(8,128)(2,1)} %get-tuple-element.39), channel_id=1, source_target_pairs={{0,1},{1,0},{2,3},{3,2},{4,5},{5,4},{6,7},{7,6},{8,9},{9,8},{10,11... | collective-permute-start | bytes 1376264 | tf_op jit(solution)/shard_map/ppermute | solution.py:571
  72.0 6.7 %all-to-all-start = ((bf16[16,7,16,128]{3,2,1,0:T(8,128)(2,1)}), bf16[16,7,16,128]{3,2,1,0:T(8,128)(2,1)S(1)}, u32[]{:S(2)}, u32[]{:S(2)}) async-start(bf16[16,7,16,128]{3,2,1,0:T(8,128)(2,1)} %bitcast.3), calls=%async_computation | async-start | bytes 917504 | tf_op jit(solution)/shard_map/all_to_all | solution.py:558
  78.7 3.7 %collective-permute-start.8 = (bf16[2,1344,128]{2,1,0:T(8,128)(2,1)}, bf16[2,1344,128]{2,1,0:T(8,128)(2,1)S(1)}, u32[]{:S(2)}, u32[]{:S(2)}) collective-permute-start(bf16[2,1344,128]{2,1,0:T(8,128)(2,1)} %get-tuple-element.44), channel_id=1, source_target_pairs={{0,1},{1,2},{2,3},{3,4},{4,5},{5,6},{6,7},{7,8},{8,9},{9,10},{10,1... | collective-permute-start | bytes 2064392 | tf_op jit(solution)/shard_map/ppermute | solution.py:440
  82.4 1.9 %collective-permute-start.9 = (bf16[2,1344,128]{2,1,0:T(8,128)(2,1)}, bf16[2,1344,128]{2,1,0:T(8,128)(2,1)S(1)}, u32[]{:S(2)}, u32[]{:S(2)}) collective-permute-start(bf16[2,1344,128]{2,1,0:T(8,128)(2,1)} %get-tuple-element.45), channel_id=1, source_target_pairs={{1,0},{2,1},{3,2},{4,3},{5,4},{6,5},{7,6},{8,7},{9,8},{10,9},{11,1... | collective-permute-start | bytes 2064392 | tf_op jit(solution)/shard_map/ppermute | solution.py:440
  86.3 9.0 %all-to-all-start.1 = ((bf16[8,7,16,128]{3,2,1,0:T(8,128)(2,1)}), bf16[8,7,16,128]{3,2,1,0:T(8,128)(2,1)S(1)}, u32[]{:S(2)}, u32[]{:S(2)}) async-start(bf16[8,7,16,128]{3,2,1,0:T(8,128)(2,1)} %total.2), calls=%async_computation.1 | async-start | bytes 458752 | tf_op jit(solution)/shard_map/all_to_all | solution.py:558
  98.0 10.6 %collective-permute-start.11 = (bf16[2,192,512]{2,1,0:T(8,128)(2,1)}, bf16[2,192,512]{2,1,0:T(8,128)(2,1)}, u32[]{:S(2)}, u32[]{:S(2)}) collective-permute-start(bf16[2,192,512]{2,1,0:T(8,128)(2,1)} %get-tuple-element.50), channel_id=1, source_target_pairs={{0,32},{32,64},{64,96},{128,160},{160,192},{192,224},{1,33},{33,65... | collective-permute-start | bytes 1179656 | tf_op jit(solution)/shard_map/ppermute | solution.py:493
  108.6 1.9 %collective-permute-start.12 = (bf16[2,192,512]{2,1,0:T(8,128)(2,1)S(1)}, bf16[2,192,512]{2,1,0:T(8,128)(2,1)}, u32[]{:S(2)}, u32[]{:S(2)}) collective-permute-start(bf16[2,192,512]{2,1,0:T(8,128)(2,1)S(1)} %get-tuple-element.51), channel_id=1, source_target_pairs={{32,0},{64,32},{96,64},{160,128},{192,160},{224,192},{33,1},{65,33... | collective-permute-start | bytes 1179656 | tf_op jit(solution)/shard_map/ppermute | solution.py:493
  111.4 9.1 %all-to-all-start.2 = ((bf16[16,7,16,128]{3,2,1,0:T(8,128)(2,1)}), bf16[16,7,16,128]{3,2,1,0:T(8,128)(2,1)S(1)}, u32[]{:S(2)}, u32[]{:S(2)}) async-start(bf16[16,7,16,128]{3,2,1,0:T(8,128)(2,1)} %total.3.earlier), calls=%async_computation.2 | async-start | bytes 917504 | tf_op jit(solution)/shard_map/all_to_all | solution.py:558
  120.4 7.3 %illumination.1.weight.weight_in = f32[512,512]{1,0:T(8,128)} custom-call(s32[96,32]{1,0:T(8,128)} %bitcast.10, s32[8,32]{1,0:T(8,128)} %counts.3, f32[3,384,128]{2,1,0:T(8,128)} %power.1, bf16[16,7,16,128]{3,2,1,0:T(8,128)(2,1)} %total.3.earlier), custom_call_target="tpu_custom_call" | custom-call | flops 20000000 | bytes 20000000 | tf_op jit(solution)/shard_map/illumination/pallas_call | solution.py:593
  127.8 4.8 %new_object.1.base = f32[2,512,512]{2,1,0:T(8,128)} custom-call(f32[2,512,512]{2,1,0:T(8,128)} %center.3, f32[2,512,512]{2,1,0:T(8,128)} %get-tuple-element.43.field, bf16[2,1344,128]{2,1,0:T(8,128)(2,1)} %copy-done.2, bf16[2,1344,128]{2,1,0:T(8,128)(2,1)} %copy-done.3, f32[512,512]{1,0:T(8,128)} %illumination.1.weight.weight_in, ...), custom_call_target="tpu_custom_call" | custom-call | flops 4000000 | bytes 12000000 | tf_op jit(solution)/shard_map/new_object/pallas_call | solution.py:603
  132.6 3.8 %rims.1 = f32[2,512,512]{2,1,0:T(8,128)} custom-call(f32[2,512,512]{2,1,0:T(8,128)} %new_object.1.base, f32[512,512]{1,0:T(8,128)S(1)} %copy-done.1, bf16[2,192,512]{2,1,0:T(8,128)(2,1)} %collective-permute-done.10.across, bf16[2,192,512]{2,1,0:T(8,128)(2,1)} %collective-permute-done.11.from_above, ...), custom_call_target="tpu_custom_call", output_to_operand_aliasing={{}: (0, {})} | custom-call | flops 40000000000 | bytes 4000000 | tf_op jit(solution)/shard_map/rims/pallas_call | solution.py:612
  136.4 3.6 %collective-permute-start.13 = (bf16[112,16,128]{2,1,0:T(8,128)(2,1)S(1)}, bf16[112,16,128]{2,1,0:T(8,128)(2,1)S(1)}, u32[]{:S(2)}, u32[]{:S(2)}) collective-permute-start(bf16[112,16,128]{2,1,0:T(8,128)(2,1)S(1)} %bitcast.6), channel_id=1, source_target_pairs={{0,1},{1,0},{2,3},{3,2},{4,5},{5,4},{6,7},{7,6},{8,9},{9,8},{10,11... | collective-permute-start | bytes 1376264 | tf_op jit(solution)/shard_map/ppermute | solution.py:629
  141.4 1.9 %new_probe.1 = f32[2,384,384]{2,1,0:T(8,128)} custom-call(bf16[112,16,128]{2,1,0:T(8,128)(2,1)S(1)} %bitcast.7, bf16[112,16,128]{2,1,0:T(8,128)(2,1)S(1)} %collective-permute-done.13.other, f32[2,384,384]{2,1,0:T(8,128)S(1)} %copy-done), custom_call_target="tpu_custom_call" | custom-call | tf_op jit(solution)/shard_map/new_probe/pallas_call | solution.py:630
  (49 shorter events, 15.4 us)
Async XLA Ops:
  2.6 24.2 %collective-permute-start = (bf16[2,192,512]{2,1,0:T(8,128)(2,1)}, bf16[2,192,512]{2,1,0:T(8,128)(2,1)S(1)}, u32[]{:S(2)}, u32[]{:S(2)}) collective-permute-start(bf16[2,192,512]{2,1,0:T(8,128)(2,1)} %cut.1), channel_id=1, source_target_pairs={{96,128},{128,96},{97,129},{129,97},{98,130},{130,98},{99,131},{13... | collective-permute-start | bytes 1179656 | tf_op jit(solution)/shard_map/ppermute | solution.py:488
  6.1 20.7 %collective-permute-start.1 = (bf16[2,192,512]{2,1,0:T(8,128)(2,1)}, bf16[2,192,512]{2,1,0:T(8,128)(2,1)S(1)}, u32[]{:S(2)}, u32[]{:S(2)}) collective-permute-start(bf16[2,192,512]{2,1,0:T(8,128)(2,1)} %get-tuple-element.29), channel_id=1, source_target_pairs={{0,32},{32,64},{64,96},{128,160},{160,192},{192,224},{1,33},{33,65... | collective-permute-start | bytes 1179656 | tf_op jit(solution)/shard_map/ppermute | solution.py:493
  16.8 11.5 %collective-permute-start.2 = (bf16[2,192,512]{2,1,0:T(8,128)(2,1)}, bf16[2,192,512]{2,1,0:T(8,128)(2,1)S(1)}, u32[]{:S(2)}, u32[]{:S(2)}) collective-permute-start(bf16[2,192,512]{2,1,0:T(8,128)(2,1)} %get-tuple-element.30), channel_id=1, source_target_pairs={{32,0},{64,32},{96,64},{160,128},{192,160},{224,192},{33,1},{65,33... | collective-permute-start | bytes 1179656 | tf_op jit(solution)/shard_map/ppermute | solution.py:493
  18.8 16.6 %collective-permute-start.3 = (bf16[2,768,128]{2,1,0:T(8,128)(2,1)}, bf16[2,768,128]{2,1,0:T(8,128)(2,1)S(1)}, u32[]{:S(2)}, u32[]{:S(2)}) collective-permute-start(bf16[2,768,128]{2,1,0:T(8,128)(2,1)} %get-tuple-element.34), channel_id=1, source_target_pairs={{0,1},{1,2},{2,3},{3,4},{4,5},{5,6},{6,7},{7,8},{8,9},{9,10},{10,1... | collective-permute-start | bytes 1179656 | tf_op jit(solution)/shard_map/ppermute | solution.py:440
  22.7 12.7 %collective-permute-start.4 = (bf16[2,768,128]{2,1,0:T(8,128)(2,1)}, bf16[2,768,128]{2,1,0:T(8,128)(2,1)S(1)}, u32[]{:S(2)}, u32[]{:S(2)}) collective-permute-start(bf16[2,768,128]{2,1,0:T(8,128)(2,1)} %get-tuple-element.35), channel_id=1, source_target_pairs={{1,0},{2,1},{3,2},{4,3},{5,4},{6,5},{7,6},{8,7},{9,8},{10,9},{11,1... | collective-permute-start | bytes 1179656 | tf_op jit(solution)/shard_map/ppermute | solution.py:440
  26.8 14.7 %copy-start.4 = (bf16[2,192,512]{2,1,0:T(8,128)(2,1)}, bf16[2,192,512]{2,1,0:T(8,128)(2,1)S(1)}, u32[]{:S(2)}) copy-start(bf16[2,192,512]{2,1,0:T(8,128)(2,1)S(1)} %collective-permute-done.across.across_in) | copy-start | bytes 1179652
  26.8 14.7 %copy-start.5 = (bf16[2,192,512]{2,1,0:T(8,128)(2,1)}, bf16[2,192,512]{2,1,0:T(8,128)(2,1)S(1)}, u32[]{:S(2)}) copy-start(bf16[2,192,512]{2,1,0:T(8,128)(2,1)S(1)} %collective-permute-done.1.above.above_in) | copy-start | bytes 1179652
  28.3 13.2 %copy-start.6 = (bf16[2,192,512]{2,1,0:T(8,128)(2,1)}, bf16[2,192,512]{2,1,0:T(8,128)(2,1)S(1)}, u32[]{:S(2)}) copy-start(bf16[2,192,512]{2,1,0:T(8,128)(2,1)S(1)} %collective-permute-done.2.below.below_in) | copy-start | bytes 1179652
  28.5 8.5 %collective-permute-start.5 = (bf16[2,576,128]{2,1,0:T(8,128)(2,1)S(1)}, bf16[2,576,128]{2,1,0:T(8,128)(2,1)S(1)}, u32[]{:S(2)}, u32[]{:S(2)}) collective-permute-start(bf16[2,576,128]{2,1,0:T(8,128)(2,1)S(1)} %get-tuple-element.36), channel_id=1, source_target_pairs={{0,1},{1,2},{2,3},{3,4},{4,5},{5,6},{6,7},{7,8},{8,9},{9,10},{10,1... | collective-permute-start | bytes 884744 | tf_op jit(solution)/shard_map/ppermute | solution.py:440
  33.4 8.0 %collective-permute-start.6 = (bf16[2,576,128]{2,1,0:T(8,128)(2,1)S(1)}, bf16[2,576,128]{2,1,0:T(8,128)(2,1)S(1)}, u32[]{:S(2)}, u32[]{:S(2)}) collective-permute-start(bf16[2,576,128]{2,1,0:T(8,128)(2,1)S(1)} %get-tuple-element.37), channel_id=1, source_target_pairs={{1,0},{2,1},{3,2},{4,3},{5,4},{6,5},{7,6},{8,7},{9,8},{10,9},{11,1... | collective-permute-start | bytes 884744 | tf_op jit(solution)/shard_map/ppermute | solution.py:440
  53.7 16.4 %collective-permute-start.7 = (bf16[112,16,128]{2,1,0:T(8,128)(2,1)}, bf16[112,16,128]{2,1,0:T(8,128)(2,1)S(1)}, u32[]{:S(2)}, u32[]{:S(2)}) collective-permute-start(bf16[112,16,128]{2,1,0:T(8,128)(2,1)} %get-tuple-element.39), channel_id=1, source_target_pairs={{0,1},{1,0},{2,3},{3,2},{4,5},{5,4},{6,7},{7,6},{8,9},{9,8},{10,11... | collective-permute-start | bytes 1376264 | tf_op jit(solution)/shard_map/ppermute | solution.py:571
  72.0 13.5 %all-to-all-start = ((bf16[16,7,16,128]{3,2,1,0:T(8,128)(2,1)}), bf16[16,7,16,128]{3,2,1,0:T(8,128)(2,1)S(1)}, u32[]{:S(2)}, u32[]{:S(2)}) async-start(bf16[16,7,16,128]{3,2,1,0:T(8,128)(2,1)} %bitcast.3), calls=%async_computation | async-start | bytes 917504 | tf_op jit(solution)/shard_map/all_to_all | solution.py:558
  78.7 16.6 %copy-start.7 = (bf16[2,192,512]{2,1,0:T(8,128)(2,1)S(1)}, bf16[2,192,512]{2,1,0:T(8,128)(2,1)}, u32[]{:S(2)}) copy-start(bf16[2,192,512]{2,1,0:T(8,128)(2,1)} %get-tuple-element.47.rim_above) | copy-start | bytes 1179652
  78.7 16.6 %copy-start.8 = (bf16[2,192,512]{2,1,0:T(8,128)(2,1)S(1)}, bf16[2,192,512]{2,1,0:T(8,128)(2,1)}, u32[]{:S(2)}) copy-start(bf16[2,192,512]{2,1,0:T(8,128)(2,1)} %get-tuple-element.48.rim_below) | copy-start | bytes 1179652
  78.7 16.5 %collective-permute-start.8 = (bf16[2,1344,128]{2,1,0:T(8,128)(2,1)}, bf16[2,1344,128]{2,1,0:T(8,128)(2,1)S(1)}, u32[]{:S(2)}, u32[]{:S(2)}) collective-permute-start(bf16[2,1344,128]{2,1,0:T(8,128)(2,1)} %get-tuple-element.44), channel_id=1, source_target_pairs={{0,1},{1,2},{2,3},{3,4},{4,5},{5,6},{6,7},{7,8},{8,9},{9,10},{10,1... | collective-permute-start | bytes 2064392 | tf_op jit(solution)/shard_map/ppermute | solution.py:440
  82.4 12.8 %collective-permute-start.9 = (bf16[2,1344,128]{2,1,0:T(8,128)(2,1)}, bf16[2,1344,128]{2,1,0:T(8,128)(2,1)S(1)}, u32[]{:S(2)}, u32[]{:S(2)}) collective-permute-start(bf16[2,1344,128]{2,1,0:T(8,128)(2,1)} %get-tuple-element.45), channel_id=1, source_target_pairs={{1,0},{2,1},{3,2},{4,3},{5,4},{6,5},{7,6},{8,7},{9,8},{10,9},{11,1... | collective-permute-start | bytes 2064392 | tf_op jit(solution)/shard_map/ppermute | solution.py:440
  86.3 24.3 %all-to-all-start.1 = ((bf16[8,7,16,128]{3,2,1,0:T(8,128)(2,1)}), bf16[8,7,16,128]{3,2,1,0:T(8,128)(2,1)S(1)}, u32[]{:S(2)}, u32[]{:S(2)}) async-start(bf16[8,7,16,128]{3,2,1,0:T(8,128)(2,1)} %total.2), calls=%async_computation.1 | async-start | bytes 458752 | tf_op jit(solution)/shard_map/all_to_all | solution.py:558
  95.2 16.1 %copy-start.2 = (bf16[2,1344,128]{2,1,0:T(8,128)(2,1)}, bf16[2,1344,128]{2,1,0:T(8,128)(2,1)S(1)}, u32[]{:S(2)}) copy-start(bf16[2,1344,128]{2,1,0:T(8,128)(2,1)S(1)} %collective-permute-done.8.from_before) | copy-start | bytes 2064388
  95.3 16.1 %copy-start.3 = (bf16[2,1344,128]{2,1,0:T(8,128)(2,1)}, bf16[2,1344,128]{2,1,0:T(8,128)(2,1)S(1)}, u32[]{:S(2)}) copy-start(bf16[2,1344,128]{2,1,0:T(8,128)(2,1)S(1)} %collective-permute-done.9.from_after) | copy-start | bytes 2064388
  96.6 35.9 %collective-permute-start.10 = (bf16[2,192,512]{2,1,0:T(8,128)(2,1)}, bf16[2,192,512]{2,1,0:T(8,128)(2,1)}, u32[]{:S(2)}, u32[]{:S(2)}) collective-permute-start(bf16[2,192,512]{2,1,0:T(8,128)(2,1)} %get-tuple-element.49), channel_id=1, source_target_pairs={{96,128},{128,96},{97,129},{129,97},{98,130},{130,98},{99,131},{13... | collective-permute-start | bytes 1179656 | tf_op jit(solution)/shard_map/ppermute | solution.py:488
  98.0 34.5 %collective-permute-start.11 = (bf16[2,192,512]{2,1,0:T(8,128)(2,1)}, bf16[2,192,512]{2,1,0:T(8,128)(2,1)}, u32[]{:S(2)}, u32[]{:S(2)}) collective-permute-start(bf16[2,192,512]{2,1,0:T(8,128)(2,1)} %get-tuple-element.50), channel_id=1, source_target_pairs={{0,32},{32,64},{64,96},{128,160},{160,192},{192,224},{1,33},{33,65... | collective-permute-start | bytes 1179656 | tf_op jit(solution)/shard_map/ppermute | solution.py:493
  108.6 23.9 %collective-permute-start.12 = (bf16[2,192,512]{2,1,0:T(8,128)(2,1)S(1)}, bf16[2,192,512]{2,1,0:T(8,128)(2,1)}, u32[]{:S(2)}, u32[]{:S(2)}) collective-permute-start(bf16[2,192,512]{2,1,0:T(8,128)(2,1)S(1)} %get-tuple-element.51), channel_id=1, source_target_pairs={{32,0},{64,32},{96,64},{160,128},{192,160},{224,192},{33,1},{65,33... | collective-permute-start | bytes 1179656 | tf_op jit(solution)/shard_map/ppermute | solution.py:493
  111.4 25.0 %all-to-all-start.2 = ((bf16[16,7,16,128]{3,2,1,0:T(8,128)(2,1)}), bf16[16,7,16,128]{3,2,1,0:T(8,128)(2,1)S(1)}, u32[]{:S(2)}, u32[]{:S(2)}) async-start(bf16[16,7,16,128]{3,2,1,0:T(8,128)(2,1)} %total.3.earlier), calls=%async_computation.2 | async-start | bytes 917504 | tf_op jit(solution)/shard_map/all_to_all | solution.py:558
  136.4 5.0 %collective-permute-start.13 = (bf16[112,16,128]{2,1,0:T(8,128)(2,1)S(1)}, bf16[112,16,128]{2,1,0:T(8,128)(2,1)S(1)}, u32[]{:S(2)}, u32[]{:S(2)}) collective-permute-start(bf16[112,16,128]{2,1,0:T(8,128)(2,1)S(1)} %bitcast.6), channel_id=1, source_target_pairs={{0,1},{1,0},{2,3},{3,2},{4,5},{5,4},{6,7},{7,6},{8,9},{9,8},{10,11... | collective-permute-start | bytes 1376264 | tf_op jit(solution)/shard_map/ppermute | solution.py:629
  (6 other events, 31.1 us)

commit v5 on v3

--- a/solution.py
+++ b/solution.py
@@ -72,14 +72,15 @@
     return [jnp.where(keep, turned[k], turned[k + 1]) for k in range(3)]
 
 
-def illumination_kernel(positions, counts, probe, out, canvas, power):
+def add_windows(tiles, positions, counts, probe, start, canvas, power):
     my_row, my_col = lax.axis_index("row"), lax.axis_index("col")
     for j in range(3):
         cols = pl.ds(j * 128, 128)
         power[j] = probe[0, :, cols] * probe[0, :, cols] + probe[1, :, cols] * probe[1, :, cols]
     first, last = PS // 128, (PS + TW) // 128
     for j in range(first, last):
-        canvas[j, pl.ds(PS, TH), :] = jnp.zeros((TH, 128), F32)
+        here = jnp.zeros((TH, 128), F32) if start is None else start[:, pl.ds((j - first) * 128, 128)]
+        canvas[j, pl.ds(PS, TH), :] = here
     lanes = lax.broadcasted_iota(jnp.int32, (BAND, 128), 1)
     grid_r, grid_c = 8, 32
 
@@ -115,10 +116,22 @@
 
         return lax.fori_loop(0, count, slot, carry)
 
-    lax.fori_loop(0, 9, tile, 0)
+    for low_tile, high_tile in tiles:
+        lax.fori_loop(low_tile, high_tile, tile, 0)
+
+
+def early_kernel(positions, counts, probe, out, canvas, power):
+    add_windows(((3, 5),), positions, counts, probe, None, canvas, power)
+    for j in range(TW // 128):
+        out[:, pl.ds(j * 128, 128)] = canvas[PS // 128 + j, pl.ds(PS, TH), :]
+
+
+def illumination_kernel(positions, counts, probe, start, earlier, out, canvas, power):
+    del earlier
+    add_windows(((0, 3), (5, 9)), positions, counts, probe, start, canvas, power)
     floor = OBJECT_REG * jnp.max(power[...])
     for j in range(TW // 128):
-        out[:, pl.ds(j * 128, 128)] = 1.0 / (canvas[first + j, pl.ds(PS, TH), :] + floor)
+        out[:, pl.ds(j * 128, 128)] = 1.0 / (canvas[PS // 128 + j, pl.ds(PS, TH), :] + floor)
 
 
 def main_kernel(
@@ -519,17 +532,18 @@
     below = within_halves(head, -1)
     before = shifted(last, "col", 1)
     after = shifted(first, "col", -1)
-    weight = pl.pallas_call(
-        illumination_kernel,
+    windows = [pltpu.VMEM((CANVAS // 128, CANVAS, 128), F32), pltpu.VMEM((3, PS, 128), F32)]
+    early = pl.pallas_call(
+        early_kernel,
         out_shape=like((TH, TW), F32),
         in_specs=[SMEM, SMEM, VMEM],
         out_specs=VMEM,
-        scratch_shapes=[pltpu.VMEM((CANVAS // 128, CANVAS, 128), F32), pltpu.VMEM((3, PS, 128), F32)],
+        scratch_shapes=windows,
         compiler_params=params(60),
         cost_estimate=pl.CostEstimate(flops=20_000_000, bytes_accessed=20_000_000, transcendentals=0),
-        name="illumination",
+        name="early",
     )(where, tile_counts, probe_field)
-    across, above, below, weight = lax.optimization_barrier((across, above, below, weight))
+    across, above, below, early = lax.optimization_barrier((across, above, below, early))
     last, first = pl.pallas_call(
         corners_kernel,
         out_shape=(like((2, PS * 3 // 2, 128), BF16),) * 2,
@@ -587,6 +601,16 @@
     from_above = within_halves(down, 1)
     sums = total_of(parts, 16, 1_000_000_000)
     half = exchanged(sums, plane).reshape(BLOCKS, 16, 128)
+    weight = pl.pallas_call(
+        illumination_kernel,
+        out_shape=like((TH, TW), F32),
+        in_specs=[SMEM, SMEM, VMEM, VMEM, ANY],
+        out_specs=VMEM,
+        scratch_shapes=windows,
+        compiler_params=params(60),
+        cost_estimate=pl.CostEstimate(flops=20_000_000, bytes_accessed=20_000_000, transcendentals=0),
+        name="illumination",
+    )(where, tile_counts, probe_field, early, sums)
     new_object = pl.pallas_call(
         object_kernel,
         out_shape=like((2, TH, TW), F32),

time: 145 us -> 143 us (0.986); the launches traced: 147 us -> 142 us
  waiting for transfers between devices: 28.1 us -> 15.7 us
  starting transfers between devices: 76.5 us -> 81.4 us
  Pallas kernels: 38.5 us -> 41.6 us
    all_to_all x3, waiting for transfers between devices: 9.99 us -> 2.45 us  [exchanged(): lax.all_to_all(pieces, ('row', 'col'), 0, 0, axis_index_groups=groups)]
    ppermute x2, waiting for transfers between devices: 9.18 us -> 3.67 us  [across_edge(): return lax.ppermute(value, 'row', [(EDGE - 1, EDGE), (EDGE, EDGE - 1)])]
    pallas_call x0 -> x1, Pallas kernels: none -> 3.77 us  [on_device(): pl.pallas_call(early_kernel, out_shape=like((TH, TW), F32), in_specs=[SME...]
    all_to_all x3, starting transfers between devices: 31.5 us -> 35 us  [exchanged(): lax.all_to_all(pieces, ('row', 'col'), 0, 0, axis_index_groups=groups)]
  transfers between devices with their start and end apart: 17 -> 17, of which waited for: 6 -> 7; matrix products, arithmetic and copies ran while one was open for 0% -> 0% of each run, Pallas kernels for 14% -> 16%
where the time goes in v5:
time: 143 us; the launch traced here: 142 us
  starting transfers between devices  81.4 us (57%)
  Pallas kernels  41.6 us (29%)
  waiting for transfers between devices  15.7 us (11%)
  other arithmetic  1.91 us (1%)
    all_to_all x3, starting transfers between devices, exchanged(): lax.all_to_all(pieces, ('row', 'col'), 0, 0, axis_index_groups=groups)  35 us
    ppermute x6, starting transfers between devices, shifted(): return lax.ppermute(value, axis, [(k, k + step) for k in range(low, high)])  18.6 us
    pallas_call x1, Pallas kernels, slots_call(): pl.pallas_call(main_kernel, out_shape=(like((2, TH, TW), F32), like((2, E...  14.7 us
    ppermute x2, starting transfers between devices, across_edge(): return lax.ppermute(value, 'row', [(EDGE - 1, EDGE), (EDGE, EDGE - 1)])  13.6 us
    ppermute x4, starting transfers between devices, within_halves(): return lax.ppermute(value, 'row', [(k, k + step) for k in rows])  11.4 us
    ppermute x6, waiting for transfers between devices, shifted(): return lax.ppermute(value, axis, [(k, k + step) for k in range(low, high)])  6.08 us
    pallas_call x1, Pallas kernels, on_device(): pl.pallas_call(illumination_kernel, out_shape=like((TH, TW), F32), in_spe...  4.82 us
    pallas_call x1, Pallas kernels, on_device(): pl.pallas_call(object_kernel, out_shape=like((2, TH, TW), F32), in_specs=...  4.78 us
  transfers between devices with their start and end apart: 17, of which 7 were waited for; matrix products, arithmetic and copies ran while one was open for 0% of the time, Pallas kernels for 16%

profile of v5, /device:TPU:57, one launch (start us, length us, event | category | flops | bytes accessed | tf_op | source)
XLA Modules:
  0.0 142.2 jit_solution(15281010855267499073)
XLA Ops:
  0.6 1.9 %cut.1 = bf16[2,192,512]{2,1,0:T(8,128)(2,1)} custom-call(f32[2,512,512]{2,1,0:T(8,128)} %center.3), custom_call_target="tpu_custom_call" | custom-call | flops 400000 | bytes 1200000 | tf_op jit(solution)/shard_map/cut/pallas_call | solution.py:509
  2.6 7.6 %collective-permute-start = (bf16[2,192,512]{2,1,0:T(8,128)(2,1)}, bf16[2,192,512]{2,1,0:T(8,128)(2,1)S(1)}, u32[]{:S(2)}, u32[]{:S(2)}) collective-permute-start(bf16[2,192,512]{2,1,0:T(8,128)(2,1)} %cut.1), channel_id=1, source_target_pairs={{96,128},{128,96},{97,129},{129,97},{98,130},{130,98},{99,131},{13... | collective-permute-start | bytes 1179656 | tf_op jit(solution)/shard_map/ppermute | solution.py:497
  10.2 2.9 %pieces.1 = (bf16[2,192,512]{2,1,0:T(8,128)(2,1)}, bf16[2,192,512]{2,1,0:T(8,128)(2,1)}, bf16[2,768,128]{2,1,0:T(8,128)(2,1)}, bf16[2,768,128]{2,1,0:T(8,128)(2,1)}) custom-call(f32[2,512,512]{2,1,0:T(8,128)} %center.3), custom_call_target="tpu_custom_call" | custom-call | flops 2000000 | bytes 4000000 | tf_op jit(solution)/shard_map/pieces/pallas_call | solution.py:522
  14.3 4.0 %collective-permute-start.2 = (bf16[2,192,512]{2,1,0:T(8,128)(2,1)}, bf16[2,192,512]{2,1,0:T(8,128)(2,1)S(1)}, u32[]{:S(2)}, u32[]{:S(2)}) collective-permute-start(bf16[2,192,512]{2,1,0:T(8,128)(2,1)} %get-tuple-element.30), channel_id=1, source_target_pairs={{32,0},{64,32},{96,64},{160,128},{192,160},{224,192},{33,1},{65,33... | collective-permute-start | bytes 1179656 | tf_op jit(solution)/shard_map/ppermute | solution.py:502
  18.3 4.5 %collective-permute-start.3 = (bf16[2,768,128]{2,1,0:T(8,128)(2,1)}, bf16[2,768,128]{2,1,0:T(8,128)(2,1)S(1)}, u32[]{:S(2)}, u32[]{:S(2)}) collective-permute-start(bf16[2,768,128]{2,1,0:T(8,128)(2,1)} %get-tuple-element.34), channel_id=1, source_target_pairs={{0,1},{1,2},{2,3},{3,4},{4,5},{5,6},{6,7},{7,8},{8,9},{9,10},{10,1... | collective-permute-start | bytes 1179656 | tf_op jit(solution)/shard_map/ppermute | solution.py:449
  24.8 3.8 %early.1.start = f32[512,512]{1,0:T(8,128)} custom-call(s32[96,32]{1,0:T(8,128)} %bitcast.9, s32[8,32]{1,0:T(8,128)} %counts.5, f32[2,384,384]{2,1,0:T(8,128)} %probe.5), custom_call_target="tpu_custom_call" | custom-call | flops 20000000 | bytes 20000000 | tf_op jit(solution)/shard_map/early/pallas_call | solution.py:536
  29.4 4.6 %collective-permute-start.5 = (bf16[2,576,128]{2,1,0:T(8,128)(2,1)S(1)}, bf16[2,576,128]{2,1,0:T(8,128)(2,1)S(1)}, u32[]{:S(2)}, u32[]{:S(2)}) collective-permute-start(bf16[2,576,128]{2,1,0:T(8,128)(2,1)S(1)} %get-tuple-element.36), channel_id=1, source_target_pairs={{0,1},{1,2},{2,3},{3,4},{4,5},{5,6},{6,7},{7,8},{8,9},{9,10},{10,1... | collective-permute-start | bytes 884744 | tf_op jit(solution)/shard_map/ppermute | solution.py:449
  33.9 1.9 %collective-permute-start.6 = (bf16[2,576,128]{2,1,0:T(8,128)(2,1)S(1)}, bf16[2,576,128]{2,1,0:T(8,128)(2,1)S(1)}, u32[]{:S(2)}, u32[]{:S(2)}) collective-permute-start(bf16[2,576,128]{2,1,0:T(8,128)(2,1)S(1)} %get-tuple-element.37), channel_id=1, source_target_pairs={{1,0},{2,1},{3,2},{4,3},{5,4},{6,5},{7,6},{8,7},{9,8},{10,9},{11,1... | collective-permute-start | bytes 884744 | tf_op jit(solution)/shard_map/ppermute | solution.py:449
  37.6 4.4 %collective-permute-done.6.corners_after_in = bf16[2,576,128]{2,1,0:T(8,128)(2,1)S(1)} collective-permute-done((bf16[2,576,128]{2,1,0:T(8,128)(2,1)S(1)}, bf16[2,576,128]{2,1,0:T(8,128)(2,1)S(1)}, u32[]{:S(2)}, u32[]{:S(2)}) %collective-permute-start.6) | collective-permute-done | bytes 294944 | tf_op jit(solution)/shard_map/ppermute | solution.py:449
  42.7 14.7 %slots.1 = (f32[2,512,512]{2,1,0:T(8,128)}, bf16[2,1344,128]{2,1,0:T(8,128)(2,1)}, bf16[2,1344,128]{2,1,0:T(8,128)(2,1)}, bf16[2,192,512]{2,1,0:T(8,128)(2,1)}, ...) custom-call(s32[96,32]{1,0:T(8,128)} %bitcast.10, s32[8,32]{1,0:T(8,128)} %counts.5, ...), custom_call_target="tpu_custom_call" | custom-call | tf_op jit(solution)/shard_map/slots/pallas_call | solution.py:455
  57.5 2.0 %collective-permute-done.7 = bf16[112,16,128]{2,1,0:T(8,128)(2,1)S(1)} collective-permute-done((bf16[112,16,128]{2,1,0:T(8,128)(2,1)}, bf16[112,16,128]{2,1,0:T(8,128)(2,1)S(1)}, u32[]{:S(2)}, u32[]{:S(2)}) %collective-permute-start.7) | collective-permute-done | bytes 458784 | tf_op jit(solution)/shard_map/ppermute | solution.py:582
  61.4 18.3 %all-to-all-start = ((bf16[16,7,16,128]{3,2,1,0:T(8,128)(2,1)}), bf16[16,7,16,128]{3,2,1,0:T(8,128)(2,1)S(1)}, u32[]{:S(2)}, u32[]{:S(2)}) async-start(bf16[16,7,16,128]{3,2,1,0:T(8,128)(2,1)} %bitcast.4), calls=%async_computation | async-start | bytes 917504 | tf_op jit(solution)/shard_map/all_to_all | solution.py:569
  79.7 3.8 %collective-permute-start.8 = (bf16[2,1344,128]{2,1,0:T(8,128)(2,1)}, bf16[2,1344,128]{2,1,0:T(8,128)(2,1)S(1)}, u32[]{:S(2)}, u32[]{:S(2)}) collective-permute-start(bf16[2,1344,128]{2,1,0:T(8,128)(2,1)} %get-tuple-element.44), channel_id=1, source_target_pairs={{0,1},{1,2},{2,3},{3,4},{4,5},{5,6},{6,7},{7,8},{8,9},{9,10},{10,1... | collective-permute-start | bytes 2064392 | tf_op jit(solution)/shard_map/ppermute | solution.py:449
  85.5 2.4 %all-to-all-done.pieces = bf16[16,7,16,128]{3,2,1,0:T(8,128)(2,1)S(1)} async-done(((bf16[16,7,16,128]{3,2,1,0:T(8,128)(2,1)}), bf16[16,7,16,128]{3,2,1,0:T(8,128)(2,1)S(1)}, u32[]{:S(2)}, u32[]{:S(2)}) %all-to-all-start) | async-done | bytes 458784 | tf_op jit(solution)/shard_map/all_to_all | solution.py:569
  88.7 12.7 %all-to-all-start.1 = ((bf16[8,7,16,128]{3,2,1,0:T(8,128)(2,1)}), bf16[8,7,16,128]{3,2,1,0:T(8,128)(2,1)S(1)}, u32[]{:S(2)}, u32[]{:S(2)}) async-start(bf16[8,7,16,128]{3,2,1,0:T(8,128)(2,1)} %total.2), calls=%async_computation.1 | async-start | bytes 458752 | tf_op jit(solution)/shard_map/all_to_all | solution.py:569
  102.8 6.0 %collective-permute-start.10 = (bf16[2,192,512]{2,1,0:T(8,128)(2,1)}, bf16[2,192,512]{2,1,0:T(8,128)(2,1)}, u32[]{:S(2)}, u32[]{:S(2)}) collective-permute-start(bf16[2,192,512]{2,1,0:T(8,128)(2,1)} %get-tuple-element.49), channel_id=1, source_target_pairs={{96,128},{128,96},{97,129},{129,97},{98,130},{130,98},{99,131},{13... | collective-permute-start | bytes 1179656 | tf_op jit(solution)/shard_map/ppermute | solution.py:497
  110.1 4.8 %collective-permute-start.12 = (bf16[2,192,512]{2,1,0:T(8,128)(2,1)S(1)}, bf16[2,192,512]{2,1,0:T(8,128)(2,1)}, u32[]{:S(2)}, u32[]{:S(2)}) collective-permute-start(bf16[2,192,512]{2,1,0:T(8,128)(2,1)S(1)} %get-tuple-element.51), channel_id=1, source_target_pairs={{32,0},{64,32},{96,64},{160,128},{192,160},{224,192},{33,1},{65,33... | collective-permute-start | bytes 1179656 | tf_op jit(solution)/shard_map/ppermute | solution.py:502
  115.7 4.0 %all-to-all-start.2 = ((bf16[16,7,16,128]{3,2,1,0:T(8,128)(2,1)}), bf16[16,7,16,128]{3,2,1,0:T(8,128)(2,1)S(1)}, u32[]{:S(2)}, u32[]{:S(2)}) async-start(bf16[16,7,16,128]{3,2,1,0:T(8,128)(2,1)} %total.3.earlier), calls=%async_computation.2 | async-start | bytes 917504 | tf_op jit(solution)/shard_map/all_to_all | solution.py:569
  119.7 4.8 %illumination.1.weight.weight_in = f32[512,512]{1,0:T(8,128)} custom-call(s32[96,32]{1,0:T(8,128)} %bitcast.11, s32[8,32]{1,0:T(8,128)} %counts.5, f32[2,384,384]{2,1,0:T(8,128)} %probe.5, f32[512,512]{1,0:T(8,128)} %early.1.start, bf16[16,7,16,128]{3,2,1,0:T(8,128)(2,1)} %total.3.earlier), custom_call_target="tpu_custom_call" | custom-call | flops 20000000 | bytes 20000000 | tf_op jit(solution)/shard_map/illumination/pallas_call | solution.py:604
  124.5 4.8 %new_object.1.base = f32[2,512,512]{2,1,0:T(8,128)} custom-call(f32[2,512,512]{2,1,0:T(8,128)} %center.3, f32[2,512,512]{2,1,0:T(8,128)} %get-tuple-element.43.field, bf16[2,1344,128]{2,1,0:T(8,128)(2,1)} %copy-done.2, bf16[2,1344,128]{2,1,0:T(8,128)(2,1)} %copy-done.3, f32[512,512]{1,0:T(8,128)} %illumination.1.weight.weight_in, ...), custom_call_target="tpu_custom_call" | custom-call | flops 4000000 | bytes 12000000 | tf_op jit(solution)/shard_map/new_object/pallas_call | solution.py:614
  129.3 3.1 %collective-permute-done.10.across = bf16[2,192,512]{2,1,0:T(8,128)(2,1)} collective-permute-done((bf16[2,192,512]{2,1,0:T(8,128)(2,1)}, bf16[2,192,512]{2,1,0:T(8,128)(2,1)}, u32[]{:S(2)}, u32[]{:S(2)}) %collective-permute-start.10) | collective-permute-done | bytes 393248 | tf_op jit(solution)/shard_map/ppermute | solution.py:497
  132.4 3.7 %rims.1 = f32[2,512,512]{2,1,0:T(8,128)} custom-call(f32[2,512,512]{2,1,0:T(8,128)} %new_object.1.base, f32[512,512]{1,0:T(8,128)S(1)} %copy-done.1, bf16[2,192,512]{2,1,0:T(8,128)(2,1)} %collective-permute-done.10.across, bf16[2,192,512]{2,1,0:T(8,128)(2,1)} %collective-permute-done.11.from_above, ...), custom_call_target="tpu_custom_call", output_to_operand_aliasing={{}: (0, {})} | custom-call | flops 40000000000 | bytes 4000000 | tf_op jit(solution)/shard_map/rims/pallas_call | solution.py:623
  136.2 2.6 %collective-permute-start.13 = (bf16[112,16,128]{2,1,0:T(8,128)(2,1)S(1)}, bf16[112,16,128]{2,1,0:T(8,128)(2,1)S(1)}, u32[]{:S(2)}, u32[]{:S(2)}) collective-permute-start(bf16[112,16,128]{2,1,0:T(8,128)(2,1)S(1)} %bitcast.6), channel_id=1, source_target_pairs={{0,1},{1,0},{2,3},{3,2},{4,5},{5,4},{6,7},{7,6},{8,9},{9,8},{10,11... | collective-permute-start | bytes 1376264 | tf_op jit(solution)/shard_map/ppermute | solution.py:640
  140.3 1.9 %new_probe.1 = f32[2,384,384]{2,1,0:T(8,128)} custom-call(bf16[112,16,128]{2,1,0:T(8,128)(2,1)S(1)} %bitcast.7, bf16[112,16,128]{2,1,0:T(8,128)(2,1)S(1)} %collective-permute-done.13.other, f32[2,384,384]{2,1,0:T(8,128)S(1)} %copy-done), custom_call_target="tpu_custom_call" | custom-call | tf_op jit(solution)/shard_map/new_probe/pallas_call | solution.py:641
  (49 shorter events, 16.0 us)
Async XLA Ops:
  2.6 26.5 %collective-permute-start = (bf16[2,192,512]{2,1,0:T(8,128)(2,1)}, bf16[2,192,512]{2,1,0:T(8,128)(2,1)S(1)}, u32[]{:S(2)}, u32[]{:S(2)}) collective-permute-start(bf16[2,192,512]{2,1,0:T(8,128)(2,1)} %cut.1), channel_id=1, source_target_pairs={{96,128},{128,96},{97,129},{129,97},{98,130},{130,98},{99,131},{13... | collective-permute-start | bytes 1179656 | tf_op jit(solution)/shard_map/ppermute | solution.py:497
  13.0 16.1 %collective-permute-start.1 = (bf16[2,192,512]{2,1,0:T(8,128)(2,1)}, bf16[2,192,512]{2,1,0:T(8,128)(2,1)S(1)}, u32[]{:S(2)}, u32[]{:S(2)}) collective-permute-start(bf16[2,192,512]{2,1,0:T(8,128)(2,1)} %get-tuple-element.29), channel_id=1, source_target_pairs={{0,32},{32,64},{64,96},{128,160},{160,192},{192,224},{1,33},{33,65... | collective-permute-start | bytes 1179656 | tf_op jit(solution)/shard_map/ppermute | solution.py:502
  14.3 14.8 %collective-permute-start.2 = (bf16[2,192,512]{2,1,0:T(8,128)(2,1)}, bf16[2,192,512]{2,1,0:T(8,128)(2,1)S(1)}, u32[]{:S(2)}, u32[]{:S(2)}) collective-permute-start(bf16[2,192,512]{2,1,0:T(8,128)(2,1)} %get-tuple-element.30), channel_id=1, source_target_pairs={{32,0},{64,32},{96,64},{160,128},{192,160},{224,192},{33,1},{65,33... | collective-permute-start | bytes 1179656 | tf_op jit(solution)/shard_map/ppermute | solution.py:502
  18.3 17.5 %collective-permute-start.3 = (bf16[2,768,128]{2,1,0:T(8,128)(2,1)}, bf16[2,768,128]{2,1,0:T(8,128)(2,1)S(1)}, u32[]{:S(2)}, u32[]{:S(2)}) collective-permute-start(bf16[2,768,128]{2,1,0:T(8,128)(2,1)} %get-tuple-element.34), channel_id=1, source_target_pairs={{0,1},{1,2},{2,3},{3,4},{4,5},{5,6},{6,7},{7,8},{8,9},{9,10},{10,1... | collective-permute-start | bytes 1179656 | tf_op jit(solution)/shard_map/ppermute | solution.py:449
  22.9 13.0 %collective-permute-start.4 = (bf16[2,768,128]{2,1,0:T(8,128)(2,1)}, bf16[2,768,128]{2,1,0:T(8,128)(2,1)S(1)}, u32[]{:S(2)}, u32[]{:S(2)}) collective-permute-start(bf16[2,768,128]{2,1,0:T(8,128)(2,1)} %get-tuple-element.35), channel_id=1, source_target_pairs={{1,0},{2,1},{3,2},{4,3},{5,4},{6,5},{7,6},{8,7},{9,8},{10,9},{11,1... | collective-permute-start | bytes 1179656 | tf_op jit(solution)/shard_map/ppermute | solution.py:449
  29.1 12.9 %copy-start.4 = (bf16[2,192,512]{2,1,0:T(8,128)(2,1)}, bf16[2,192,512]{2,1,0:T(8,128)(2,1)S(1)}, u32[]{:S(2)}) copy-start(bf16[2,192,512]{2,1,0:T(8,128)(2,1)S(1)} %collective-permute-done.across.across_in) | copy-start | bytes 1179652
  29.1 12.9 %copy-start.5 = (bf16[2,192,512]{2,1,0:T(8,128)(2,1)}, bf16[2,192,512]{2,1,0:T(8,128)(2,1)S(1)}, u32[]{:S(2)}) copy-start(bf16[2,192,512]{2,1,0:T(8,128)(2,1)S(1)} %collective-permute-done.1.above.above_in) | copy-start | bytes 1179652
  29.1 12.9 %copy-start.6 = (bf16[2,192,512]{2,1,0:T(8,128)(2,1)}, bf16[2,192,512]{2,1,0:T(8,128)(2,1)S(1)}, u32[]{:S(2)}) copy-start(bf16[2,192,512]{2,1,0:T(8,128)(2,1)S(1)} %collective-permute-done.2.below.below_in) | copy-start | bytes 1179652
  29.4 8.2 %collective-permute-start.5 = (bf16[2,576,128]{2,1,0:T(8,128)(2,1)S(1)}, bf16[2,576,128]{2,1,0:T(8,128)(2,1)S(1)}, u32[]{:S(2)}, u32[]{:S(2)}) collective-permute-start(bf16[2,576,128]{2,1,0:T(8,128)(2,1)S(1)} %get-tuple-element.36), channel_id=1, source_target_pairs={{0,1},{1,2},{2,3},{3,4},{4,5},{5,6},{6,7},{7,8},{8,9},{9,10},{10,1... | collective-permute-start | bytes 884744 | tf_op jit(solution)/shard_map/ppermute | solution.py:449
  33.9 8.0 %collective-permute-start.6 = (bf16[2,576,128]{2,1,0:T(8,128)(2,1)S(1)}, bf16[2,576,128]{2,1,0:T(8,128)(2,1)S(1)}, u32[]{:S(2)}, u32[]{:S(2)}) collective-permute-start(bf16[2,576,128]{2,1,0:T(8,128)(2,1)S(1)} %get-tuple-element.37), channel_id=1, source_target_pairs={{1,0},{2,1},{3,2},{4,3},{5,4},{6,5},{7,6},{8,7},{9,8},{10,9},{11,1... | collective-permute-start | bytes 884744 | tf_op jit(solution)/shard_map/ppermute | solution.py:449
  57.4 2.1 %collective-permute-start.7 = (bf16[112,16,128]{2,1,0:T(8,128)(2,1)}, bf16[112,16,128]{2,1,0:T(8,128)(2,1)S(1)}, u32[]{:S(2)}, u32[]{:S(2)}) collective-permute-start(bf16[112,16,128]{2,1,0:T(8,128)(2,1)} %get-tuple-element.39), channel_id=1, source_target_pairs={{0,1},{1,0},{2,3},{3,2},{4,5},{5,4},{6,7},{7,6},{8,9},{9,8},{10,11... | collective-permute-start | bytes 1376264 | tf_op jit(solution)/shard_map/ppermute | solution.py:582
  61.4 26.5 %all-to-all-start = ((bf16[16,7,16,128]{3,2,1,0:T(8,128)(2,1)}), bf16[16,7,16,128]{3,2,1,0:T(8,128)(2,1)S(1)}, u32[]{:S(2)}, u32[]{:S(2)}) async-start(bf16[16,7,16,128]{3,2,1,0:T(8,128)(2,1)} %bitcast.4), calls=%async_computation | async-start | bytes 917504 | tf_op jit(solution)/shard_map/all_to_all | solution.py:569
  79.7 21.7 %copy-start.7 = (bf16[2,192,512]{2,1,0:T(8,128)(2,1)S(1)}, bf16[2,192,512]{2,1,0:T(8,128)(2,1)}, u32[]{:S(2)}) copy-start(bf16[2,192,512]{2,1,0:T(8,128)(2,1)} %get-tuple-element.47.rim_above) | copy-start | bytes 1179652
  79.7 21.7 %copy-start.8 = (bf16[2,192,512]{2,1,0:T(8,128)(2,1)S(1)}, bf16[2,192,512]{2,1,0:T(8,128)(2,1)}, u32[]{:S(2)}) copy-start(bf16[2,192,512]{2,1,0:T(8,128)(2,1)} %get-tuple-element.48.rim_below) | copy-start | bytes 1179652
  79.7 21.7 %collective-permute-start.8 = (bf16[2,1344,128]{2,1,0:T(8,128)(2,1)}, bf16[2,1344,128]{2,1,0:T(8,128)(2,1)S(1)}, u32[]{:S(2)}, u32[]{:S(2)}) collective-permute-start(bf16[2,1344,128]{2,1,0:T(8,128)(2,1)} %get-tuple-element.44), channel_id=1, source_target_pairs={{0,1},{1,2},{2,3},{3,4},{4,5},{5,6},{6,7},{7,8},{8,9},{9,10},{10,1... | collective-permute-start | bytes 2064392 | tf_op jit(solution)/shard_map/ppermute | solution.py:449
  83.6 17.9 %collective-permute-start.9 = (bf16[2,1344,128]{2,1,0:T(8,128)(2,1)}, bf16[2,1344,128]{2,1,0:T(8,128)(2,1)S(1)}, u32[]{:S(2)}, u32[]{:S(2)}) collective-permute-start(bf16[2,1344,128]{2,1,0:T(8,128)(2,1)} %get-tuple-element.45), channel_id=1, source_target_pairs={{1,0},{2,1},{3,2},{4,3},{5,4},{6,5},{7,6},{8,7},{9,8},{10,9},{11,1... | collective-permute-start | bytes 2064392 | tf_op jit(solution)/shard_map/ppermute | solution.py:449
  88.7 26.2 %all-to-all-start.1 = ((bf16[8,7,16,128]{3,2,1,0:T(8,128)(2,1)}), bf16[8,7,16,128]{3,2,1,0:T(8,128)(2,1)S(1)}, u32[]{:S(2)}, u32[]{:S(2)}) async-start(bf16[8,7,16,128]{3,2,1,0:T(8,128)(2,1)} %total.2), calls=%async_computation.1 | async-start | bytes 458752 | tf_op jit(solution)/shard_map/all_to_all | solution.py:569
  101.4 14.3 %copy-start.2 = (bf16[2,1344,128]{2,1,0:T(8,128)(2,1)}, bf16[2,1344,128]{2,1,0:T(8,128)(2,1)S(1)}, u32[]{:S(2)}) copy-start(bf16[2,1344,128]{2,1,0:T(8,128)(2,1)S(1)} %collective-permute-done.8.from_before) | copy-start | bytes 2064388
  101.4 14.3 %copy-start.3 = (bf16[2,1344,128]{2,1,0:T(8,128)(2,1)}, bf16[2,1344,128]{2,1,0:T(8,128)(2,1)S(1)}, u32[]{:S(2)}) copy-start(bf16[2,1344,128]{2,1,0:T(8,128)(2,1)S(1)} %collective-permute-done.9.from_after) | copy-start | bytes 2064388
  102.8 29.6 %collective-permute-start.10 = (bf16[2,192,512]{2,1,0:T(8,128)(2,1)}, bf16[2,192,512]{2,1,0:T(8,128)(2,1)}, u32[]{:S(2)}, u32[]{:S(2)}) collective-permute-start(bf16[2,192,512]{2,1,0:T(8,128)(2,1)} %get-tuple-element.49), channel_id=1, source_target_pairs={{96,128},{128,96},{97,129},{129,97},{98,130},{130,98},{99,131},{13... | collective-permute-start | bytes 1179656 | tf_op jit(solution)/shard_map/ppermute | solution.py:497
  108.8 23.6 %collective-permute-start.11 = (bf16[2,192,512]{2,1,0:T(8,128)(2,1)}, bf16[2,192,512]{2,1,0:T(8,128)(2,1)}, u32[]{:S(2)}, u32[]{:S(2)}) collective-permute-start(bf16[2,192,512]{2,1,0:T(8,128)(2,1)} %get-tuple-element.50), channel_id=1, source_target_pairs={{0,32},{32,64},{64,96},{128,160},{160,192},{192,224},{1,33},{33,65... | collective-permute-start | bytes 1179656 | tf_op jit(solution)/shard_map/ppermute | solution.py:502
  110.1 22.3 %collective-permute-start.12 = (bf16[2,192,512]{2,1,0:T(8,128)(2,1)S(1)}, bf16[2,192,512]{2,1,0:T(8,128)(2,1)}, u32[]{:S(2)}, u32[]{:S(2)}) collective-permute-start(bf16[2,192,512]{2,1,0:T(8,128)(2,1)S(1)} %get-tuple-element.51), channel_id=1, source_target_pairs={{32,0},{64,32},{96,64},{160,128},{192,160},{224,192},{33,1},{65,33... | collective-permute-start | bytes 1179656 | tf_op jit(solution)/shard_map/ppermute | solution.py:502
  115.7 20.4 %all-to-all-start.2 = ((bf16[16,7,16,128]{3,2,1,0:T(8,128)(2,1)}), bf16[16,7,16,128]{3,2,1,0:T(8,128)(2,1)S(1)}, u32[]{:S(2)}, u32[]{:S(2)}) async-start(bf16[16,7,16,128]{3,2,1,0:T(8,128)(2,1)} %total.3.earlier), calls=%async_computation.2 | async-start | bytes 917504 | tf_op jit(solution)/shard_map/all_to_all | solution.py:569
  136.2 4.1 %collective-permute-start.13 = (bf16[112,16,128]{2,1,0:T(8,128)(2,1)S(1)}, bf16[112,16,128]{2,1,0:T(8,128)(2,1)S(1)}, u32[]{:S(2)}, u32[]{:S(2)}) collective-permute-start(bf16[112,16,128]{2,1,0:T(8,128)(2,1)S(1)} %bitcast.6), channel_id=1, source_target_pairs={{0,1},{1,0},{2,3},{3,2},{4,5},{5,4},{6,7},{7,6},{8,9},{9,8},{10,11... | collective-permute-start | bytes 1376264 | tf_op jit(solution)/shard_map/ppermute | solution.py:640
  (6 other events, 36.2 us)
